TPU v7x, 768 devices: a whole 4x8x12 slice. The times are simulated.
768 devices in a mesh: seq: 96 (over z, x, core), head: 8 (over y).
Axes of the slice: x: 4, y: 8, z: 12, core: 2. Of those that a mesh axis runs over, the one named last changes fastest.
Arguments:
- queries: float32 [32, 12288, 128], P('head', 'seq'), may hold values from -1.75 to 1.75
- keys: float32 [32, 12288, 128], P('head', 'seq'), may hold values from -1.75 to 1.75
- values: float32 [32, 12288, 128], P('head', 'seq'), may hold values from -10 to 10
- out_grad: float32 [32, 12288, 128], P('head', 'seq'), may hold values from -6 to 6
- norm_gain: float32 [32, 128], P('head'), may hold values from 0.1 to 1.9
- log_decay: float32 [32, 12288], P('head', 'seq'), may hold values from -1.5 to 0
- doc_ids: int32 [12288], P('seq'), may hold values from 0 to 95, never falling along the last dimension, each value on 1 to 512 neighbouring positions
Outputs:
- query_grad: float32 [32, 12288, 128], P('head', 'seq')
- key_grad: float32 [32, 12288, 128], P('head', 'seq')
- value_grad: float32 [32, 12288, 128], P('head', 'seq')
Inputs may be any that keep to these rules, and one draw needn't show every extreme that they name: `doc_ids`: document numbers never fall along the tokens; each document is 1 to 512 consecutive tokens, and one has exactly 512.
All inputs are finite; a program needn't handle non-finite values.
Results may differ from a plain program's by a relative error of at most 0.0003.
Values sent between devices are 32-bit elements; how exact they have to be, the bound alone decides.
No kernel may reach another device: no remote copies, remote signals or barrier semaphores. Data moves between devices by JAX's collectives and lax.ppermute only.
A program may use at most 64 MiB of HBM per device.

v0:
```python
import jax
import jax.numpy as jnp
from jax import lax
from jax.sharding import PartitionSpec as P

HOPS = 4


EPSILON = 1e-06
PRECISE = lax.Precision.HIGHEST


def from_behind(array, axis, by):
    size = lax.axis_size(axis)
    pairs = [(i, i + by) for i in range(size) if 0 <= i + by < size]
    return lax.ppermute(array, axis, pairs)


def from_everyone(array, axis):
    size = lax.axis_size(axis)
    return lax.all_to_all(
        jnp.broadcast_to(array[None], (size, *array.shape)), axis, 0, 0, tiled=True
    )


def over_copies(array, axis):
    everything = from_everyone(array, axis)
    return jnp.sum(everything, axis=0)


def in_one(arrays, axis):
    vector, at, done = (jnp.concatenate([a.reshape(-1) for a in arrays]), 0, [])
    so_far = over_copies(vector, axis)
    for a in arrays:
        done.append(so_far[at : at + a.size].reshape(a.shape))
        at += a.size
    return tuple(done)


def product(pattern, left_side, right_side):
    return jnp.einsum(
        pattern, left_side, right_side, precision=PRECISE, preferred_element_type=jnp.float32
    )


def join_forward(earlier, latter):
    early_state, early_pass, early_first, early_last = earlier
    late_state, late_pass, late_first, late_last = latter
    linked = (early_last == late_first) & (late_first == late_last) | (late_first <= 0.0)
    weight = jnp.where(linked, late_pass, 0.0)
    merged = late_state + weight[:, None, None] * early_state
    return (
        merged,
        early_pass * late_pass,
        jnp.where(early_first <= 0.0, late_first, early_first),
        jnp.where(late_last <= 0.0, early_last, late_last),
    )


def join_backward(upper_part, lower_part):
    high_state, high_pass, high_first, high_last = upper_part
    low_state, low_pass, low_first, low_last = lower_part
    linked = (low_last == high_first) & (low_first == low_last) | (low_first <= 0.0)
    weight = jnp.where(linked, low_pass, 0.0)
    merged = low_state + weight[:, None, None] * high_state
    return (
        merged,
        high_pass * low_pass,
        jnp.where(low_first <= 0.0, high_first, low_first),
        jnp.where(high_last <= 0.0, low_last, high_last),
    )


def per_device(queries, keys, values, out_grad, norm_gain, log_decay, doc_ids):
    head_count, tok_rows, head_width = queries.shape
    cumulative = jnp.cumsum(log_decay, axis=1)
    labels = doc_ids.astype(jnp.float32) + 1.0
    rows_iota = lax.broadcasted_iota(jnp.int32, (tok_rows, tok_rows), 0)
    cols_iota = lax.broadcasted_iota(jnp.int32, (tok_rows, tok_rows), 1)
    allowed = ((labels[:, None] == labels[None, :]) & (rows_iota >= cols_iota))[None]
    spread = cumulative[:, :, None] - cumulative[:, None, :]
    within = jnp.where(allowed, jnp.exp(jnp.where(allowed, spread, 0.0)), 0.0)
    scores = product("htd,hsd->hts", queries, keys)
    weighted = within * scores
    out_local = product("hts,hsd->htd", weighted, values)
    decay_tail = jnp.exp(cumulative[:, -1:] - cumulative)
    to_end = jnp.where((labels == labels[-1])[None, :], decay_tail, 0.0)
    kv_state = product("hsi,hsj->hij", keys * to_end[:, :, None], values)
    passing = jnp.exp(cumulative[:, -1])
    own_forward = (kv_state, passing, labels[0], labels[-1])
    carried = own_forward
    for repeat in range(HOPS):
        arrived = from_behind((carried[0], carried[1], carried[2], carried[3]), "seq", 1)
        if repeat + 1 < HOPS:
            carried = join_forward(arrived, own_forward)
    prior_state = arrived[0]
    from_prior = jnp.where((labels == arrived[3])[None, :], jnp.exp(cumulative), 0.0)
    attended = out_local + from_prior[:, :, None] * product("hti,hij->htj", queries, prior_state)
    scaled_grad = norm_gain[:, None, :] * out_grad
    totals = in_one(
        (jnp.sum(attended * attended, axis=(0, 2)), jnp.sum(scaled_grad * attended, axis=(0, 2))),
        "head",
    )
    width_all = head_count * head_width * lax.axis_size("head")
    inv_root = lax.rsqrt(totals[0] / width_all + EPSILON)
    coupling = totals[1] / width_all
    attn_grad = inv_root[None, :, None] * (
        scaled_grad - attended * (coupling * inv_root * inv_root)[None, :, None]
    )
    from_start = jnp.where((labels == labels[0])[None, :], jnp.exp(cumulative), 0.0)
    grad_state = product("hti,htj->hij", queries * from_start[:, :, None], attn_grad)
    own_backward = (grad_state, passing, labels[0], labels[-1])
    carried_back = own_backward
    for repeat in range(HOPS):
        arrived_back = from_behind(
            (carried_back[0], carried_back[1], carried_back[2], carried_back[3]), "seq", -1
        )
        if repeat + 1 < HOPS:
            carried_back = join_backward(arrived_back, own_backward)
    grad_weighted = within * product("htd,hsd->hts", attn_grad, values)
    query_grad = product("hts,hsd->htd", grad_weighted, keys)
    query_grad = query_grad + from_prior[:, :, None] * product(
        "htj,hij->hti", attn_grad, prior_state
    )
    key_local = product("hts,htd->hsd", grad_weighted, queries)
    value_local = product("hts,htd->hsd", weighted, attn_grad)
    later_state = arrived_back[0]
    to_next = jnp.where((labels == arrived_back[2])[None, :], decay_tail, 0.0)
    key_grad = key_local + to_next[:, :, None] * product("hij,hsj->hsi", later_state, values)
    value_grad = value_local + to_next[:, :, None] * product("hij,hsi->hsj", later_state, keys)
    return (query_grad, key_grad, value_grad)


def solution(mesh):
    in_specs = (
        P("head", "seq", None),
        P("head", "seq", None),
        P("head", "seq", None),
        P("head", "seq", None),
        P("head", None),
        P("head", "seq"),
        P("seq"),
    )
    out_specs = (P("head", "seq", None), P("head", "seq", None), P("head", "seq", None))
    return jax.shard_map(
        per_device, mesh=mesh, in_specs=in_specs, out_specs=out_specs, check_vma=False
    )
```

profile of v0, /device:TPU:455, one launch (start us, length us, event | category | flops | bytes accessed | tf_op | source)
XLA Modules:
  0.0 165.3 jit_solution(3433981730398427969)
XLA Ops:
  0.6 0.7 convert_add_fusion
  1.9 2.6 %collective-permute-start.8 = (f32[]{:T(128)}, f32[]{:T(128)}, u32[]{:S(2)}, u32[]{:S(2)}) collective-permute-start(f32[]{:T(128)} %bitcast.1), channel_id=1, source_target_pairs={{8,0},{16,8},{24,16},{32,24},{40,32},{48,40},{56,48},{64,56},{72,6... | collective-permute-start | bytes 20 | tf_op jit(solution)/shard_map/ppermute | solution.py:16
  4.5 6.3 %collective-permute-start = (f32[]{:T(128)}, f32[]{:T(128)}, u32[]{:S(2)}, u32[]{:S(2)}) collective-permute-start(f32[]{:T(128)} %bitcast), channel_id=1, source_target_pairs={{0,8},{8,16},{16,24},{24,32},{32,40},{40,48},{48,56},{56,64},{64,7... | collective-permute-start | bytes 20 | tf_op jit(solution)/shard_map/ppermute | solution.py:16
  13.9 2.7 %collective-permute-start.9 = (f32[]{:T(128)}, f32[]{:T(128)}, u32[]{:S(2)}, u32[]{:S(2)}) collective-permute-start(f32[]{:T(128)} %select_n.130), channel_id=1, source_target_pairs={{8,0},{16,8},{24,16},{32,24},{40,32},{48,40},{56,48},{64,56},{72,6... | collective-permute-start | bytes 20 | tf_op jit(solution)/shard_map/ppermute | solution.py:16
  17.9 8.1 %collective-permute-start.1 = (f32[]{:T(128)}, f32[]{:T(128)}, u32[]{:S(2)}, u32[]{:S(2)}) collective-permute-start(f32[]{:T(128)} %select_n.119), channel_id=1, source_target_pairs={{0,8},{8,16},{16,24},{24,32},{32,40},{40,48},{48,56},{56,64},{64,7... | collective-permute-start | bytes 20 | tf_op jit(solution)/shard_map/ppermute | solution.py:16
  27.3 2.9 %collective-permute-start.10 = (f32[]{:T(128)}, f32[]{:T(128)}, u32[]{:S(2)}, u32[]{:S(2)}) collective-permute-start(f32[]{:T(128)} %select_n.131), channel_id=1, source_target_pairs={{8,0},{16,8},{24,16},{32,24},{40,32},{48,40},{56,48},{64,56},{72,6... | collective-permute-start | bytes 20 | tf_op jit(solution)/shard_map/ppermute | solution.py:16
  31.5 8.0 %collective-permute-start.2 = (f32[]{:T(128)}, f32[]{:T(128)}, u32[]{:S(2)}, u32[]{:S(2)}) collective-permute-start(f32[]{:T(128)} %select_n.120), channel_id=1, source_target_pairs={{0,8},{8,16},{16,24},{24,32},{32,40},{40,48},{48,56},{56,64},{64,7... | collective-permute-start | bytes 20 | tf_op jit(solution)/shard_map/ppermute | solution.py:16
  40.8 2.9 %collective-permute-start.11 = (f32[]{:T(128)}, f32[]{:T(128)}, u32[]{:S(2)}, u32[]{:S(2)}) collective-permute-start(f32[]{:T(128)} %select_n.132), channel_id=1, source_target_pairs={{8,0},{16,8},{24,16},{32,24},{40,32},{48,40},{56,48},{64,56},{72,6... | collective-permute-start | bytes 20 | tf_op jit(solution)/shard_map/ppermute | solution.py:16
  45.0 8.0 %collective-permute-start.3 = (f32[]{:T(128)}, f32[]{:T(128)}, u32[]{:S(2)}, u32[]{:S(2)}) collective-permute-start(f32[]{:T(128)} %select_n.121), channel_id=1, source_target_pairs={{0,8},{8,16},{16,24},{24,32},{32,40},{40,48},{48,56},{56,64},{64,7... | collective-permute-start | bytes 20 | tf_op jit(solution)/shard_map/ppermute | solution.py:16
  53.0 2.5 %broadcast_compare_fusion.1 = (pred[128]{0:T(512)(128)(4,1)S(1)}, pred[128]{0:T(512)(128)(4,1)S(1)}, pred[128]{0:T(512)(128)(4,1)S(1)}, pred[128]{0:T(512)(128)(4,1)S(1)}) fusion(f32[]{:T(128)} %collective-permute-done.11, s32[128]{0:T(128)S(1)} %copy-done.6, f32[]{:T(128)} %bitcast.1, f32[]{:T(128)} %collective-permute-done.3, f32[]{:T(128)} %bitcast), kind=kLoop, calls=%fused_computation.45 | loop fusion | flops 768 | bytes 1040 | tf_op jit(solution)/shard_map/eq | solution.py:128
  55.6 1.6 fusion.6
  57.2 7.6 %collective-permute-start.4 = (f32[4,128,128]{2,1,0:T(8,128)S(1)}, f32[4,128,128]{2,1,0:T(8,128)S(1)}, u32[]{:S(2)}, u32[]{:S(2)}) collective-permute-start(f32[4,128,128]{2,1,0:T(8,128)S(1)} %fusion.6), channel_id=1, source_target_pairs={{0,8},{8,16},{16,24},{24,32},{32,40},{40,48},{48,56},{56,64},{64,7... | collective-permute-start | bytes 786440 | tf_op jit(solution)/shard_map/ppermute | solution.py:16
  73.9 2.0 %collective-permute-start.5 = (f32[4,128,128]{2,1,0:T(8,128)S(1)}, f32[4,128,128]{2,1,0:T(8,128)S(1)}, u32[]{:S(2)}, u32[]{:S(2)}) collective-permute-start(f32[4,128,128]{2,1,0:T(8,128)S(1)} %multiply_add_fusion.6), channel_id=1, source_target_pairs={{0,8},{8,16},{16,24},{24,32},{32,40},{40,48},{48,56},{56,64},{64,7... | collective-permute-start | bytes 786440 | tf_op jit(solution)/shard_map/ppermute | solution.py:16
  75.9 3.3 %collective-permute-done.5 = f32[4,128,128]{2,1,0:T(8,128)S(1)} collective-permute-done((f32[4,128,128]{2,1,0:T(8,128)S(1)}, f32[4,128,128]{2,1,0:T(8,128)S(1)}, u32[]{:S(2)}, u32[]{:S(2)}) %collective-permute-start.5) | collective-permute-done | bytes 262176 | tf_op jit(solution)/shard_map/ppermute | solution.py:16
  79.3 7.7 %collective-permute-start.6 = (f32[4,128,128]{2,1,0:T(8,128)S(1)}, f32[4,128,128]{2,1,0:T(8,128)S(1)}, u32[]{:S(2)}, u32[]{:S(2)}) collective-permute-start(f32[4,128,128]{2,1,0:T(8,128)S(1)} %multiply_add_fusion.5), channel_id=1, source_target_pairs={{0,8},{8,16},{16,24},{24,32},{32,40},{40,48},{48,56},{56,64},{64,7... | collective-permute-start | bytes 786440 | tf_op jit(solution)/shard_map/ppermute | solution.py:16
  87.1 3.2 %collective-permute-done.6 = f32[4,128,128]{2,1,0:T(8,128)S(1)} collective-permute-done((f32[4,128,128]{2,1,0:T(8,128)S(1)}, f32[4,128,128]{2,1,0:T(8,128)S(1)}, u32[]{:S(2)}, u32[]{:S(2)}) %collective-permute-start.6) | collective-permute-done | bytes 262176 | tf_op jit(solution)/shard_map/ppermute | solution.py:16
  90.4 7.8 %collective-permute-start.7 = (f32[4,128,128]{2,1,0:T(8,128)S(1)}, f32[4,128,128]{2,1,0:T(8,128)S(1)}, u32[]{:S(2)}, u32[]{:S(2)}) collective-permute-start(f32[4,128,128]{2,1,0:T(8,128)S(1)} %multiply_add_fusion.4), channel_id=1, source_target_pairs={{0,8},{8,16},{16,24},{24,32},{32,40},{40,48},{48,56},{56,64},{64,7... | collective-permute-start | bytes 786440 | tf_op jit(solution)/shard_map/ppermute | solution.py:16
  98.3 0.7 convolution_multiply_fusion.3
  99.7 1.9 %collective-permute-done.7 = f32[4,128,128]{2,1,0:T(8,128)S(1)} collective-permute-done((f32[4,128,128]{2,1,0:T(8,128)S(1)}, f32[4,128,128]{2,1,0:T(8,128)S(1)}, u32[]{:S(2)}, u32[]{:S(2)}) %collective-permute-start.7) | collective-permute-done | bytes 262176 | tf_op jit(solution)/shard_map/ppermute | solution.py:16
  102.2 13.2 %all_to_all.6 = f32[8,1,256]{2,1,0:T(1,128)S(1)} all-to-all(f32[8,1,256]{2,1,0:T(1,128)S(1)} %broadcast_in_dim.91), channel_id=1, replica_groups=mesh['seq'=96,'head'=8] {'head'}, dimensions={0} | all-to-all | bytes 16384 | tf_op jit(solution)/shard_map/all_to_all | solution.py:21
  115.6 0.7 fusion.4
  116.3 1.9 %collective-permute-start.12 = (f32[4,128,128]{2,1,0:T(8,128)S(1)}, f32[4,128,128]{2,1,0:T(8,128)S(1)}, u32[]{:S(2)}, u32[]{:S(2)}) collective-permute-start(f32[4,128,128]{2,1,0:T(8,128)S(1)} %fusion.4), channel_id=1, source_target_pairs={{8,0},{16,8},{24,16},{32,24},{40,32},{48,40},{56,48},{64,56},{72,6... | collective-permute-start | bytes 786440 | tf_op jit(solution)/shard_map/ppermute | solution.py:16
  118.2 11.3 %collective-permute-done.12 = f32[4,128,128]{2,1,0:T(8,128)S(1)} collective-permute-done((f32[4,128,128]{2,1,0:T(8,128)S(1)}, f32[4,128,128]{2,1,0:T(8,128)S(1)}, u32[]{:S(2)}, u32[]{:S(2)}) %collective-permute-start.12) | collective-permute-done | bytes 262176 | tf_op jit(solution)/shard_map/ppermute | solution.py:16
  129.6 1.9 %collective-permute-start.13 = (f32[4,128,128]{2,1,0:T(8,128)S(1)}, f32[4,128,128]{2,1,0:T(8,128)S(1)}, u32[]{:S(2)}, u32[]{:S(2)}) collective-permute-start(f32[4,128,128]{2,1,0:T(8,128)S(1)} %multiply_add_fusion.2), channel_id=1, source_target_pairs={{8,0},{16,8},{24,16},{32,24},{40,32},{48,40},{56,48},{64,56},{72,6... | collective-permute-start | bytes 786440 | tf_op jit(solution)/shard_map/ppermute | solution.py:16
  132.2 8.5 %collective-permute-done.13 = f32[4,128,128]{2,1,0:T(8,128)S(1)} collective-permute-done((f32[4,128,128]{2,1,0:T(8,128)S(1)}, f32[4,128,128]{2,1,0:T(8,128)S(1)}, u32[]{:S(2)}, u32[]{:S(2)}) %collective-permute-start.13) | collective-permute-done | bytes 262176 | tf_op jit(solution)/shard_map/ppermute | solution.py:16
  140.7 1.9 %collective-permute-start.14 = (f32[4,128,128]{2,1,0:T(8,128)S(1)}, f32[4,128,128]{2,1,0:T(8,128)S(1)}, u32[]{:S(2)}, u32[]{:S(2)}) collective-permute-start(f32[4,128,128]{2,1,0:T(8,128)S(1)} %multiply_add_fusion.1), channel_id=1, source_target_pairs={{8,0},{16,8},{24,16},{32,24},{40,32},{48,40},{56,48},{64,56},{72,6... | collective-permute-start | bytes 786440 | tf_op jit(solution)/shard_map/ppermute | solution.py:16
  143.9 7.9 %collective-permute-done.14 = f32[4,128,128]{2,1,0:T(8,128)S(1)} collective-permute-done((f32[4,128,128]{2,1,0:T(8,128)S(1)}, f32[4,128,128]{2,1,0:T(8,128)S(1)}, u32[]{:S(2)}, u32[]{:S(2)}) %collective-permute-start.14) | collective-permute-done | bytes 262176 | tf_op jit(solution)/shard_map/ppermute | solution.py:16
  151.8 1.9 %collective-permute-start.15 = (f32[4,128,128]{2,1,0:T(8,128)S(1)}, f32[4,128,128]{2,1,0:T(8,128)S(1)}, u32[]{:S(2)}, u32[]{:S(2)}) collective-permute-start(f32[4,128,128]{2,1,0:T(8,128)S(1)} %multiply_add_fusion), channel_id=1, source_target_pairs={{8,0},{16,8},{24,16},{32,24},{40,32},{48,40},{56,48},{64,56},{72,6... | collective-permute-start | bytes 786440 | tf_op jit(solution)/shard_map/ppermute | solution.py:16
  154.2 1.3 multiply_add_fusion.3
  155.5 7.4 %collective-permute-done.15 = f32[4,128,128]{2,1,0:T(8,128)S(1)} collective-permute-done((f32[4,128,128]{2,1,0:T(8,128)S(1)}, f32[4,128,128]{2,1,0:T(8,128)S(1)}, u32[]{:S(2)}, u32[]{:S(2)}) %collective-permute-start.15) | collective-permute-done | bytes 262176 | tf_op jit(solution)/shard_map/ppermute | solution.py:16
  162.8 1.1 fusion.1
  163.9 1.4 fusion.3
  (47 shorter events, 5.7 us)
Async XLA Ops:
  0.6 55.0 %copy-start = (f32[4,128,128]{2,1,0:T(8,128)S(1)}, f32[4,128,128]{2,1,0:T(8,128)}, u32[]{:S(2)}) copy-start(f32[4,128,128]{2,1,0:T(8,128)} %param.9) | copy-start | bytes 786436
  1.9 10.7 %collective-permute-start.8 = (f32[]{:T(128)}, f32[]{:T(128)}, u32[]{:S(2)}, u32[]{:S(2)}) collective-permute-start(f32[]{:T(128)} %bitcast.1), channel_id=1, source_target_pairs={{8,0},{16,8},{24,16},{32,24},{40,32},{48,40},{56,48},{64,56},{72,6... | collective-permute-start | bytes 20 | tf_op jit(solution)/shard_map/ppermute | solution.py:16
  4.5 7.6 %copy-start.5 = (f32[4,128]{1,0:T(4,128)S(1)}, f32[4,128]{1,0:T(4,128)}, u32[]{:S(2)}) copy-start(f32[4,128]{1,0:T(4,128)} %param.12) | copy-start | bytes 6148
  4.5 12.1 %collective-permute-start = (f32[]{:T(128)}, f32[]{:T(128)}, u32[]{:S(2)}, u32[]{:S(2)}) collective-permute-start(f32[]{:T(128)} %bitcast), channel_id=1, source_target_pairs={{0,8},{8,16},{16,24},{24,32},{32,40},{40,48},{48,56},{56,64},{64,7... | collective-permute-start | bytes 20 | tf_op jit(solution)/shard_map/ppermute | solution.py:16
  13.9 12.1 %collective-permute-start.9 = (f32[]{:T(128)}, f32[]{:T(128)}, u32[]{:S(2)}, u32[]{:S(2)}) collective-permute-start(f32[]{:T(128)} %select_n.130), channel_id=1, source_target_pairs={{8,0},{16,8},{24,16},{32,24},{40,32},{48,40},{56,48},{64,56},{72,6... | collective-permute-start | bytes 20 | tf_op jit(solution)/shard_map/ppermute | solution.py:16
  17.9 12.3 %collective-permute-start.1 = (f32[]{:T(128)}, f32[]{:T(128)}, u32[]{:S(2)}, u32[]{:S(2)}) collective-permute-start(f32[]{:T(128)} %select_n.119), channel_id=1, source_target_pairs={{0,8},{8,16},{16,24},{24,32},{32,40},{40,48},{48,56},{56,64},{64,7... | collective-permute-start | bytes 20 | tf_op jit(solution)/shard_map/ppermute | solution.py:16
  27.3 12.2 %collective-permute-start.10 = (f32[]{:T(128)}, f32[]{:T(128)}, u32[]{:S(2)}, u32[]{:S(2)}) collective-permute-start(f32[]{:T(128)} %select_n.131), channel_id=1, source_target_pairs={{8,0},{16,8},{24,16},{32,24},{40,32},{48,40},{56,48},{64,56},{72,6... | collective-permute-start | bytes 20 | tf_op jit(solution)/shard_map/ppermute | solution.py:16
  31.5 12.2 %collective-permute-start.2 = (f32[]{:T(128)}, f32[]{:T(128)}, u32[]{:S(2)}, u32[]{:S(2)}) collective-permute-start(f32[]{:T(128)} %select_n.120), channel_id=1, source_target_pairs={{0,8},{8,16},{16,24},{24,32},{32,40},{40,48},{48,56},{56,64},{64,7... | collective-permute-start | bytes 20 | tf_op jit(solution)/shard_map/ppermute | solution.py:16
  40.8 12.2 %copy-start.6 = (s32[128]{0:T(128)S(1)}, s32[128]{0:T(128)}, u32[]{:S(2)}) copy-start(s32[128]{0:T(128)} %param.13) | copy-start | bytes 1540
  40.8 12.2 %collective-permute-start.11 = (f32[]{:T(128)}, f32[]{:T(128)}, u32[]{:S(2)}, u32[]{:S(2)}) collective-permute-start(f32[]{:T(128)} %select_n.132), channel_id=1, source_target_pairs={{8,0},{16,8},{24,16},{32,24},{40,32},{48,40},{56,48},{64,56},{72,6... | collective-permute-start | bytes 20 | tf_op jit(solution)/shard_map/ppermute | solution.py:16
  45.0 8.0 %collective-permute-start.3 = (f32[]{:T(128)}, f32[]{:T(128)}, u32[]{:S(2)}, u32[]{:S(2)}) collective-permute-start(f32[]{:T(128)} %select_n.121), channel_id=1, source_target_pairs={{0,8},{8,16},{16,24},{24,32},{32,40},{40,48},{48,56},{56,64},{64,7... | collective-permute-start | bytes 20 | tf_op jit(solution)/shard_map/ppermute | solution.py:16
  57.2 16.6 %collective-permute-start.4 = (f32[4,128,128]{2,1,0:T(8,128)S(1)}, f32[4,128,128]{2,1,0:T(8,128)S(1)}, u32[]{:S(2)}, u32[]{:S(2)}) collective-permute-start(f32[4,128,128]{2,1,0:T(8,128)S(1)} %fusion.6), channel_id=1, source_target_pairs={{0,8},{8,16},{16,24},{24,32},{32,40},{40,48},{48,56},{56,64},{64,7... | collective-permute-start | bytes 786440 | tf_op jit(solution)/shard_map/ppermute | solution.py:16
  73.9 5.3 %collective-permute-start.5 = (f32[4,128,128]{2,1,0:T(8,128)S(1)}, f32[4,128,128]{2,1,0:T(8,128)S(1)}, u32[]{:S(2)}, u32[]{:S(2)}) collective-permute-start(f32[4,128,128]{2,1,0:T(8,128)S(1)} %multiply_add_fusion.6), channel_id=1, source_target_pairs={{0,8},{8,16},{16,24},{24,32},{32,40},{40,48},{48,56},{56,64},{64,7... | collective-permute-start | bytes 786440 | tf_op jit(solution)/shard_map/ppermute | solution.py:16
  79.3 11.0 %collective-permute-start.6 = (f32[4,128,128]{2,1,0:T(8,128)S(1)}, f32[4,128,128]{2,1,0:T(8,128)S(1)}, u32[]{:S(2)}, u32[]{:S(2)}) collective-permute-start(f32[4,128,128]{2,1,0:T(8,128)S(1)} %multiply_add_fusion.5), channel_id=1, source_target_pairs={{0,8},{8,16},{16,24},{24,32},{32,40},{40,48},{48,56},{56,64},{64,7... | collective-permute-start | bytes 786440 | tf_op jit(solution)/shard_map/ppermute | solution.py:16
  90.3 8.0 %copy-start.1 = (f32[4,128,128]{2,1,0:T(8,128)S(1)}, f32[4,128,128]{2,1,0:T(8,128)}, u32[]{:S(2)}) copy-start(f32[4,128,128]{2,1,0:T(8,128)} %param.7) | copy-start | bytes 786436
  90.3 8.0 %copy-start.2 = (f32[4,128,128]{2,1,0:T(8,128)S(1)}, f32[4,128,128]{2,1,0:T(8,128)}, u32[]{:S(2)}) copy-start(f32[4,128,128]{2,1,0:T(8,128)} %param.8) | copy-start | bytes 786436
  90.4 8.6 %copy-start.3 = (f32[4,128,128]{2,1,0:T(8,128)S(1)}, f32[4,128,128]{2,1,0:T(8,128)}, u32[]{:S(2)}) copy-start(f32[4,128,128]{2,1,0:T(8,128)} %param.10) | copy-start | bytes 786436
  90.4 11.1 %collective-permute-start.7 = (f32[4,128,128]{2,1,0:T(8,128)S(1)}, f32[4,128,128]{2,1,0:T(8,128)S(1)}, u32[]{:S(2)}, u32[]{:S(2)}) collective-permute-start(f32[4,128,128]{2,1,0:T(8,128)S(1)} %multiply_add_fusion.4), channel_id=1, source_target_pairs={{0,8},{8,16},{16,24},{24,32},{32,40},{40,48},{48,56},{56,64},{64,7... | collective-permute-start | bytes 786440 | tf_op jit(solution)/shard_map/ppermute | solution.py:16
  99.1 2.5 %copy-start.4 = (f32[4,128]{1,0:T(4,128)S(1)}, f32[4,128]{1,0:T(4,128)}, u32[]{:S(2)}) copy-start(f32[4,128]{1,0:T(4,128)} %param.11) | copy-start | bytes 6148
  116.3 13.2 %collective-permute-start.12 = (f32[4,128,128]{2,1,0:T(8,128)S(1)}, f32[4,128,128]{2,1,0:T(8,128)S(1)}, u32[]{:S(2)}, u32[]{:S(2)}) collective-permute-start(f32[4,128,128]{2,1,0:T(8,128)S(1)} %fusion.4), channel_id=1, source_target_pairs={{8,0},{16,8},{24,16},{32,24},{40,32},{48,40},{56,48},{64,56},{72,6... | collective-permute-start | bytes 786440 | tf_op jit(solution)/shard_map/ppermute | solution.py:16
  129.6 11.0 %collective-permute-start.13 = (f32[4,128,128]{2,1,0:T(8,128)S(1)}, f32[4,128,128]{2,1,0:T(8,128)S(1)}, u32[]{:S(2)}, u32[]{:S(2)}) collective-permute-start(f32[4,128,128]{2,1,0:T(8,128)S(1)} %multiply_add_fusion.2), channel_id=1, source_target_pairs={{8,0},{16,8},{24,16},{32,24},{40,32},{48,40},{56,48},{64,56},{72,6... | collective-permute-start | bytes 786440 | tf_op jit(solution)/shard_map/ppermute | solution.py:16
  140.7 11.0 %collective-permute-start.14 = (f32[4,128,128]{2,1,0:T(8,128)S(1)}, f32[4,128,128]{2,1,0:T(8,128)S(1)}, u32[]{:S(2)}, u32[]{:S(2)}) collective-permute-start(f32[4,128,128]{2,1,0:T(8,128)S(1)} %multiply_add_fusion.1), channel_id=1, source_target_pairs={{8,0},{16,8},{24,16},{32,24},{40,32},{48,40},{56,48},{64,56},{72,6... | collective-permute-start | bytes 786440 | tf_op jit(solution)/shard_map/ppermute | solution.py:16
  151.8 11.0 %collective-permute-start.15 = (f32[4,128,128]{2,1,0:T(8,128)S(1)}, f32[4,128,128]{2,1,0:T(8,128)S(1)}, u32[]{:S(2)}, u32[]{:S(2)}) collective-permute-start(f32[4,128,128]{2,1,0:T(8,128)S(1)} %multiply_add_fusion), channel_id=1, source_target_pairs={{8,0},{16,8},{24,16},{32,24},{40,32},{48,40},{56,48},{64,56},{72,6... | collective-permute-start | bytes 786440 | tf_op jit(solution)/shard_map/ppermute | solution.py:16
where the time goes:
time: 166 us; the launch traced here: 165 us
  starting transfers between devices  74.3 us (45%)
  waiting for transfers between devices  43.3 us (26%)
  between operations  18.9 us (11%)
  blocking collectives  13.2 us (8%)
  matrix products  10.2 us (6%)
  other arithmetic  4.42 us (3%)
    ppermute x16, starting transfers between devices, from_behind(): return lax.ppermute(array, axis, pairs)  74.3 us
    ppermute x16, waiting for transfers between devices, from_behind(): return lax.ppermute(array, axis, pairs)  43.3 us
    all_to_all x1, blocking collectives, from_everyone(): lax.all_to_all(jnp.broadcast_to(array[None], (size, *array.shape)), axis,...  13.2 us
    dot_general x12, matrix products, product(): jnp.einsum(pattern, left_side, right_side, precision=PRECISE, preferred_e...  10.2 us
  transfers between devices with their start and end apart: 16, of which 7 were waited for; matrix products, arithmetic and copies ran while one was open for 3% of the time, Pallas kernels for 0%

commit v1 on v0

v1 whole, which is shorter than its diff:
```python
import functools

import jax
import jax.numpy as jnp
from jax import lax
from jax.experimental import pallas as pl
from jax.experimental.pallas import tpu as pltpu
from jax.sharding import Mesh
from jax.sharding import PartitionSpec as P

EPSILON = 1e-06
F32 = jnp.float32
BF16 = jnp.bfloat16
NN = (((1,), (0,)), ((), ()))
NT = (((1,), (1,)), ((), ()))
TN = (((0,), (0,)), ((), ()))
VMEM_LIMIT = 24 * 2**20
LAST, FIRST, EXTRA = 4, 5, 8


def split(x):
    high = x.astype(BF16)
    return high, (x - high.astype(F32)).astype(BF16)


def dot3(left, right, dims):
    one = functools.partial(lax.dot_general, dimension_numbers=dims, preferred_element_type=F32)
    return one(left[0], right[0]) + (one(left[0], right[1]) + one(left[1], right[0]))


def kernel_call(body, outs, flops):
    return pl.pallas_call(
        body,
        out_shape=outs,
        compiler_params=pltpu.CompilerParams(vmem_limit_bytes=VMEM_LIMIT),
        cost_estimate=pl.CostEstimate(flops=flops, bytes_accessed=2**20, transcendentals=0),
    )


def as_columns(row, rows):
    return jnp.broadcast_to(row, (rows, row.shape[1])).T


def lower_mask(rows):
    return lax.broadcasted_iota(jnp.int32, (rows, rows), 0) >= lax.broadcasted_iota(
        jnp.int32, (rows, rows), 1
    )


def running(lower, decay_row):
    return jnp.sum(jnp.where(lower, decay_row, 0.0), axis=1, keepdims=True)


def state_body(keys, values, decay, docs, out):
    heads, rows, width = keys.shape
    lower = lower_mask(rows)
    label_row = docs[...].astype(F32)
    label = as_columns(label_row, rows)[:, :1]
    last, first = label_row[:, rows - 1 :], label_row[:, :1]
    base = heads * rows
    for h in range(heads):
        cumulative = running(lower, decay[h : h + 1, :])
        total = cumulative[rows - 1 :, :]
        weight = jnp.where(label == last, jnp.exp(total - cumulative), 0.0)
        state = dot3(split(keys[h] * weight), split(values[h]), TN)
        out[h * width : (h + 1) * width, :] = state
        out[base + h : base + h + 1, :] = jnp.broadcast_to(total, (1, width))
    out[base + LAST : base + LAST + 1, :] = jnp.broadcast_to(last, (1, width))
    out[base + FIRST : base + FIRST + 1, :] = jnp.broadcast_to(first, (1, width))
    out[base + FIRST + 1 : base + EXTRA, :] = jnp.zeros((EXTRA - FIRST - 1, width), F32)


def chip_meta(both, out, base, heads):
    width = out.shape[1]
    out[base : base + heads, :] = both[0, base : base + heads, :] + both[1, base : base + heads, :]
    out[base + LAST : base + LAST + 1, :] = both[1, base + LAST : base + LAST + 1, :]
    out[base + FIRST : base + FIRST + 1, :] = both[0, base + FIRST : base + FIRST + 1, :]
    out[base + FIRST + 1 : base + EXTRA, :] = jnp.zeros((EXTRA - FIRST - 1, width), F32)


def row_of(ref, which, at):
    return ref[which, at : at + 1, :]


def forward_join_body(heads, both, out):
    width = out.shape[1]
    base = heads * width
    linked = row_of(both, 0, base + LAST) == row_of(both, 1, base + LAST)
    for h in range(heads):
        weight = jnp.where(linked, jnp.exp(row_of(both, 1, base + h)), 0.0)
        at = slice(h * width, (h + 1) * width)
        out[at, :] = both[1, at, :] + weight * both[0, at, :]
    chip_meta(both, out, base, heads)


def backward_join_body(heads, both, meta, out):
    width = out.shape[1]
    base = heads * width
    linked = row_of(meta, 0, base + FIRST) == row_of(meta, 1, base + FIRST)
    for h in range(heads):
        weight = jnp.where(linked, jnp.exp(row_of(meta, 0, base + h)), 0.0)
        at = slice(h * width, (h + 1) * width)
        out[at, :] = both[0, at, :] + weight * both[1, at, :]
    chip_meta(meta, out, base, heads)


def local_body(queries, keys, values, out_grad, gain, decay, docs, sent, out_local, scaled, within, weighted, started):
    del sent
    heads, rows, width = queries.shape
    lower = lower_mask(rows)
    label_row = docs[...].astype(F32)
    label = as_columns(label_row, rows)
    allowed = lower & (label == label_row)
    first = label_row[:, :1]
    for h in range(heads):
        cumulative = running(lower, decay[h : h + 1, :])
        spread = cumulative - jnp.broadcast_to(cumulative, (rows, rows)).T
        weight = jnp.where(allowed, jnp.exp(jnp.where(allowed, spread, 0.0)), 0.0)
        scores = dot3(split(queries[h]), split(keys[h]), NT)
        both = weight * scores
        within[h] = weight
        weighted[h] = both
        out_local[h] = dot3(split(both), split(values[h]), NN)
        scaled[h] = gain[h : h + 1, :] * out_grad[h]
        from_start = jnp.where(label[:, :1] == first, jnp.exp(cumulative), 0.0)
        started[h] = queries[h] * from_start


def attended_body(queries, out_local, scaled, decay, docs, core, states, arrived, attended, prior, from_prior, sums):
    heads, rows, width = queries.shape
    base = heads * width
    lower = lower_mask(rows)
    label = as_columns(docs[...].astype(F32), rows)
    second = core[0, 0] == 1
    near = row_of(arrived, 0, base + LAST)
    chained = near == row_of(arrived, 1, base + LAST)
    inner = row_of(states, 0, base + LAST)
    linked = inner == near
    ahead = jnp.where(second, inner, near)
    squares = jnp.zeros((rows, width), F32)
    inners = jnp.zeros((rows, width), F32)
    for h in range(heads):
        at = slice(h * width, (h + 1) * width)
        weight = jnp.where(chained, jnp.exp(row_of(arrived, 0, base + h)), 0.0)
        state = arrived[0, at, :] + weight * arrived[1, at, :]
        passed = jnp.where(linked, jnp.exp(row_of(states, 0, base + h)), 0.0)
        state = jnp.where(second, passed, 1.0) * state + jnp.where(second, states[0, at, :], 0.0)
        prior[h] = state
        cumulative = running(lower, decay[h : h + 1, :])
        reach = jnp.where(label == ahead, jnp.exp(cumulative), 0.0)
        from_prior[h] = reach
        value = out_local[h] + reach * dot3(split(queries[h]), split(state), NN)
        attended[h] = value
        squares += value * value
        inners += scaled[h] * value
    two = jnp.concatenate(
        [
            jnp.sum(squares.T, axis=0, keepdims=True),
            jnp.sum(inners.T, axis=0, keepdims=True),
            jnp.zeros((6, rows), F32),
        ],
        axis=0,
    )
    for i in range(sums.shape[0] // 8):
        sums[8 * i : 8 * i + 8, :] = two


def grad_state_body(width_all, sums, attended, scaled, started, grad, out):
    heads, rows, width = attended.shape
    total = sums[0:8, :]
    for i in range(1, sums.shape[0] // 8):
        total += sums[8 * i : 8 * i + 8, :]
    inverse_row = lax.rsqrt(total[0:1, :] / width_all + EPSILON)
    coupling_row = total[1:2, :] / width_all * inverse_row * inverse_row
    inverse = as_columns(inverse_row, rows)
    coupling = as_columns(coupling_row, rows)
    for h in range(heads):
        value = inverse * (scaled[h] - attended[h] * coupling)
        grad[h] = value
        out[h * width : (h + 1) * width, :] = dot3(split(started[h]), split(value), TN)


def main_grad_body(queries, keys, values, within, weighted, grad, prior, from_prior, sent, query_grad, key_local, value_local):
    del sent
    for h in range(queries.shape[0]):
        of_grad = split(grad[h])
        of_keys = split(keys[h])
        of_both = split(within[h] * dot3(of_grad, split(values[h]), NT))
        query_grad[h] = dot3(of_both, of_keys, NN) + from_prior[h] * dot3(of_grad, split(prior[h]), NT)
        key_local[h] = dot3(of_both, split(queries[h]), TN)
        value_local[h] = dot3(split(weighted[h]), of_grad, TN)


def last_grad_body(keys, values, decay, docs, core, key_local, value_local, meta, states, arrived, key_grad, value_grad):
    heads, rows, width = keys.shape
    base = heads * width
    lower = lower_mask(rows)
    label = as_columns(docs[...].astype(F32), rows)
    first = core[0, 0] == 0
    near = row_of(arrived, 0, base + FIRST)
    chained = near == row_of(arrived, 1, base + FIRST)
    inner = row_of(meta, 1, base + FIRST)
    linked = inner == near
    ahead = jnp.where(first, inner, near)
    for h in range(heads):
        at = slice(h * width, (h + 1) * width)
        weight = jnp.where(chained, jnp.exp(row_of(arrived, 0, base + h)), 0.0)
        state = arrived[0, at, :] + weight * arrived[1, at, :]
        passed = jnp.where(linked, jnp.exp(row_of(meta, 1, base + h)), 0.0)
        state = jnp.where(first, passed, 1.0) * state + jnp.where(first, states[1, at, :], 0.0)
        of_state = split(state)
        cumulative = running(lower, decay[h : h + 1, :])
        to_next = jnp.where(label == ahead, jnp.exp(cumulative[rows - 1 :, :] - cumulative), 0.0)
        key_grad[h] = key_local[h] + to_next * dot3(split(values[h]), of_state, NT)
        value_grad[h] = value_local[h] + to_next * dot3(split(keys[h]), of_state, NN)


def per_device(queries, keys, values, out_grad, norm_gain, log_decay, doc_ids):
    heads, rows, width = queries.shape
    seq = lax.axis_size("chip") * 2
    group = lax.axis_size("head")
    docs = doc_ids.reshape(1, rows)
    core = lax.axis_index("core").astype(jnp.int32).reshape(1, 1)
    shape = lambda *dims: jax.ShapeDtypeStruct(dims, F32)
    block = shape(heads, rows, width)
    payload = shape(heads * width + EXTRA, width)
    product = 6 * heads * rows * width * width

    own = kernel_call(state_body, payload, product)(keys, values, log_decay, docs)
    states = lax.all_gather(own, "core")
    chip_state = kernel_call(functools.partial(forward_join_body, heads), payload, product // 64)(states)
    ahead = [(i, i + 2 + 2 * (i % 2)) for i in range(seq)]
    moved = lax.ppermute(chip_state, ("chip", "core"), [(a, b) for a, b in ahead if b < seq])
    out_local, scaled, within, weighted, started = kernel_call(local_body, (block,) * 5, 2 * product)(
        queries, keys, values, out_grad, norm_gain, log_decay, docs, chip_state
    )
    arrived = lax.all_gather(moved, "core")
    attended, prior, from_prior, sums = kernel_call(
        attended_body, (block, block, block, shape(8 * group, rows)), product
    )(queries, out_local, scaled, log_decay, docs, core, states, arrived)
    sums = lax.all_to_all(sums, "head", 0, 0, tiled=True)
    grad, own_back = kernel_call(
        functools.partial(grad_state_body, heads * width * group), (block, shape(heads * width, width)), product
    )(sums, attended, scaled, started)
    states_back = lax.all_gather(own_back, "core")
    chip_back = kernel_call(functools.partial(backward_join_body, heads), payload, product // 64)(
        states_back, states
    )
    behind = [(i, i - 2 - 2 * (i % 2)) for i in range(seq)]
    moved_back = lax.ppermute(chip_back, ("chip", "core"), [(a, b) for a, b in behind if b >= 0])
    query_grad, key_local, value_local = kernel_call(main_grad_body, (block,) * 3, 5 * product)(
        queries, keys, values, within, weighted, grad, prior, from_prior, chip_back
    )
    arrived_back = lax.all_gather(moved_back, "core")
    key_grad, value_grad = kernel_call(last_grad_body, (block,) * 2, 2 * product)(
        keys, values, log_decay, docs, core, key_local, value_local, states, states_back, arrived_back
    )
    return query_grad, key_grad, value_grad


def solution(mesh):
    seq, head = mesh.devices.shape
    fine = Mesh(mesh.devices.reshape(seq // 2, 2, head), ("chip", "core", "head"))
    tokens = ("chip", "core")
    block = P("head", tokens, None)
    return jax.shard_map(
        per_device,
        mesh=fine,
        in_specs=(block, block, block, block, P("head", None), P("head", tokens), P(tokens)),
        out_specs=(block, block, block),
        check_vma=False,
    )
```

time: 166 us -> 57.8 us (0.35)
  the two profiles are of different devices: /device:TPU:455 before, /device:TPU:199 now
where the time goes in v1:
time: 57.8 us; the launch traced here: 57.4 us
  blocking collectives  25.8 us (45%)
  waiting for transfers between devices  11.3 us (20%)
  starting transfers between devices  9.24 us (16%)
  Pallas kernels  6.39 us (11%)
  local copies, waits for them, and re-layouts  3.89 us (7%)
  between operations  0.76 us (1%)
    all_to_all x1, blocking collectives, per_device(): sums = lax.all_to_all(sums, 'head', 0, 0, tiled=True)  13.5 us
    ppermute x1, waiting for transfers between devices, per_device(): lax.ppermute(chip_back, ('chip', 'core'), [(a, b) for a, b in behind if b...  7.04 us
    ppermute x1, starting transfers between devices, per_device(): lax.ppermute(chip_state, ('chip', 'core'), [(a, b) for a, b in ahead if b...  6.19 us
    ppermute x1, waiting for transfers between devices, per_device(): lax.ppermute(chip_state, ('chip', 'core'), [(a, b) for a, b in ahead if b...  4.28 us
    all_gather x1, blocking collectives, per_device(): arrived_back = lax.all_gather(moved_back, 'core')  4.09 us
    unnamed x20, local copies, waits for them, and re-layouts  3.89 us
    all_gather x1, blocking collectives, per_device(): states_back = lax.all_gather(own_back, 'core')  3.44 us
    ppermute x1, starting transfers between devices, per_device(): lax.ppermute(chip_back, ('chip', 'core'), [(a, b) for a, b in behind if b...  3.06 us
  transfers between devices with their start and end apart: 2, of which 2 were waited for; matrix products, arithmetic and copies ran while one was open for 0% of the time, Pallas kernels for 6%

profile of v1, /device:TPU:199, one launch (start us, length us, event | category | flops | bytes accessed | tf_op | source)
XLA Modules:
  0.0 57.4 jit_solution(12799377245851864544)
XLA Ops:
  0.6 0.0 copy-start.8
  0.6 0.6 %copy-done.8 = s32[128]{0:T(128)S(1)} copy-done((s32[128]{0:T(128)S(1)}, s32[128]{0:T(128)}, u32[]{:S(2)}) %copy-start.8) | copy-done | bytes 536
  1.3 0.0 copy-start
  1.3 0.9 %copy-done = f32[4,128,128]{2,1,0:T(8,128)S(1)} copy-done((f32[4,128,128]{2,1,0:T(8,128)S(1)}, f32[4,128,128]{2,1,0:T(8,128)}, u32[]{:S(2)}) %copy-start) | copy-done | bytes 262168
  2.2 0.0 copy-start.2
  2.2 0.9 %copy-done.2 = f32[4,128,128]{2,1,0:T(8,128)S(1)} copy-done((f32[4,128,128]{2,1,0:T(8,128)S(1)}, f32[4,128,128]{2,1,0:T(8,128)}, u32[]{:S(2)}) %copy-start.2) | copy-done | bytes 262168
  3.2 0.0 copy-start.6
  3.2 0.7 %copy-done.6 = f32[4,128]{1,0:T(4,128)S(1)} copy-done((f32[4,128]{1,0:T(4,128)S(1)}, f32[4,128]{1,0:T(4,128)}, u32[]{:S(2)}) %copy-start.6) | copy-done | bytes 2072
  3.9 0.6 %shard_map.94 = f32[520,128]{1,0:T(8,128)S(1)} custom-call(f32[4,128,128]{2,1,0:T(8,128)S(1)} %copy-done, f32[4,128,128]{2,1,0:T(8,128)S(1)} %copy-done.2, f32[4,128]{1,0:T(4,128)S(1)} %copy-done.6, s32[1,128]{1,0:T(1,128)S(1)} %bitcast.18), custom_call_target="tpu_custom_call" | custom-call | flops 50331648 | bytes 1048576 | tf_op jit(solution)/shard_map/pallas_call | solution.py:229
  4.5 0.0 copy-start.5
  4.5 2.6 %all-gather = f32[1040,128]{1,0:T(8,128)S(1)} all-gather(f32[520,128]{1,0:T(8,128)S(1)} %shard_map.94), channel_id=2, replica_groups=mesh['chip'=48,'core'=2,'head'=8] {'core'}, dimensions={0}, use_global_device_ids=true | all-gather | bytes 798720 | tf_op jit(solution)/shard_map/all_gather | solution.py:230
  7.2 6.2 %collective-permute-start = (f32[520,128]{1,0:T(8,128)S(1)}, f32[520,128]{1,0:T(8,128)S(1)}, u32[]{:S(2)}, u32[]{:S(2)}) collective-permute-start(f32[520,128]{1,0:T(8,128)S(1)} %shard_map.95.sent), channel_id=1, source_target_pairs={{0,16},{8,40},{16,32},{24,56},{32,48},{40,72},{48,64},{56,88},{64,... | collective-permute-start | bytes 798728 | tf_op jit(solution)/shard_map/ppermute | solution.py:233
  13.4 0.0 copy-start.9
  13.4 0.0 copy-start.7
  13.4 0.0 copy-done.5
  13.4 0.0 copy-done.1
  13.4 0.0 copy-done.3
  13.4 0.0 copy-done.4
  13.4 0.6 %copy-done.9 = f32[4,128]{1,0:T(4,128)S(1)} copy-done((f32[4,128]{1,0:T(4,128)S(1)}, f32[4,128]{1,0:T(4,128)}, u32[]{:S(2)}) %copy-start.9) | copy-done | bytes 2072
  14.1 0.0 copy-done.7
  14.1 1.2 %shard_map.96 = (f32[4,128,128]{2,1,0:T(8,128)S(1)}, f32[4,128,128]{2,1,0:T(8,128)S(1)}, f32[4,128,128]{2,1,0:T(8,128)S(1)}, f32[4,128,128]{2,1,0:T(8,128)S(1)}, f32[4,128,128]{2,1,0:T(8,128)S(1)}) custom-call(f32[4,128,128]{2,1,0:T(8,128)S(1)} %copy-done.4, f32[4,128,128]{2,1,0:T(8,128)S(1)} %copy-done.1, f32[4,128,128]{2,1,0:T(8,128)S(1)} %copy-done.3, ...), custom_call_target="tpu_custom_call" | custom-call | flops 100663296 | bytes 1048576 | tf_op jit(solution)/shard_map/pallas_call | solution.py:234
  15.3 4.3 %collective-permute-done = f32[520,128]{1,0:T(8,128)S(1)} collective-permute-done((f32[520,128]{1,0:T(8,128)S(1)}, f32[520,128]{1,0:T(8,128)S(1)}, u32[]{:S(2)}, u32[]{:S(2)}) %collective-permute-start) | collective-permute-done | bytes 266272 | tf_op jit(solution)/shard_map/ppermute | solution.py:233
  19.6 2.2 %all-gather.1 = f32[1040,128]{1,0:T(8,128)S(1)} all-gather(f32[520,128]{1,0:T(8,128)S(1)} %collective-permute-done), channel_id=3, replica_groups=mesh['chip'=48,'core'=2,'head'=8] {'core'}, dimensions={0}, use_global_device_ids=true | all-gather | bytes 798720 | tf_op jit(solution)/shard_map/all_gather | solution.py:237
  21.7 0.4 shard_map.97
  22.2 13.5 %all_to_all.11 = f32[8,8,128]{2,1,0:T(8,128)S(1)} all-to-all(f32[8,8,128]{2,1,0:T(8,128)S(1)} %bitcast.17), channel_id=1, replica_groups=mesh['chip'=48,'core'=2,'head'=8] {'head'}, dimensions={0} | all-to-all | bytes 65536 | tf_op jit(solution)/shard_map/all_to_all | solution.py:241
  35.7 0.4 shard_map.98
  36.1 3.4 %all-gather.2 = f32[1024,128]{1,0:T(8,128)S(1)} all-gather(f32[512,128]{1,0:T(8,128)S(1)} %get-tuple-element.29), channel_id=4, replica_groups=mesh['chip'=48,'core'=2,'head'=8] {'core'}, dimensions={0}, use_global_device_ids=true | all-gather | bytes 786432 | tf_op jit(solution)/shard_map/all_gather | solution.py:245
  39.5 3.1 %collective-permute-start.1 = (f32[520,128]{1,0:T(8,128)S(1)}, f32[520,128]{1,0:T(8,128)S(1)}, u32[]{:S(2)}, u32[]{:S(2)}) collective-permute-start(f32[520,128]{1,0:T(8,128)S(1)} %shard_map.99.sent), channel_id=1, source_target_pairs={{16,0},{32,16},{40,8},{48,32},{56,24},{64,48},{72,40},{80,64},{88,... | collective-permute-start | bytes 798728 | tf_op jit(solution)/shard_map/ppermute | solution.py:250
  42.6 2.4 %shard_map.100 = (f32[4,128,128]{2,1,0:T(8,128)}, f32[4,128,128]{2,1,0:T(8,128)S(1)}, f32[4,128,128]{2,1,0:T(8,128)S(1)}) custom-call(f32[4,128,128]{2,1,0:T(8,128)S(1)} %copy-done.4, f32[4,128,128]{2,1,0:T(8,128)S(1)} %copy-done.1, f32[4,128,128]{2,1,0:T(8,128)S(1)} %copy-done.3, f32[4,128,128]{2,1,0:T(8,128)S(1)} %get-tuple-element.19.within, ...), custom_call_target="tpu_custom_call" | custom-call | flops 251658240 | bytes 1048576 | tf_op jit(solution)/shard_map/pallas_call | solution.py:251
  45.0 7.0 %collective-permute-done.1 = f32[520,128]{1,0:T(8,128)S(1)} collective-permute-done((f32[520,128]{1,0:T(8,128)S(1)}, f32[520,128]{1,0:T(8,128)S(1)}, u32[]{:S(2)}, u32[]{:S(2)}) %collective-permute-start.1) | collective-permute-done | bytes 266272 | tf_op jit(solution)/shard_map/ppermute | solution.py:250
  52.0 4.1 %all-gather.3 = f32[1040,128]{1,0:T(8,128)S(1)} all-gather(f32[520,128]{1,0:T(8,128)S(1)} %collective-permute-done.1), channel_id=5, replica_groups=mesh['chip'=48,'core'=2,'head'=8] {'core'}, dimensions={0}, use_global_device_ids=true | all-gather | bytes 798720 | tf_op jit(solution)/shard_map/all_gather | solution.py:254
  56.1 1.3 %shard_map.101 = (f32[4,128,128]{2,1,0:T(8,128)}, f32[4,128,128]{2,1,0:T(8,128)}) custom-call(f32[4,128,128]{2,1,0:T(8,128)S(1)} %copy-done.1, f32[4,128,128]{2,1,0:T(8,128)S(1)} %copy-done.3, f32[4,128]{1,0:T(4,128)S(1)} %copy-done.7, s32[1,128]{1,0:T(1,128)S(1)} %bitcast.21, s32[1,1]{1,0:T(1,128)} %bitcast.2.core, ...), custom_call_target="tpu_custom_call" | custom-call | flops 100663296 | bytes 1048576 | tf_op jit(solution)/shard_map/pallas_call | solution.py:255
  (5 shorter events, 0.1 us)
Async XLA Ops:
  0.6 0.7 %copy-start.8 = (s32[128]{0:T(128)S(1)}, s32[128]{0:T(128)}, u32[]{:S(2)}) copy-start(s32[128]{0:T(128)} %param.13) | copy-start | bytes 1540
  1.3 0.9 %copy-start = (f32[4,128,128]{2,1,0:T(8,128)S(1)}, f32[4,128,128]{2,1,0:T(8,128)}, u32[]{:S(2)}) copy-start(f32[4,128,128]{2,1,0:T(8,128)} %keys.7) | copy-start | bytes 786436
  2.2 0.9 %copy-start.2 = (f32[4,128,128]{2,1,0:T(8,128)S(1)}, f32[4,128,128]{2,1,0:T(8,128)}, u32[]{:S(2)}) copy-start(f32[4,128,128]{2,1,0:T(8,128)} %values.7) | copy-start | bytes 786436
  3.2 0.7 %copy-start.6 = (f32[4,128]{1,0:T(4,128)S(1)}, f32[4,128]{1,0:T(4,128)}, u32[]{:S(2)}) copy-start(f32[4,128]{1,0:T(4,128)} %decay.7) | copy-start | bytes 6148
  4.5 8.9 %copy-start.5 = (f32[4,128,128]{2,1,0:T(8,128)S(1)}, f32[4,128,128]{2,1,0:T(8,128)}, u32[]{:S(2)}) copy-start(f32[4,128,128]{2,1,0:T(8,128)} %out_grad.1) | copy-start | bytes 786436
  7.1 6.3 %copy-start.1 = (f32[4,128,128]{2,1,0:T(8,128)S(1)}, f32[4,128,128]{2,1,0:T(8,128)}, u32[]{:S(2)}) copy-start(f32[4,128,128]{2,1,0:T(8,128)} %keys.7) | copy-start | bytes 786436
  7.1 6.3 %copy-start.3 = (f32[4,128,128]{2,1,0:T(8,128)S(1)}, f32[4,128,128]{2,1,0:T(8,128)}, u32[]{:S(2)}) copy-start(f32[4,128,128]{2,1,0:T(8,128)} %values.7) | copy-start | bytes 786436
  7.1 6.3 %copy-start.4 = (f32[4,128,128]{2,1,0:T(8,128)S(1)}, f32[4,128,128]{2,1,0:T(8,128)}, u32[]{:S(2)}) copy-start(f32[4,128,128]{2,1,0:T(8,128)} %queries.5) | copy-start | bytes 786436
  7.2 12.4 %collective-permute-start = (f32[520,128]{1,0:T(8,128)S(1)}, f32[520,128]{1,0:T(8,128)S(1)}, u32[]{:S(2)}, u32[]{:S(2)}) collective-permute-start(f32[520,128]{1,0:T(8,128)S(1)} %shard_map.95.sent), channel_id=1, source_target_pairs={{0,16},{8,40},{16,32},{24,56},{32,48},{40,72},{48,64},{56,88},{64,... | collective-permute-start | bytes 798728 | tf_op jit(solution)/shard_map/ppermute | solution.py:233
  13.4 0.7 %copy-start.9 = (f32[4,128]{1,0:T(4,128)S(1)}, f32[4,128]{1,0:T(4,128)}, u32[]{:S(2)}) copy-start(f32[4,128]{1,0:T(4,128)} %gain.1) | copy-start | bytes 6148
  13.4 0.7 %copy-start.7 = (f32[4,128]{1,0:T(4,128)S(1)}, f32[4,128]{1,0:T(4,128)}, u32[]{:S(2)}) copy-start(f32[4,128]{1,0:T(4,128)} %decay.7) | copy-start | bytes 6148
  39.5 12.5 %collective-permute-start.1 = (f32[520,128]{1,0:T(8,128)S(1)}, f32[520,128]{1,0:T(8,128)S(1)}, u32[]{:S(2)}, u32[]{:S(2)}) collective-permute-start(f32[520,128]{1,0:T(8,128)S(1)} %shard_map.99.sent), channel_id=1, source_target_pairs={{16,0},{32,16},{40,8},{48,32},{56,24},{64,48},{72,40},{80,64},{88,... | collective-permute-start | bytes 798728 | tf_op jit(solution)/shard_map/ppermute | solution.py:250

commit v2 on v1

--- a/solution.py
+++ b/solution.py
@@ -28,13 +28,26 @@
     return one(left[0], right[0]) + (one(left[0], right[1]) + one(left[1], right[0]))
 
 
-def kernel_call(body, outs, flops):
-    return pl.pallas_call(
-        body,
-        out_shape=outs,
-        compiler_params=pltpu.CompilerParams(vmem_limit_bytes=VMEM_LIMIT),
-        cost_estimate=pl.CostEstimate(flops=flops, bytes_accessed=2**20, transcendentals=0),
-    )
+def kernel_call(body, outs, flops, kinds="", out_kinds="", scratch=()):
+    spaces = {"h": pltpu.HBM, "s": pltpu.SMEM, "v": pltpu.VMEM}
+
+    def call(*operands):
+        of = [pl.BlockSpec(memory_space=spaces[c]) for c in kinds.ljust(len(operands), "v")]
+        more = {}
+        if out_kinds:
+            made = [pl.BlockSpec(memory_space=spaces[c]) for c in out_kinds]
+            more["out_specs"] = tuple(made)
+        return pl.pallas_call(
+            body,
+            out_shape=outs,
+            in_specs=of,
+            scratch_shapes=list(scratch),
+            compiler_params=pltpu.CompilerParams(vmem_limit_bytes=VMEM_LIMIT),
+            cost_estimate=pl.CostEstimate(flops=flops, bytes_accessed=2**20, transcendentals=0),
+            **more,
+        )(*operands)
+
+    return call
 
 
 def as_columns(row, rows):
@@ -51,23 +64,41 @@
     return jnp.sum(jnp.where(lower, decay_row, 0.0), axis=1, keepdims=True)
 
 
-def state_body(keys, values, decay, docs, out):
+def state_body(
+    queries_hbm, keys_hbm, values_hbm, cotangent_hbm, gain_hbm, decay_hbm, docs_hbm,
+    out, queries, keys, values, cotangent, gain, decay, docs, arrival,
+):
     heads, rows, width = keys.shape
+    pairs = [(docs_hbm, docs), (decay_hbm, decay)]
+    for h in range(heads):
+        pairs += [(keys_hbm.at[h], keys.at[h]), (values_hbm.at[h], values.at[h])]
+    pairs += [(gain_hbm, gain), (queries_hbm, queries), (cotangent_hbm, cotangent)]
+    copies = [pltpu.make_async_copy(a, b, arrival.at[i]) for i, (a, b) in enumerate(pairs)]
+    for copy in copies:
+        copy.start()
     lower = lower_mask(rows)
+    base = heads * rows
+    copies[0].wait()
     label_row = docs[...].astype(F32)
     label = as_columns(label_row, rows)[:, :1]
     last, first = label_row[:, rows - 1 :], label_row[:, :1]
-    base = heads * rows
-    for h in range(heads):
-        cumulative = running(lower, decay[h : h + 1, :])
-        total = cumulative[rows - 1 :, :]
-        weight = jnp.where(label == last, jnp.exp(total - cumulative), 0.0)
-        state = dot3(split(keys[h] * weight), split(values[h]), TN)
-        out[h * width : (h + 1) * width, :] = state
-        out[base + h : base + h + 1, :] = jnp.broadcast_to(total, (1, width))
     out[base + LAST : base + LAST + 1, :] = jnp.broadcast_to(last, (1, width))
     out[base + FIRST : base + FIRST + 1, :] = jnp.broadcast_to(first, (1, width))
     out[base + FIRST + 1 : base + EXTRA, :] = jnp.zeros((EXTRA - FIRST - 1, width), F32)
+    copies[1].wait()
+    weights = []
+    for h in range(heads):
+        cumulative = running(lower, decay[h : h + 1, :])
+        total = cumulative[rows - 1 :, :]
+        weights.append(jnp.where(label == last, jnp.exp(total - cumulative), 0.0))
+        out[base + h : base + h + 1, :] = jnp.broadcast_to(total, (1, width))
+    for h in range(heads):
+        copies[2 + 2 * h].wait()
+        copies[3 + 2 * h].wait()
+        state = dot3(split(keys[h] * weights[h]), split(values[h]), TN)
+        out[h * width : (h + 1) * width, :] = state
+    for copy in copies[2 + 2 * heads :]:
+        copy.wait()
 
 
 def chip_meta(both, out, base, heads):
@@ -126,7 +157,7 @@
         started[h] = queries[h] * from_start
 
 
-def attended_body(queries, out_local, scaled, decay, docs, core, states, arrived, attended, prior, from_prior, sums):
+def attended_body(core, queries, out_local, scaled, decay, docs, states, arrived, attended, prior, from_prior, sums):
     heads, rows, width = queries.shape
     base = heads * width
     lower = lower_mask(rows)
@@ -191,28 +222,35 @@
         value_local[h] = dot3(split(weighted[h]), of_grad, TN)
 
 
-def last_grad_body(keys, values, decay, docs, core, key_local, value_local, meta, states, arrived, key_grad, value_grad):
+def last_grad_body(
+    core, keys, values, decay, docs, key_local, value_local, meta, states, arrived,
+    key_grad_hbm, value_grad_hbm, key_grad, value_grad, sent,
+):
     heads, rows, width = keys.shape
     base = heads * width
     lower = lower_mask(rows)
-    label = as_columns(docs[...].astype(F32), rows)
     first = core[0, 0] == 0
     near = row_of(arrived, 0, base + FIRST)
     chained = near == row_of(arrived, 1, base + FIRST)
     inner = row_of(meta, 1, base + FIRST)
     linked = inner == near
-    ahead = jnp.where(first, inner, near)
+    ahead = as_columns(docs[...].astype(F32), rows) == jnp.where(first, inner, near)
+    copies = []
     for h in range(heads):
         at = slice(h * width, (h + 1) * width)
         weight = jnp.where(chained, jnp.exp(row_of(arrived, 0, base + h)), 0.0)
         state = arrived[0, at, :] + weight * arrived[1, at, :]
         passed = jnp.where(linked, jnp.exp(row_of(meta, 1, base + h)), 0.0)
-        state = jnp.where(first, passed, 1.0) * state + jnp.where(first, states[1, at, :], 0.0)
-        of_state = split(state)
+        of_state = split(jnp.where(first, states[1, at, :] + passed * state, state))
         cumulative = running(lower, decay[h : h + 1, :])
-        to_next = jnp.where(label == ahead, jnp.exp(cumulative[rows - 1 :, :] - cumulative), 0.0)
+        to_next = jnp.where(ahead, jnp.exp(cumulative[rows - 1 :, :] - cumulative), 0.0)
         key_grad[h] = key_local[h] + to_next * dot3(split(values[h]), of_state, NT)
         value_grad[h] = value_local[h] + to_next * dot3(split(keys[h]), of_state, NN)
+        for i, (a, b) in enumerate(((key_grad, key_grad_hbm), (value_grad, value_grad_hbm))):
+            copies.append(pltpu.make_async_copy(a.at[h], b.at[h], sent.at[2 * h + i]))
+            copies[-1].start()
+    for copy in copies:
+        copy.wait()
 
 
 def per_device(queries, keys, values, out_grad, norm_gain, log_decay, doc_ids):
@@ -226,7 +264,14 @@
     payload = shape(heads * width + EXTRA, width)
     product = 6 * heads * rows * width * width
 
-    own = kernel_call(state_body, payload, product)(keys, values, log_decay, docs)
+    given = [queries, keys, values, out_grad, norm_gain, log_decay, docs]
+    own, queries, keys, values, out_grad, norm_gain, log_decay, docs = kernel_call(
+        state_body,
+        (payload, *(jax.ShapeDtypeStruct(a.shape, a.dtype) for a in given)),
+        product,
+        "h" * len(given),
+        scratch=(pltpu.SemaphoreType.DMA((2 * heads + 5,)),),
+    )(*(pltpu.with_memory_space_constraint(a, pltpu.HBM) for a in given))
     states = lax.all_gather(own, "core")
     chip_state = kernel_call(functools.partial(forward_join_body, heads), payload, product // 64)(states)
     ahead = [(i, i + 2 + 2 * (i % 2)) for i in range(seq)]
@@ -236,8 +281,8 @@
     )
     arrived = lax.all_gather(moved, "core")
     attended, prior, from_prior, sums = kernel_call(
-        attended_body, (block, block, block, shape(8 * group, rows)), product
-    )(queries, out_local, scaled, log_decay, docs, core, states, arrived)
+        attended_body, (block, block, block, shape(8 * group, rows)), product, "s"
+    )(core, queries, out_local, scaled, log_decay, docs, states, arrived)
     sums = lax.all_to_all(sums, "head", 0, 0, tiled=True)
     grad, own_back = kernel_call(
         functools.partial(grad_state_body, heads * width * group), (block, shape(heads * width, width)), product
@@ -252,9 +297,15 @@
         queries, keys, values, within, weighted, grad, prior, from_prior, chip_back
     )
     arrived_back = lax.all_gather(moved_back, "core")
-    key_grad, value_grad = kernel_call(last_grad_body, (block,) * 2, 2 * product)(
-        keys, values, log_decay, docs, core, key_local, value_local, states, states_back, arrived_back
-    )
+    held = pltpu.VMEM((heads, rows, width), F32)
+    key_grad, value_grad = kernel_call(
+        last_grad_body,
+        (block,) * 2,
+        2 * product,
+        "s",
+        "hh",
+        (held, held, pltpu.SemaphoreType.DMA((2 * heads,))),
+    )(core, keys, values, log_decay, docs, key_local, value_local, states, states_back, arrived_back)
     return query_grad, key_grad, value_grad
 
 

time: 57.8 us -> 55.6 us (0.962)
  local copies, waits for them, and re-layouts: 3.89 us -> 0 us
  Pallas kernels: 6.39 us -> 7.9 us
  waiting for transfers between devices: 11.3 us -> 12 us
    unnamed x20 -> x0, local copies, waits for them, and re-layouts: 3.89 us -> none
    pallas_call x8, Pallas kernels: 6.39 us -> 7.9 us  [call(): pl.pallas_call(body, out_shape=outs, in_specs=of, scratch_shapes=list(scr...]
    ppermute x1, waiting for transfers between devices: 4.28 us -> 4.97 us  [per_device(): lax.ppermute(chip_state, ('chip', 'core'), [(a, b) for a, b in ahead if b...]
where the time goes in v2:
time: 55.6 us; the launch traced here: 55.4 us
  blocking collectives  25.7 us (46%)
  waiting for transfers between devices  12 us (22%)
  starting transfers between devices  9.11 us (16%)
  Pallas kernels  7.9 us (14%)
  between operations  0.69 us (1%)
    all_to_all x1, blocking collectives, per_device(): sums = lax.all_to_all(sums, 'head', 0, 0, tiled=True)  13.5 us
    pallas_call x8, Pallas kernels, call(): pl.pallas_call(body, out_shape=outs, in_specs=of, scratch_shapes=list(scr...  7.9 us
    ppermute x1, waiting for transfers between devices, per_device(): lax.ppermute(chip_back, ('chip', 'core'), [(a, b) for a, b in behind if b...  7.05 us
    ppermute x1, starting transfers between devices, per_device(): lax.ppermute(chip_state, ('chip', 'core'), [(a, b) for a, b in ahead if b...  6.05 us
    ppermute x1, waiting for transfers between devices, per_device(): lax.ppermute(chip_state, ('chip', 'core'), [(a, b) for a, b in ahead if b...  4.97 us
    all_gather x1, blocking collectives, per_device(): arrived_back = lax.all_gather(moved_back, 'core')  4.08 us
    all_gather x1, blocking collectives, per_device(): states_back = lax.all_gather(own_back, 'core')  3.44 us
    ppermute x1, starting transfers between devices, per_device(): lax.ppermute(chip_back, ('chip', 'core'), [(a, b) for a, b in behind if b...  3.06 us
  transfers between devices with their start and end apart: 2, of which 2 were waited for; matrix products, arithmetic and copies ran while one was open for 0% of the time, Pallas kernels for 6%

profile of v2, /device:TPU:199, one launch (start us, length us, event | category | flops | bytes accessed | tf_op | source)
XLA Modules:
  0.0 55.4 jit_solution(12509450841032652007)
XLA Ops:
  0.6 2.2 %shard_map.94 = (f32[520,128]{1,0:T(8,128)S(1)}, f32[4,128,128]{2,1,0:T(8,128)S(1)}, f32[4,128,128]{2,1,0:T(8,128)S(1)}, f32[4,128,128]{2,1,0:T(8,128)S(1)}, f32...) custom-call(f32[4,128,128]{2,1,0:T(8,128)} %queries_hbm.1, ...), custom_call_target="tpu_custom_call" | custom-call | flops 50331648 | bytes 1048576 | tf_op jit(solution)/shard_map/pallas_call | solution.py:40
  2.9 2.5 %all-gather = f32[1040,128]{1,0:T(8,128)S(1)} all-gather(f32[520,128]{1,0:T(8,128)S(1)} %get-tuple-element.34), channel_id=2, replica_groups=mesh['chip'=48,'core'=2,'head'=8] {'core'}, dimensions={0}, use_global_device_ids=true | all-gather | bytes 798720 | tf_op jit(solution)/shard_map/all_gather | solution.py:275
  5.4 6.1 %collective-permute-start = (f32[520,128]{1,0:T(8,128)S(1)}, f32[520,128]{1,0:T(8,128)S(1)}, u32[]{:S(2)}, u32[]{:S(2)}) collective-permute-start(f32[520,128]{1,0:T(8,128)S(1)} %shard_map.95.sent), channel_id=1, source_target_pairs={{0,16},{8,40},{16,32},{24,56},{32,48},{40,72},{48,64},{56,88},{64,... | collective-permute-start | bytes 798728 | tf_op jit(solution)/shard_map/ppermute | solution.py:278
  11.5 1.2 %shard_map.96 = (f32[4,128,128]{2,1,0:T(8,128)S(1)}, f32[4,128,128]{2,1,0:T(8,128)S(1)}, f32[4,128,128]{2,1,0:T(8,128)S(1)}, f32[4,128,128]{2,1,0:T(8,128)S(1)}, f32[4,128,128]{2,1,0:T(8,128)S(1)}) custom-call(f32[4,128,128]{2,1,0:T(8,128)S(1)} %get-tuple-element.27.queries, f32[4,128,128]{2,1,0:T(8,128)S(1)} %get-tuple-element.28.keys, ...), custom_call_target="tpu_custom_call" | custom-call | flops 100663296 | bytes 1048576 | tf_op jit(solution)/shard_map/pallas_call | solution.py:40
  12.7 5.0 %collective-permute-done = f32[520,128]{1,0:T(8,128)S(1)} collective-permute-done((f32[520,128]{1,0:T(8,128)S(1)}, f32[520,128]{1,0:T(8,128)S(1)}, u32[]{:S(2)}, u32[]{:S(2)}) %collective-permute-start) | collective-permute-done | bytes 266272 | tf_op jit(solution)/shard_map/ppermute | solution.py:278
  17.7 2.2 %all-gather.1 = f32[1040,128]{1,0:T(8,128)S(1)} all-gather(f32[520,128]{1,0:T(8,128)S(1)} %collective-permute-done), channel_id=3, replica_groups=mesh['chip'=48,'core'=2,'head'=8] {'core'}, dimensions={0}, use_global_device_ids=true | all-gather | bytes 798720 | tf_op jit(solution)/shard_map/all_gather | solution.py:282
  19.8 0.4 shard_map.97
  20.2 13.5 %all_to_all.11 = f32[8,8,128]{2,1,0:T(8,128)S(1)} all-to-all(f32[8,8,128]{2,1,0:T(8,128)S(1)} %bitcast.17), channel_id=1, replica_groups=mesh['chip'=48,'core'=2,'head'=8] {'head'}, dimensions={0} | all-to-all | bytes 65536 | tf_op jit(solution)/shard_map/all_to_all | solution.py:286
  33.7 0.4 shard_map.98
  34.1 3.4 %all-gather.2 = f32[1024,128]{1,0:T(8,128)S(1)} all-gather(f32[512,128]{1,0:T(8,128)S(1)} %get-tuple-element.45), channel_id=4, replica_groups=mesh['chip'=48,'core'=2,'head'=8] {'core'}, dimensions={0}, use_global_device_ids=true | all-gather | bytes 786432 | tf_op jit(solution)/shard_map/all_gather | solution.py:290
  37.6 3.1 %collective-permute-start.1 = (f32[520,128]{1,0:T(8,128)S(1)}, f32[520,128]{1,0:T(8,128)S(1)}, u32[]{:S(2)}, u32[]{:S(2)}) collective-permute-start(f32[520,128]{1,0:T(8,128)S(1)} %shard_map.99.sent), channel_id=1, source_target_pairs={{16,0},{32,16},{40,8},{48,32},{56,24},{64,48},{72,40},{80,64},{88,... | collective-permute-start | bytes 798728 | tf_op jit(solution)/shard_map/ppermute | solution.py:295
  40.7 2.4 %shard_map.100 = (f32[4,128,128]{2,1,0:T(8,128)}, f32[4,128,128]{2,1,0:T(8,128)S(1)}, f32[4,128,128]{2,1,0:T(8,128)S(1)}) custom-call(f32[4,128,128]{2,1,0:T(8,128)S(1)} %get-tuple-element.27.queries, f32[4,128,128]{2,1,0:T(8,128)S(1)} %get-tuple-element.28.keys, f32[4,128,128]{2,1,0:T(8,128)S(1)} %get-tuple-element.29.values, ...), custom_call_target="tpu_custom_call" | custom-call | flops 251658240 | bytes 1048576 | tf_op jit(solution)/shard_map/pallas_call | solution.py:40
  43.0 7.0 %collective-permute-done.1 = f32[520,128]{1,0:T(8,128)S(1)} collective-permute-done((f32[520,128]{1,0:T(8,128)S(1)}, f32[520,128]{1,0:T(8,128)S(1)}, u32[]{:S(2)}, u32[]{:S(2)}) %collective-permute-start.1) | collective-permute-done | bytes 266272 | tf_op jit(solution)/shard_map/ppermute | solution.py:295
  50.1 4.1 %all-gather.3 = f32[1040,128]{1,0:T(8,128)S(1)} all-gather(f32[520,128]{1,0:T(8,128)S(1)} %collective-permute-done.1), channel_id=5, replica_groups=mesh['chip'=48,'core'=2,'head'=8] {'core'}, dimensions={0}, use_global_device_ids=true | all-gather | bytes 798720 | tf_op jit(solution)/shard_map/all_gather | solution.py:299
  54.2 1.2 %shard_map.101 = (f32[4,128,128]{2,1,0:T(8,128)}, f32[4,128,128]{2,1,0:T(8,128)}) custom-call(s32[1,1]{1,0:T(1,128)} %bitcast.2.core, f32[4,128,128]{2,1,0:T(8,128)S(1)} %get-tuple-element.28.keys, f32[4,128,128]{2,1,0:T(8,128)S(1)} %get-tuple-element.29.values, f32[4,128]{1,0:T(4,128)S(1)} %get-tuple-element.32.decay, s32[1,128]{1,0:T(1,128)S(1)} %get-tuple-element.33.docs, ...), custom_call_target="tpu_custom_call" | custom-call | flops 100663296 | bytes 1048576 | tf_op jit(solution)/shard_map/pallas_call | solution.py:40
  (2 shorter events, 0.1 us)
Async XLA Ops:
  5.4 12.3 %collective-permute-start = (f32[520,128]{1,0:T(8,128)S(1)}, f32[520,128]{1,0:T(8,128)S(1)}, u32[]{:S(2)}, u32[]{:S(2)}) collective-permute-start(f32[520,128]{1,0:T(8,128)S(1)} %shard_map.95.sent), channel_id=1, source_target_pairs={{0,16},{8,40},{16,32},{24,56},{32,48},{40,72},{48,64},{56,88},{64,... | collective-permute-start | bytes 798728 | tf_op jit(solution)/shard_map/ppermute | solution.py:278
  37.6 12.5 %collective-permute-start.1 = (f32[520,128]{1,0:T(8,128)S(1)}, f32[520,128]{1,0:T(8,128)S(1)}, u32[]{:S(2)}, u32[]{:S(2)}) collective-permute-start(f32[520,128]{1,0:T(8,128)S(1)} %shard_map.99.sent), channel_id=1, source_target_pairs={{16,0},{32,16},{40,8},{48,32},{56,24},{64,48},{72,40},{80,64},{88,... | collective-permute-start | bytes 798728 | tf_op jit(solution)/shard_map/ppermute | solution.py:295

commit v3 on v2

--- a/solution.py
+++ b/solution.py
@@ -65,14 +65,14 @@
 
 
 def state_body(
-    queries_hbm, keys_hbm, values_hbm, cotangent_hbm, gain_hbm, decay_hbm, docs_hbm,
-    out, queries, keys, values, cotangent, gain, decay, docs, arrival,
+    keys_hbm, values_hbm, gain_hbm, decay_hbm, docs_hbm,
+    out, keys, values, gain, decay, docs, arrival,
 ):
     heads, rows, width = keys.shape
     pairs = [(docs_hbm, docs), (decay_hbm, decay)]
     for h in range(heads):
         pairs += [(keys_hbm.at[h], keys.at[h]), (values_hbm.at[h], values.at[h])]
-    pairs += [(gain_hbm, gain), (queries_hbm, queries), (cotangent_hbm, cotangent)]
+    pairs.append((gain_hbm, gain))
     copies = [pltpu.make_async_copy(a, b, arrival.at[i]) for i, (a, b) in enumerate(pairs)]
     for copy in copies:
         copy.start()
@@ -188,19 +188,16 @@
         [
             jnp.sum(squares.T, axis=0, keepdims=True),
             jnp.sum(inners.T, axis=0, keepdims=True),
-            jnp.zeros((6, rows), F32),
         ],
         axis=0,
     )
-    for i in range(sums.shape[0] // 8):
-        sums[8 * i : 8 * i + 8, :] = two
+    for i in range(sums.shape[0]):
+        sums[i] = two
 
 
 def grad_state_body(width_all, sums, attended, scaled, started, grad, out):
     heads, rows, width = attended.shape
-    total = sums[0:8, :]
-    for i in range(1, sums.shape[0] // 8):
-        total += sums[8 * i : 8 * i + 8, :]
+    total = jnp.sum(sums[...], axis=0)
     inverse_row = lax.rsqrt(total[0:1, :] / width_all + EPSILON)
     coupling_row = total[1:2, :] / width_all * inverse_row * inverse_row
     inverse = as_columns(inverse_row, rows)
@@ -211,24 +208,33 @@
         out[h * width : (h + 1) * width, :] = dot3(split(started[h]), split(value), TN)
 
 
-def main_grad_body(queries, keys, values, within, weighted, grad, prior, from_prior, sent, query_grad, key_local, value_local):
+def main_grad_body(
+    queries, keys, values, decay, within, weighted, grad, prior, from_prior, sent,
+    query_grad, key_local, value_local, tails, *halves,
+):
     del sent
+    lower = lower_mask(queries.shape[1])
     for h in range(queries.shape[0]):
         of_grad = split(grad[h])
         of_keys = split(keys[h])
-        of_both = split(within[h] * dot3(of_grad, split(values[h]), NT))
+        of_values = split(values[h])
+        of_both = split(within[h] * dot3(of_grad, of_values, NT))
         query_grad[h] = dot3(of_both, of_keys, NN) + from_prior[h] * dot3(of_grad, split(prior[h]), NT)
         key_local[h] = dot3(of_both, split(queries[h]), TN)
         value_local[h] = dot3(split(weighted[h]), of_grad, TN)
+        for half, part in zip(halves, (*of_keys, *of_values)):
+            half[h] = part
+        cumulative = running(lower, decay[h : h + 1, :])
+        tail = jnp.exp(cumulative[queries.shape[1] - 1 :, :] - cumulative)
+        tails[h] = jnp.broadcast_to(tail, tails.shape[1:])
 
 
 def last_grad_body(
-    core, keys, values, decay, docs, key_local, value_local, meta, states, arrived,
-    key_grad_hbm, value_grad_hbm, key_grad, value_grad, sent,
+    core, keys_high, keys_low, values_high, values_low, tails, docs, key_local, value_local,
+    meta, states, arrived, key_grad_hbm, value_grad_hbm, key_grad, value_grad, sent,
 ):
-    heads, rows, width = keys.shape
+    heads, rows, width = tails.shape
     base = heads * width
-    lower = lower_mask(rows)
     first = core[0, 0] == 0
     near = row_of(arrived, 0, base + FIRST)
     chained = near == row_of(arrived, 1, base + FIRST)
@@ -242,10 +248,9 @@
         state = arrived[0, at, :] + weight * arrived[1, at, :]
         passed = jnp.where(linked, jnp.exp(row_of(meta, 1, base + h)), 0.0)
         of_state = split(jnp.where(first, states[1, at, :] + passed * state, state))
-        cumulative = running(lower, decay[h : h + 1, :])
-        to_next = jnp.where(ahead, jnp.exp(cumulative[rows - 1 :, :] - cumulative), 0.0)
-        key_grad[h] = key_local[h] + to_next * dot3(split(values[h]), of_state, NT)
-        value_grad[h] = value_local[h] + to_next * dot3(split(keys[h]), of_state, NN)
+        to_next = jnp.where(ahead, tails[h], 0.0)
+        key_grad[h] = key_local[h] + to_next * dot3((values_high[h], values_low[h]), of_state, NT)
+        value_grad[h] = value_local[h] + to_next * dot3((keys_high[h], keys_low[h]), of_state, NN)
         for i, (a, b) in enumerate(((key_grad, key_grad_hbm), (value_grad, value_grad_hbm))):
             copies.append(pltpu.make_async_copy(a.at[h], b.at[h], sent.at[2 * h + i]))
             copies[-1].start()
@@ -264,13 +269,13 @@
     payload = shape(heads * width + EXTRA, width)
     product = 6 * heads * rows * width * width
 
-    given = [queries, keys, values, out_grad, norm_gain, log_decay, docs]
-    own, queries, keys, values, out_grad, norm_gain, log_decay, docs = kernel_call(
+    given = [keys, values, norm_gain, log_decay, docs]
+    own, keys, values, norm_gain, log_decay, docs = kernel_call(
         state_body,
         (payload, *(jax.ShapeDtypeStruct(a.shape, a.dtype) for a in given)),
         product,
         "h" * len(given),
-        scratch=(pltpu.SemaphoreType.DMA((2 * heads + 5,)),),
+        scratch=(pltpu.SemaphoreType.DMA((2 * heads + 3,)),),
     )(*(pltpu.with_memory_space_constraint(a, pltpu.HBM) for a in given))
     states = lax.all_gather(own, "core")
     chip_state = kernel_call(functools.partial(forward_join_body, heads), payload, product // 64)(states)
@@ -281,7 +286,7 @@
     )
     arrived = lax.all_gather(moved, "core")
     attended, prior, from_prior, sums = kernel_call(
-        attended_body, (block, block, block, shape(8 * group, rows)), product, "s"
+        attended_body, (block, block, block, shape(group, 2, rows)), product, "s"
     )(core, queries, out_local, scaled, log_decay, docs, states, arrived)
     sums = lax.all_to_all(sums, "head", 0, 0, tiled=True)
     grad, own_back = kernel_call(
@@ -293,8 +298,11 @@
     )
     behind = [(i, i - 2 - 2 * (i % 2)) for i in range(seq)]
     moved_back = lax.ppermute(chip_back, ("chip", "core"), [(a, b) for a, b in behind if b >= 0])
-    query_grad, key_local, value_local = kernel_call(main_grad_body, (block,) * 3, 5 * product)(
-        queries, keys, values, within, weighted, grad, prior, from_prior, chip_back
+    half = jax.ShapeDtypeStruct((heads, rows, width), BF16)
+    query_grad, key_local, value_local, tails, *halves = kernel_call(
+        main_grad_body, (block,) * 4 + (half,) * 4, 5 * product
+    )(
+        queries, keys, values, log_decay, within, weighted, grad, prior, from_prior, chip_back
     )
     arrived_back = lax.all_gather(moved_back, "core")
     held = pltpu.VMEM((heads, rows, width), F32)
@@ -305,7 +313,7 @@
         "s",
         "hh",
         (held, held, pltpu.SemaphoreType.DMA((2 * heads,))),
-    )(core, keys, values, log_decay, docs, key_local, value_local, states, states_back, arrived_back)
+    )(core, *halves, tails, docs, key_local, value_local, states, states_back, arrived_back)
     return query_grad, key_grad, value_grad
 
 

time: 55.6 us -> 55.5 us (level)
  transfers between devices with their start and end apart: 2 -> 2, of which waited for: 2 -> 2; matrix products, arithmetic and copies ran while one was open for 0% -> 0% of each run, Pallas kernels for 6% -> 7%
where the time goes in v3:
time: 55.5 us; the launch traced here: 55.2 us
  blocking collectives  25.4 us (46%)
  waiting for transfers between devices  12 us (22%)
  starting transfers between devices  9.24 us (17%)
  Pallas kernels  7.88 us (14%)
  between operations  0.71 us (1%)
    all_to_all x1, blocking collectives, per_device(): sums = lax.all_to_all(sums, 'head', 0, 0, tiled=True)  13.2 us
    pallas_call x8, Pallas kernels, call(): pl.pallas_call(body, out_shape=outs, in_specs=of, scratch_shapes=list(scr...  7.88 us
    ppermute x1, waiting for transfers between devices, per_device(): lax.ppermute(chip_back, ('chip', 'core'), [(a, b) for a, b in behind if b...  7.05 us
    ppermute x1, starting transfers between devices, per_device(): lax.ppermute(chip_state, ('chip', 'core'), [(a, b) for a, b in ahead if b...  6.19 us
    ppermute x1, waiting for transfers between devices, per_device(): lax.ppermute(chip_state, ('chip', 'core'), [(a, b) for a, b in ahead if b...  4.95 us
    all_gather x1, blocking collectives, per_device(): arrived_back = lax.all_gather(moved_back, 'core')  4.08 us
    all_gather x1, blocking collectives, per_device(): states_back = lax.all_gather(own_back, 'core')  3.45 us
    ppermute x1, starting transfers between devices, per_device(): lax.ppermute(chip_back, ('chip', 'core'), [(a, b) for a, b in behind if b...  3.05 us
  transfers between devices with their start and end apart: 2, of which 2 were waited for; matrix products, arithmetic and copies ran while one was open for 0% of the time, Pallas kernels for 7%

profile of v3, /device:TPU:199, one launch (start us, length us, event | category | flops | bytes accessed | tf_op | source)
XLA Modules:
  0.0 55.2 jit_solution(4393985701923853335)
XLA Ops:
  0.6 2.2 %shard_map.94 = (f32[520,128]{1,0:T(8,128)S(1)}, f32[4,128,128]{2,1,0:T(8,128)S(1)}, f32[4,128,128]{2,1,0:T(8,128)S(1)}, f32[4,128]{1,0:T(4,128)S(1)}, f32[4,128]{1,0:T(4,128)S(1)}, /*index=5*/s32[1,128]{1,0:T(1,128)S(1)}) custom-call(f32[4,128,128]{2,1,0:T(8,128)} %keys_hbm.1, f32[4,128,128]{2,1,0:T(8,128)} %values_hbm.1, f32[4,128]{1,0:T(4,128)} %gain_hbm.1, ...), custom_call_target="tpu_custom_call" | custom-call | flops 50331648 | bytes 1048576 | tf_op jit(solution)/shard_map/pallas_call | solution.py:40
  2.9 2.5 %all-gather = f32[1040,128]{1,0:T(8,128)S(1)} all-gather(f32[520,128]{1,0:T(8,128)S(1)} %get-tuple-element.35), channel_id=2, replica_groups=mesh['chip'=48,'core'=2,'head'=8] {'core'}, dimensions={0}, use_global_device_ids=true | all-gather | bytes 798720 | tf_op jit(solution)/shard_map/all_gather | solution.py:280
  5.3 0.0 copy-start
  5.4 0.0 copy-start.1
  5.4 6.2 %collective-permute-start = (f32[520,128]{1,0:T(8,128)S(1)}, f32[520,128]{1,0:T(8,128)S(1)}, u32[]{:S(2)}, u32[]{:S(2)}) collective-permute-start(f32[520,128]{1,0:T(8,128)S(1)} %shard_map.95.sent), channel_id=1, source_target_pairs={{0,16},{8,40},{16,32},{24,56},{32,48},{40,72},{48,64},{56,88},{64,... | collective-permute-start | bytes 798728 | tf_op jit(solution)/shard_map/ppermute | solution.py:283
  11.6 0.0 copy-done
  11.6 0.0 copy-done.1
  11.6 1.2 %shard_map.96 = (f32[4,128,128]{2,1,0:T(8,128)S(1)}, f32[4,128,128]{2,1,0:T(8,128)S(1)}, f32[4,128,128]{2,1,0:T(8,128)S(1)}, f32[4,128,128]{2,1,0:T(8,128)S(1)}, f32[4,128,128]{2,1,0:T(8,128)S(1)}) custom-call(f32[4,128,128]{2,1,0:T(8,128)S(1)} %copy-done, f32[4,128,128]{2,1,0:T(8,128)S(1)} %get-tuple-element.30.keys, ...), custom_call_target="tpu_custom_call" | custom-call | flops 100663296 | bytes 1048576 | tf_op jit(solution)/shard_map/pallas_call | solution.py:40
  12.8 4.9 %collective-permute-done = f32[520,128]{1,0:T(8,128)S(1)} collective-permute-done((f32[520,128]{1,0:T(8,128)S(1)}, f32[520,128]{1,0:T(8,128)S(1)}, u32[]{:S(2)}, u32[]{:S(2)}) %collective-permute-start) | collective-permute-done | bytes 266272 | tf_op jit(solution)/shard_map/ppermute | solution.py:283
  17.8 2.2 %all-gather.1 = f32[1040,128]{1,0:T(8,128)S(1)} all-gather(f32[520,128]{1,0:T(8,128)S(1)} %collective-permute-done), channel_id=3, replica_groups=mesh['chip'=48,'core'=2,'head'=8] {'core'}, dimensions={0}, use_global_device_ids=true | all-gather | bytes 798720 | tf_op jit(solution)/shard_map/all_gather | solution.py:287
  19.9 0.4 shard_map.97
  20.4 13.2 %all_to_all.5.sums = f32[8,2,128]{2,1,0:T(2,128)S(1)} all-to-all(f32[8,2,128]{2,1,0:T(2,128)S(1)} %get-tuple-element.40), channel_id=1, replica_groups=mesh['chip'=48,'core'=2,'head'=8] {'head'}, dimensions={0} | all-to-all | bytes 16384 | tf_op jit(solution)/shard_map/all_to_all | solution.py:291
  33.5 0.4 shard_map.98
  33.9 3.5 %all-gather.2 = f32[1024,128]{1,0:T(8,128)S(1)} all-gather(f32[512,128]{1,0:T(8,128)S(1)} %get-tuple-element.46), channel_id=4, replica_groups=mesh['chip'=48,'core'=2,'head'=8] {'core'}, dimensions={0}, use_global_device_ids=true | all-gather | bytes 786432 | tf_op jit(solution)/shard_map/all_gather | solution.py:295
  37.4 3.1 %collective-permute-start.1 = (f32[520,128]{1,0:T(8,128)S(1)}, f32[520,128]{1,0:T(8,128)S(1)}, u32[]{:S(2)}, u32[]{:S(2)}) collective-permute-start(f32[520,128]{1,0:T(8,128)S(1)} %shard_map.99.sent), channel_id=1, source_target_pairs={{16,0},{32,16},{40,8},{48,32},{56,24},{64,48},{72,40},{80,64},{88,... | collective-permute-start | bytes 798728 | tf_op jit(solution)/shard_map/ppermute | solution.py:300
  40.5 2.4 %shard_map.100 = (f32[4,128,128]{2,1,0:T(8,128)}, f32[4,128,128]{2,1,0:T(8,128)S(1)}, f32[4,128,128]{2,1,0:T(8,128)S(1)}, f32[4,128,128]{2,1,0:T(8,128)S(1)}, bf...) custom-call(f32[4,128,128]{2,1,0:T(8,128)S(1)} %copy-done, ...), custom_call_target="tpu_custom_call" | custom-call | flops 251658240 | bytes 1048576 | tf_op jit(solution)/shard_map/pallas_call | solution.py:40
  42.9 7.0 %collective-permute-done.1 = f32[520,128]{1,0:T(8,128)S(1)} collective-permute-done((f32[520,128]{1,0:T(8,128)S(1)}, f32[520,128]{1,0:T(8,128)S(1)}, u32[]{:S(2)}, u32[]{:S(2)}) %collective-permute-start.1) | collective-permute-done | bytes 266272 | tf_op jit(solution)/shard_map/ppermute | solution.py:300
  49.9 4.1 %all-gather.3 = f32[1040,128]{1,0:T(8,128)S(1)} all-gather(f32[520,128]{1,0:T(8,128)S(1)} %collective-permute-done.1), channel_id=5, replica_groups=mesh['chip'=48,'core'=2,'head'=8] {'core'}, dimensions={0}, use_global_device_ids=true | all-gather | bytes 798720 | tf_op jit(solution)/shard_map/all_gather | solution.py:307
  54.0 1.2 %shard_map.101 = (f32[4,128,128]{2,1,0:T(8,128)}, f32[4,128,128]{2,1,0:T(8,128)}) custom-call(s32[1,1]{1,0:T(1,128)} %bitcast.2.core, bf16[4,128,128]{2,1,0:T(8,128)(2,1)S(1)} %get-tuple-element.48.keys_high, bf16[4,128,128]{2,1,0:T(8,128)(2,1)S(1)} %get-tuple-element.49.keys_low, bf16[4,128,128]{2,1,0:T(8,128)(2,1)S(1)} %get-tuple-element.50.values_high, ...), custom_call_target="tpu_custom_call" | custom-call | flops 100663296 | bytes 1048576 | tf_op jit(solution)/shard_map/pallas_call | solution.py:40
  (2 shorter events, 0.1 us)
Async XLA Ops:
  5.3 6.2 %copy-start = (f32[4,128,128]{2,1,0:T(8,128)S(1)}, f32[4,128,128]{2,1,0:T(8,128)}, u32[]{:S(2)}) copy-start(f32[4,128,128]{2,1,0:T(8,128)} %queries.5) | copy-start | bytes 786436
  5.4 6.2 %copy-start.1 = (f32[4,128,128]{2,1,0:T(8,128)S(1)}, f32[4,128,128]{2,1,0:T(8,128)}, u32[]{:S(2)}) copy-start(f32[4,128,128]{2,1,0:T(8,128)} %out_grad.1) | copy-start | bytes 786436
  5.4 12.4 %collective-permute-start = (f32[520,128]{1,0:T(8,128)S(1)}, f32[520,128]{1,0:T(8,128)S(1)}, u32[]{:S(2)}, u32[]{:S(2)}) collective-permute-start(f32[520,128]{1,0:T(8,128)S(1)} %shard_map.95.sent), channel_id=1, source_target_pairs={{0,16},{8,40},{16,32},{24,56},{32,48},{40,72},{48,64},{56,88},{64,... | collective-permute-start | bytes 798728 | tf_op jit(solution)/shard_map/ppermute | solution.py:283
  37.4 12.5 %collective-permute-start.1 = (f32[520,128]{1,0:T(8,128)S(1)}, f32[520,128]{1,0:T(8,128)S(1)}, u32[]{:S(2)}, u32[]{:S(2)}) collective-permute-start(f32[520,128]{1,0:T(8,128)S(1)} %shard_map.99.sent), channel_id=1, source_target_pairs={{16,0},{32,16},{40,8},{48,32},{56,24},{64,48},{72,40},{80,64},{88,... | collective-permute-start | bytes 798728 | tf_op jit(solution)/shard_map/ppermute | solution.py:300

commit v4 on v3

--- a/solution.py
+++ b/solution.py
@@ -14,7 +14,7 @@
 NN = (((1,), (0,)), ((), ()))
 NT = (((1,), (1,)), ((), ()))
 TN = (((0,), (0,)), ((), ()))
-VMEM_LIMIT = 24 * 2**20
+VMEM_LIMIT = 12 * 2**20
 LAST, FIRST, EXTRA = 4, 5, 8
 
 
@@ -124,102 +124,137 @@
     chip_meta(both, out, base, heads)
 
 
-def backward_join_body(heads, both, meta, out):
-    width = out.shape[1]
-    base = heads * width
-    linked = row_of(meta, 0, base + FIRST) == row_of(meta, 1, base + FIRST)
-    for h in range(heads):
-        weight = jnp.where(linked, jnp.exp(row_of(meta, 0, base + h)), 0.0)
-        at = slice(h * width, (h + 1) * width)
-        out[at, :] = both[0, at, :] + weight * both[1, at, :]
-    chip_meta(meta, out, base, heads)
-
-
-def local_body(queries, keys, values, out_grad, gain, decay, docs, sent, out_local, scaled, within, weighted, started):
+def scaled_place(asked, made, h, heads, each, rows):
+    half = heads // 2
+    return (asked, each + h * rows) if h < half else (made, each + (h - half) * rows)
+
+
+def token_rows(asked, made, h, heads, rows):
+    at = slice(h * rows, (h + 1) * rows)
+    of, row = scaled_place(asked, made, h, heads, heads * rows, rows)
+    return asked[at, :], made[at, :], of[row : row + rows, :]
+
+
+def local_body(
+    queries, keys, values, out_grad, gain, decay, docs, sent, asked, made, within, weighted
+):
     del sent
     heads, rows, width = queries.shape
+    each = heads * rows
     lower = lower_mask(rows)
     label_row = docs[...].astype(F32)
-    label = as_columns(label_row, rows)
-    allowed = lower & (label == label_row)
-    first = label_row[:, :1]
+    allowed = lower & (as_columns(label_row, rows) == label_row)
     for h in range(heads):
         cumulative = running(lower, decay[h : h + 1, :])
         spread = cumulative - jnp.broadcast_to(cumulative, (rows, rows)).T
         weight = jnp.where(allowed, jnp.exp(jnp.where(allowed, spread, 0.0)), 0.0)
-        scores = dot3(split(queries[h]), split(keys[h]), NT)
-        both = weight * scores
+        both = weight * dot3(split(queries[h]), split(keys[h]), NT)
         within[h] = weight
         weighted[h] = both
-        out_local[h] = dot3(split(both), split(values[h]), NN)
-        scaled[h] = gain[h : h + 1, :] * out_grad[h]
-        from_start = jnp.where(label[:, :1] == first, jnp.exp(cumulative), 0.0)
-        started[h] = queries[h] * from_start
-
-
-def attended_body(core, queries, out_local, scaled, decay, docs, states, arrived, attended, prior, from_prior, sums):
-    heads, rows, width = queries.shape
+        at = h * rows
+        asked[at : at + rows, :] = queries[h]
+        made[at : at + rows, :] = dot3(split(both), split(values[h]), NN)
+        of, row = scaled_place(asked, made, h, heads, each, rows)
+        of[row : row + rows, :] = gain[h : h + 1, :] * out_grad[h]
+    meta = asked.shape[0] - EXTRA
+    asked[meta : meta + heads, :] = decay[...]
+    asked[meta + heads : meta + EXTRA, :] = jnp.broadcast_to(label_row, (EXTRA - heads, rows))
+
+
+def pick(condition, one, other):
+    return jnp.where(condition, one, other)
+
+
+def link(near_row, far_row, total_row):
+    return jnp.where(near_row == far_row, jnp.exp(total_row), 0.0)
+
+
+def attended_body(core, asked, made, states, arrived, attended, priors, reaches, sums):
+    _, heads, rows, width = attended.shape
     base = heads * width
+    meta = asked.shape[1] - EXTRA
     lower = lower_mask(rows)
-    label = as_columns(docs[...].astype(F32), rows)
     second = core[0, 0] == 1
     near = row_of(arrived, 0, base + LAST)
-    chained = near == row_of(arrived, 1, base + LAST)
     inner = row_of(states, 0, base + LAST)
-    linked = inner == near
-    ahead = jnp.where(second, inner, near)
-    squares = jnp.zeros((rows, width), F32)
-    inners = jnp.zeros((rows, width), F32)
+    allowed = [
+        as_columns(row_of(asked, c, meta + heads), rows) == label
+        for c, label in enumerate((near, inner))
+    ]
+    squares = [jnp.zeros((rows, width), F32)] * 2
+    inners = [jnp.zeros((rows, width), F32)] * 2
     for h in range(heads):
         at = slice(h * width, (h + 1) * width)
-        weight = jnp.where(chained, jnp.exp(row_of(arrived, 0, base + h)), 0.0)
-        state = arrived[0, at, :] + weight * arrived[1, at, :]
-        passed = jnp.where(linked, jnp.exp(row_of(states, 0, base + h)), 0.0)
-        state = jnp.where(second, passed, 1.0) * state + jnp.where(second, states[0, at, :], 0.0)
-        prior[h] = state
-        cumulative = running(lower, decay[h : h + 1, :])
-        reach = jnp.where(label == ahead, jnp.exp(cumulative), 0.0)
-        from_prior[h] = reach
-        value = out_local[h] + reach * dot3(split(queries[h]), split(state), NN)
-        attended[h] = value
-        squares += value * value
-        inners += scaled[h] * value
-    two = jnp.concatenate(
-        [
-            jnp.sum(squares.T, axis=0, keepdims=True),
-            jnp.sum(inners.T, axis=0, keepdims=True),
-        ],
-        axis=0,
-    )
-    for i in range(sums.shape[0]):
-        sums[i] = two
-
-
-def grad_state_body(width_all, sums, attended, scaled, started, grad, out):
-    heads, rows, width = attended.shape
+        far = link(near, row_of(arrived, 1, base + LAST), row_of(arrived, 0, base + h))
+        outer_state = arrived[0, at, :] + far * arrived[1, at, :]
+        passed = link(near, inner, row_of(states, 0, base + h))
+        inner_state = states[0, at, :] + passed * outer_state
+        priors[h] = pick(second, inner_state, outer_state)
+        for c, state in enumerate((outer_state, inner_state)):
+            queries, local, scaled = token_rows(asked.at[c], made.at[c], h, heads, rows)
+            cumulative = running(lower, row_of(asked, c, meta + h))
+            reach = jnp.where(allowed[c], jnp.exp(cumulative), 0.0)
+            reaches[c, h] = reach
+            value = local + reach * dot3(split(queries), split(state), NN)
+            attended[c, h] = value
+            squares[c] += value * value
+            inners[c] += scaled * value
+    for c in range(2):
+        two = jnp.concatenate(
+            [
+                jnp.sum(squares[c].T, axis=0, keepdims=True),
+                jnp.sum(inners[c].T, axis=0, keepdims=True),
+            ],
+            axis=0,
+        )
+        for i in range(sums.shape[0]):
+            sums[i, :, c * rows : (c + 1) * rows] = two
+
+
+def grad_state_body(width_all, sums, attended, asked, made, states, grad, out, back):
+    _, heads, rows, width = attended.shape
+    base = heads * width
+    meta = asked.shape[1] - EXTRA
     total = jnp.sum(sums[...], axis=0)
     inverse_row = lax.rsqrt(total[0:1, :] / width_all + EPSILON)
     coupling_row = total[1:2, :] / width_all * inverse_row * inverse_row
-    inverse = as_columns(inverse_row, rows)
-    coupling = as_columns(coupling_row, rows)
-    for h in range(heads):
-        value = inverse * (scaled[h] - attended[h] * coupling)
-        grad[h] = value
-        out[h * width : (h + 1) * width, :] = dot3(split(started[h]), split(value), TN)
+    lower = lower_mask(rows)
+    first_label = row_of(states, 0, base + FIRST)
+    second_label = row_of(states, 1, base + FIRST)
+    inverse = [as_columns(inverse_row[:, c * rows : (c + 1) * rows], rows) for c in range(2)]
+    coupling = [as_columns(coupling_row[:, c * rows : (c + 1) * rows], rows) for c in range(2)]
+    started = [
+        as_columns(row_of(asked, c, meta + heads), rows) == label
+        for c, label in enumerate((first_label, second_label))
+    ]
+    for h in range(heads):
+        at = slice(h * width, (h + 1) * width)
+        of_cores = []
+        for c in range(2):
+            queries, _, scaled = token_rows(asked.at[c], made.at[c], h, heads, rows)
+            value = inverse[c] * (scaled - attended[c, h] * coupling[c])
+            grad[c, h] = value
+            cumulative = running(lower, row_of(asked, c, meta + h))
+            reach = jnp.where(started[c], jnp.exp(cumulative), 0.0)
+            of_cores.append(dot3(split(queries * reach), split(value), TN))
+        back[at, :] = of_cores[1]
+        passed = link(first_label, second_label, row_of(states, 0, base + h))
+        out[at, :] = of_cores[0] + passed * of_cores[1]
+    chip_meta(states, out, base, heads)
 
 
 def main_grad_body(
-    queries, keys, values, decay, within, weighted, grad, prior, from_prior, sent,
+    core, queries, keys, values, decay, within, weighted, grad, prior, from_prior, sent,
     query_grad, key_local, value_local, tails, *halves,
 ):
     del sent
     lower = lower_mask(queries.shape[1])
     for h in range(queries.shape[0]):
-        of_grad = split(grad[h])
+        of_grad = split(grad[core[0, 0], h])
         of_keys = split(keys[h])
         of_values = split(values[h])
         of_both = split(within[h] * dot3(of_grad, of_values, NT))
-        query_grad[h] = dot3(of_both, of_keys, NN) + from_prior[h] * dot3(of_grad, split(prior[h]), NT)
+        query_grad[h] = dot3(of_both, of_keys, NN) + from_prior[core[0, 0], h] * dot3(of_grad, split(prior[h]), NT)
         key_local[h] = dot3(of_both, split(queries[h]), TN)
         value_local[h] = dot3(split(weighted[h]), of_grad, TN)
         for half, part in zip(halves, (*of_keys, *of_values)):
@@ -231,7 +266,7 @@
 
 def last_grad_body(
     core, keys_high, keys_low, values_high, values_low, tails, docs, key_local, value_local,
-    meta, states, arrived, key_grad_hbm, value_grad_hbm, key_grad, value_grad, sent,
+    meta, back, arrived, key_grad_hbm, value_grad_hbm, key_grad, value_grad, sent,
 ):
     heads, rows, width = tails.shape
     base = heads * width
@@ -247,7 +282,7 @@
         weight = jnp.where(chained, jnp.exp(row_of(arrived, 0, base + h)), 0.0)
         state = arrived[0, at, :] + weight * arrived[1, at, :]
         passed = jnp.where(linked, jnp.exp(row_of(meta, 1, base + h)), 0.0)
-        of_state = split(jnp.where(first, states[1, at, :] + passed * state, state))
+        of_state = split(jnp.where(first, back[at, :] + passed * state, state))
         to_next = jnp.where(ahead, tails[h], 0.0)
         key_grad[h] = key_local[h] + to_next * dot3((values_high[h], values_low[h]), of_state, NT)
         value_grad[h] = value_local[h] + to_next * dot3((keys_high[h], keys_low[h]), of_state, NN)
@@ -281,28 +316,39 @@
     chip_state = kernel_call(functools.partial(forward_join_body, heads), payload, product // 64)(states)
     ahead = [(i, i + 2 + 2 * (i % 2)) for i in range(seq)]
     moved = lax.ppermute(chip_state, ("chip", "core"), [(a, b) for a, b in ahead if b < seq])
-    out_local, scaled, within, weighted, started = kernel_call(local_body, (block,) * 5, 2 * product)(
-        queries, keys, values, out_grad, norm_gain, log_decay, docs, chip_state
-    )
+    more = heads // 2 * rows
+    asked, made, within, weighted = kernel_call(
+        local_body,
+        (
+            shape(heads * rows + more + EXTRA, width),
+            shape(2 * heads * rows - more, width),
+            block,
+            block,
+        ),
+        2 * product,
+    )(queries, keys, values, out_grad, norm_gain, log_decay, docs, chip_state)
+    asked = lax.all_gather(asked, "core")
+    made, asked = lax.optimization_barrier((made, asked))
+    made = lax.all_gather(made, "core")
+    moved, made = lax.optimization_barrier((moved, made))
     arrived = lax.all_gather(moved, "core")
+    twice = shape(2, heads, rows, width)
     attended, prior, from_prior, sums = kernel_call(
-        attended_body, (block, block, block, shape(group, 2, rows)), product, "s"
-    )(core, queries, out_local, scaled, log_decay, docs, states, arrived)
+        attended_body, (twice, block, twice, shape(group, 2, 2 * rows)), 2 * product, "s"
+    )(core, asked, made, states, arrived)
     sums = lax.all_to_all(sums, "head", 0, 0, tiled=True)
-    grad, own_back = kernel_call(
-        functools.partial(grad_state_body, heads * width * group), (block, shape(heads * width, width)), product
-    )(sums, attended, scaled, started)
-    states_back = lax.all_gather(own_back, "core")
-    chip_back = kernel_call(functools.partial(backward_join_body, heads), payload, product // 64)(
-        states_back, states
-    )
+    grad, chip_back, back = kernel_call(
+        functools.partial(grad_state_body, heads * width * group),
+        (twice, payload, shape(heads * width, width)),
+        2 * product,
+    )(sums, attended, asked, made, states)
     behind = [(i, i - 2 - 2 * (i % 2)) for i in range(seq)]
     moved_back = lax.ppermute(chip_back, ("chip", "core"), [(a, b) for a, b in behind if b >= 0])
     half = jax.ShapeDtypeStruct((heads, rows, width), BF16)
     query_grad, key_local, value_local, tails, *halves = kernel_call(
-        main_grad_body, (block,) * 4 + (half,) * 4, 5 * product
+        main_grad_body, (block,) * 4 + (half,) * 4, 5 * product, "s"
     )(
-        queries, keys, values, log_decay, within, weighted, grad, prior, from_prior, chip_back
+        core, queries, keys, values, log_decay, within, weighted, grad, prior, from_prior, chip_back
     )
     arrived_back = lax.all_gather(moved_back, "core")
     held = pltpu.VMEM((heads, rows, width), F32)
@@ -313,7 +359,7 @@
         "s",
         "hh",
         (held, held, pltpu.SemaphoreType.DMA((2 * heads,))),
-    )(core, *halves, tails, docs, key_local, value_local, states, states_back, arrived_back)
+    )(core, *halves, tails, docs, key_local, value_local, states, back, arrived_back)
     return query_grad, key_grad, value_grad
 
 

time: 55.5 us -> 53 us (0.955)
  waiting for transfers between devices: 12 us -> 6.44 us
  blocking collectives: 25.4 us -> 27.7 us
  Pallas kernels: 7.88 us -> 8.47 us
    ppermute x1, waiting for transfers between devices: 4.95 us -> 0.21 us  [per_device(): lax.ppermute(chip_state, ('chip', 'core'), [(a, b) for a, b in ahead if b...]
    all_gather x1 -> x2, blocking collectives: 3.45 us -> 4.73 us  [the longest x1 2.38 us: per_device(): asked = lax.all_gather(asked, 'core')]
    ppermute x1, waiting for transfers between devices: 7.05 us -> 6.23 us  [per_device(): lax.ppermute(chip_back, ('chip', 'core'), [(a, b) for a, b in behind if b...]
    all_gather x1, blocking collectives: 4.08 us -> 4.84 us  [per_device(): arrived_back = lax.all_gather(moved_back, 'core')]
    pallas_call x8 -> x7, Pallas kernels: 7.88 us -> 8.47 us  [call(): pl.pallas_call(body, out_shape=outs, in_specs=of, scratch_shapes=list(scr...]
where the time goes in v4:
time: 53 us; the launch traced here: 52.8 us
  blocking collectives  27.7 us (52%)
  starting transfers between devices  9.39 us (18%)
  Pallas kernels  8.47 us (16%)
  waiting for transfers between devices  6.44 us (12%)
  between operations  0.7 us (1%)
    all_to_all x1, blocking collectives, per_device(): sums = lax.all_to_all(sums, 'head', 0, 0, tiled=True)  13.3 us
    pallas_call x7, Pallas kernels, call(): pl.pallas_call(body, out_shape=outs, in_specs=of, scratch_shapes=list(scr...  8.47 us
    ppermute x1, waiting for transfers between devices, per_device(): lax.ppermute(chip_back, ('chip', 'core'), [(a, b) for a, b in behind if b...  6.23 us
    ppermute x1, starting transfers between devices, per_device(): lax.ppermute(chip_state, ('chip', 'core'), [(a, b) for a, b in ahead if b...  6.19 us
    all_gather x1, blocking collectives, per_device(): arrived_back = lax.all_gather(moved_back, 'core')  4.84 us
    ppermute x1, starting transfers between devices, per_device(): lax.ppermute(chip_back, ('chip', 'core'), [(a, b) for a, b in behind if b...  3.21 us
    all_gather x1, blocking collectives, per_device(): states = lax.all_gather(own, 'core')  2.49 us
    all_gather x1, blocking collectives, per_device(): arrived = lax.all_gather(moved, 'core')  2.39 us
  transfers between devices with their start and end apart: 2, of which 2 were waited for; matrix products, arithmetic and copies ran while one was open for 0% of the time, Pallas kernels for 7%

profile of v4, /device:TPU:199, one launch (start us, length us, event | category | flops | bytes accessed | tf_op | source)
XLA Modules:
  0.0 52.8 jit_solution(8253945103227645362)
XLA Ops:
  0.6 2.2 %shard_map.94 = (f32[520,128]{1,0:T(8,128)S(1)}, f32[4,128,128]{2,1,0:T(8,128)S(1)}, f32[4,128,128]{2,1,0:T(8,128)S(1)}, f32[4,128]{1,0:T(4,128)S(1)}, f32[4,128]{1,0:T(4,128)S(1)}, /*index=5*/s32[1,128]{1,0:T(1,128)S(1)}) custom-call(f32[4,128,128]{2,1,0:T(8,128)} %keys_hbm.1, f32[4,128,128]{2,1,0:T(8,128)} %values_hbm.1, f32[4,128]{1,0:T(4,128)} %gain_hbm.1, ...), custom_call_target="tpu_custom_call" | custom-call | flops 50331648 | bytes 1048576 | tf_op jit(solution)/shard_map/pallas_call | solution.py:40
  2.9 2.5 %all-gather = f32[1040,128]{1,0:T(8,128)S(1)} all-gather(f32[520,128]{1,0:T(8,128)S(1)} %get-tuple-element.39), channel_id=2, replica_groups=mesh['chip'=48,'core'=2,'head'=8] {'core'}, dimensions={0}, use_global_device_ids=true | all-gather | bytes 798720 | tf_op jit(solution)/shard_map/all_gather | solution.py:315
  5.3 0.0 copy-start
  5.4 0.0 copy-start.1
  5.4 6.2 %collective-permute-start = (f32[520,128]{1,0:T(8,128)S(1)}, f32[520,128]{1,0:T(8,128)}, u32[]{:S(2)}, u32[]{:S(2)}) collective-permute-start(f32[520,128]{1,0:T(8,128)S(1)} %shard_map.95.sent), channel_id=1, source_target_pairs={{0,16},{8,40},{16,32},{24,56},{32,48},{40,72},{48,64},{56,88},{64,... | collective-permute-start | bytes 798728 | tf_op jit(solution)/shard_map/ppermute | solution.py:318
  11.6 0.0 copy-done
  11.6 0.0 copy-done.1
  11.6 1.2 %shard_map.96 = (f32[776,128]{1,0:T(8,128)S(1)}, f32[768,128]{1,0:T(8,128)S(1)}, f32[4,128,128]{2,1,0:T(8,128)S(1)}, f32[4,128,128]{2,1,0:T(8,128)S(1)}) custom-call(f32[4,128,128]{2,1,0:T(8,128)S(1)} %copy-done, f32[4,128,128]{2,1,0:T(8,128)S(1)} %get-tuple-element.34.keys, f32[4,128,128]{2,1,0:T(8,128)S(1)} %get-tuple-element.35.values, ...), custom_call_target="tpu_custom_call" | custom-call | flops 100663296 | bytes 1048576 | tf_op jit(solution)/shard_map/pallas_call | solution.py:40
  12.8 2.4 %all-gather.1 = f32[1552,128]{1,0:T(8,128)S(1)} all-gather(f32[776,128]{1,0:T(8,128)S(1)} %get-tuple-element.43), channel_id=3, replica_groups=mesh['chip'=48,'core'=2,'head'=8] {'core'}, dimensions={0}, use_global_device_ids=true | all-gather | bytes 1191936 | tf_op jit(solution)/shard_map/all_gather | solution.py:330
  15.2 2.4 %all-gather.2 = f32[1536,128]{1,0:T(8,128)S(1)} all-gather(f32[768,128]{1,0:T(8,128)S(1)} %get-tuple-element.45), channel_id=4, replica_groups=mesh['chip'=48,'core'=2,'head'=8] {'core'}, dimensions={0}, use_global_device_ids=true | all-gather | bytes 1179648 | tf_op jit(solution)/shard_map/all_gather | solution.py:332
  17.6 0.2 collective-permute-done
  17.8 2.4 %all-gather.3 = f32[1040,128]{1,0:T(8,128)S(1)} all-gather(f32[520,128]{1,0:T(8,128)} %collective-permute-done), channel_id=5, replica_groups=mesh['chip'=48,'core'=2,'head'=8] {'core'}, dimensions={0}, use_global_device_ids=true | all-gather | bytes 798720 | tf_op jit(solution)/shard_map/all_gather | solution.py:334
  20.2 0.6 %shard_map.97 = (f32[2,4,128,128]{3,2,1,0:T(8,128)S(1)}, f32[4,128,128]{2,1,0:T(8,128)S(1)}, f32[2,4,128,128]{3,2,1,0:T(8,128)S(1)}, f32[8,2,256]{2,1,0:T(2,128)S(1)}) custom-call(s32[1,1]{1,0:T(1,128)} %bitcast.core, f32[2,776,128]{2,1,0:T(8,128)S(1)} %bitcast.11, f32[2,768,128]{2,1,0:T(8,128)S(1)} %bitcast.13, f32[2,520,128]{2,1,0:T(8,128)S(1)} %bitcast.8, ...), custom_call_target="tpu_custom_call" | custom-call | flops 100663296 | bytes 1048576 | tf_op jit(solution)/shard_map/pallas_call | solution.py:40
  20.8 13.3 %all_to_all.5.sums = f32[8,2,256]{2,1,0:T(2,128)S(1)} all-to-all(f32[8,2,256]{2,1,0:T(2,128)S(1)} %get-tuple-element.48), channel_id=1, replica_groups=mesh['chip'=48,'core'=2,'head'=8] {'head'}, dimensions={0} | all-to-all | bytes 32768 | tf_op jit(solution)/shard_map/all_to_all | solution.py:339
  34.1 0.8 %shard_map.98 = (f32[2,4,128,128]{3,2,1,0:T(8,128)S(1)}, f32[520,128]{1,0:T(8,128)S(1)}, f32[512,128]{1,0:T(8,128)S(1)}) custom-call(f32[8,2,256]{2,1,0:T(2,128)S(1)} %all_to_all.5.sums, f32[2,4,128,128]{3,2,1,0:T(8,128)S(1)} %get-tuple-element.49.attended, f32[2,776,128]{2,1,0:T(8,128)S(1)} %bitcast.12, f32[2,768,128]{2,1,0:T(8,128)S(1)} %bitcast.14, ...), custom_call_target="tpu_custom_call" | custom-call | flops 100663296 | bytes 1048576 | tf_op jit(solution)/shard_map/pallas_call | solution.py:40
  34.9 3.2 %collective-permute-start.1 = (f32[520,128]{1,0:T(8,128)S(1)}, f32[520,128]{1,0:T(8,128)S(1)}, u32[]{:S(2)}, u32[]{:S(2)}) collective-permute-start(f32[520,128]{1,0:T(8,128)S(1)} %get-tuple-element.53.sent), channel_id=1, source_target_pairs={{16,0},{32,16},{40,8},{48,32},{56,24},{64,48},{72,40},{80,64},{88,... | collective-permute-start | bytes 798728 | tf_op jit(solution)/shard_map/ppermute | solution.py:346
  38.1 2.4 %shard_map.99 = (f32[4,128,128]{2,1,0:T(8,128)}, f32[4,128,128]{2,1,0:T(8,128)S(1)}, f32[4,128,128]{2,1,0:T(8,128)S(1)}, f32[4,128,128]{2,1,0:T(8,128)S(1)}, bf1...) custom-call(s32[1,1]{1,0:T(1,128)} %bitcast.core, ...), custom_call_target="tpu_custom_call" | custom-call | flops 251658240 | bytes 1048576 | tf_op jit(solution)/shard_map/pallas_call | solution.py:40
  40.5 6.2 %collective-permute-done.1 = f32[520,128]{1,0:T(8,128)S(1)} collective-permute-done((f32[520,128]{1,0:T(8,128)S(1)}, f32[520,128]{1,0:T(8,128)S(1)}, u32[]{:S(2)}, u32[]{:S(2)}) %collective-permute-start.1) | collective-permute-done | bytes 266272 | tf_op jit(solution)/shard_map/ppermute | solution.py:346
  46.7 4.8 %all-gather.4 = f32[1040,128]{1,0:T(8,128)S(1)} all-gather(f32[520,128]{1,0:T(8,128)S(1)} %collective-permute-done.1), channel_id=6, replica_groups=mesh['chip'=48,'core'=2,'head'=8] {'core'}, dimensions={0}, use_global_device_ids=true | all-gather | bytes 798720 | tf_op jit(solution)/shard_map/all_gather | solution.py:353
  51.5 1.2 %shard_map.100 = (f32[4,128,128]{2,1,0:T(8,128)}, f32[4,128,128]{2,1,0:T(8,128)}) custom-call(s32[1,1]{1,0:T(1,128)} %bitcast.core, bf16[4,128,128]{2,1,0:T(8,128)(2,1)S(1)} %get-tuple-element.55.keys_high, bf16[4,128,128]{2,1,0:T(8,128)(2,1)S(1)} %get-tuple-element.56.keys_low, bf16[4,128,128]{2,1,0:T(8,128)(2,1)S(1)} %get-tuple-element.57.values_high, ...), custom_call_target="tpu_custom_call" | custom-call | flops 100663296 | bytes 1048576 | tf_op jit(solution)/shard_map/pallas_call | solution.py:40
  (1 shorter events, 0.0 us)
Async XLA Ops:
  5.3 6.2 %copy-start = (f32[4,128,128]{2,1,0:T(8,128)S(1)}, f32[4,128,128]{2,1,0:T(8,128)}, u32[]{:S(2)}) copy-start(f32[4,128,128]{2,1,0:T(8,128)} %queries.3) | copy-start | bytes 786436
  5.4 6.2 %copy-start.1 = (f32[4,128,128]{2,1,0:T(8,128)S(1)}, f32[4,128,128]{2,1,0:T(8,128)}, u32[]{:S(2)}) copy-start(f32[4,128,128]{2,1,0:T(8,128)} %out_grad.1) | copy-start | bytes 786436
  5.4 12.4 %collective-permute-start = (f32[520,128]{1,0:T(8,128)S(1)}, f32[520,128]{1,0:T(8,128)}, u32[]{:S(2)}, u32[]{:S(2)}) collective-permute-start(f32[520,128]{1,0:T(8,128)S(1)} %shard_map.95.sent), channel_id=1, source_target_pairs={{0,16},{8,40},{16,32},{24,56},{32,48},{40,72},{48,64},{56,88},{64,... | collective-permute-start | bytes 798728 | tf_op jit(solution)/shard_map/ppermute | solution.py:318
  34.9 11.8 %collective-permute-start.1 = (f32[520,128]{1,0:T(8,128)S(1)}, f32[520,128]{1,0:T(8,128)S(1)}, u32[]{:S(2)}, u32[]{:S(2)}) collective-permute-start(f32[520,128]{1,0:T(8,128)S(1)} %get-tuple-element.53.sent), channel_id=1, source_target_pairs={{16,0},{32,16},{40,8},{48,32},{56,24},{64,48},{72,40},{80,64},{88,... | collective-permute-start | bytes 798728 | tf_op jit(solution)/shard_map/ppermute | solution.py:346

commit v5 on v4

--- a/solution.py
+++ b/solution.py
@@ -69,10 +69,9 @@
     out, keys, values, gain, decay, docs, arrival,
 ):
     heads, rows, width = keys.shape
-    pairs = [(docs_hbm, docs), (decay_hbm, decay)]
-    for h in range(heads):
-        pairs += [(keys_hbm.at[h], keys.at[h]), (values_hbm.at[h], values.at[h])]
-    pairs.append((gain_hbm, gain))
+    pairs = [
+        (docs_hbm, docs), (decay_hbm, decay), (keys_hbm, keys), (values_hbm, values), (gain_hbm, gain),
+    ]
     copies = [pltpu.make_async_copy(a, b, arrival.at[i]) for i, (a, b) in enumerate(pairs)]
     for copy in copies:
         copy.start()
@@ -92,13 +91,11 @@
         total = cumulative[rows - 1 :, :]
         weights.append(jnp.where(label == last, jnp.exp(total - cumulative), 0.0))
         out[base + h : base + h + 1, :] = jnp.broadcast_to(total, (1, width))
-    for h in range(heads):
-        copies[2 + 2 * h].wait()
-        copies[3 + 2 * h].wait()
+    for copy in copies[2:]:
+        copy.wait()
+    for h in range(heads):
         state = dot3(split(keys[h] * weights[h]), split(values[h]), TN)
         out[h * width : (h + 1) * width, :] = state
-    for copy in copies[2 + 2 * heads :]:
-        copy.wait()
 
 
 def chip_meta(both, out, base, heads):
@@ -169,11 +166,28 @@
     return jnp.where(near_row == far_row, jnp.exp(total_row), 0.0)
 
 
-def attended_body(core, asked, made, states, arrived, attended, priors, reaches, sums):
-    _, heads, rows, width = attended.shape
+def prepare_body(asked, states, high, low, start_high, start_low, passes):
+    _, heads, rows, width = high.shape
     base = heads * width
     meta = asked.shape[1] - EXTRA
     lower = lower_mask(rows)
+    for c in range(2):
+        label = as_columns(row_of(asked, c, meta + heads), rows)
+        started = label == row_of(states, c, base + FIRST)
+        for h in range(heads):
+            queries = asked[c, h * rows : (h + 1) * rows, :]
+            high[c, h], low[c, h] = split(queries)
+            decay = jnp.exp(running(lower, row_of(asked, c, meta + h)))
+            passes[c, h] = jnp.broadcast_to(decay, (rows, width))
+            start_high[c, h], start_low[c, h] = split((queries * jnp.where(started, decay, 0.0)).T)
+
+
+def attended_body(
+    core, asked, made, states, high, low, passes, arrived, attended, priors, reaches, sums
+):
+    _, heads, rows, width = attended.shape
+    base = heads * width
+    meta = asked.shape[1] - EXTRA
     second = core[0, 0] == 1
     near = row_of(arrived, 0, base + LAST)
     inner = row_of(states, 0, base + LAST)
@@ -191,11 +205,10 @@
         inner_state = states[0, at, :] + passed * outer_state
         priors[h] = pick(second, inner_state, outer_state)
         for c, state in enumerate((outer_state, inner_state)):
-            queries, local, scaled = token_rows(asked.at[c], made.at[c], h, heads, rows)
-            cumulative = running(lower, row_of(asked, c, meta + h))
-            reach = jnp.where(allowed[c], jnp.exp(cumulative), 0.0)
+            _, local, scaled = token_rows(asked.at[c], made.at[c], h, heads, rows)
+            reach = jnp.where(allowed[c], passes[c, h], 0.0)
             reaches[c, h] = reach
-            value = local + reach * dot3(split(queries), split(state), NN)
+            value = local + reach * dot3((high[c, h], low[c, h]), split(state), NN)
             attended[c, h] = value
             squares[c] += value * value
             inners[c] += scaled * value
@@ -211,32 +224,26 @@
             sums[i, :, c * rows : (c + 1) * rows] = two
 
 
-def grad_state_body(width_all, sums, attended, asked, made, states, grad, out, back):
+def grad_state_body(
+    width_all, sums, attended, asked, made, states, start_high, start_low, grad, out, back
+):
     _, heads, rows, width = attended.shape
     base = heads * width
-    meta = asked.shape[1] - EXTRA
     total = jnp.sum(sums[...], axis=0)
     inverse_row = lax.rsqrt(total[0:1, :] / width_all + EPSILON)
     coupling_row = total[1:2, :] / width_all * inverse_row * inverse_row
-    lower = lower_mask(rows)
     first_label = row_of(states, 0, base + FIRST)
     second_label = row_of(states, 1, base + FIRST)
     inverse = [as_columns(inverse_row[:, c * rows : (c + 1) * rows], rows) for c in range(2)]
     coupling = [as_columns(coupling_row[:, c * rows : (c + 1) * rows], rows) for c in range(2)]
-    started = [
-        as_columns(row_of(asked, c, meta + heads), rows) == label
-        for c, label in enumerate((first_label, second_label))
-    ]
     for h in range(heads):
         at = slice(h * width, (h + 1) * width)
         of_cores = []
         for c in range(2):
-            queries, _, scaled = token_rows(asked.at[c], made.at[c], h, heads, rows)
+            _, _, scaled = token_rows(asked.at[c], made.at[c], h, heads, rows)
             value = inverse[c] * (scaled - attended[c, h] * coupling[c])
             grad[c, h] = value
-            cumulative = running(lower, row_of(asked, c, meta + h))
-            reach = jnp.where(started[c], jnp.exp(cumulative), 0.0)
-            of_cores.append(dot3(split(queries * reach), split(value), TN))
+            of_cores.append(dot3((start_high[c, h], start_low[c, h]), split(value), NN))
         back[at, :] = of_cores[1]
         passed = link(first_label, second_label, row_of(states, 0, base + h))
         out[at, :] = of_cores[0] + passed * of_cores[1]
@@ -310,7 +317,7 @@
         (payload, *(jax.ShapeDtypeStruct(a.shape, a.dtype) for a in given)),
         product,
         "h" * len(given),
-        scratch=(pltpu.SemaphoreType.DMA((2 * heads + 3,)),),
+        scratch=(pltpu.SemaphoreType.DMA((len(given),)),),
     )(*(pltpu.with_memory_space_constraint(a, pltpu.HBM) for a in given))
     states = lax.all_gather(own, "core")
     chip_state = kernel_call(functools.partial(forward_join_body, heads), payload, product // 64)(states)
@@ -330,18 +337,22 @@
     asked = lax.all_gather(asked, "core")
     made, asked = lax.optimization_barrier((made, asked))
     made = lax.all_gather(made, "core")
-    moved, made = lax.optimization_barrier((moved, made))
+    twice = shape(2, heads, rows, width)
+    halves_twice = jax.ShapeDtypeStruct(twice.shape, BF16)
+    high, low, start_high, start_low, passes = kernel_call(
+        prepare_body, (halves_twice,) * 4 + (twice,), product // 4
+    )(asked, states)
+    moved, made, passes = lax.optimization_barrier((moved, made, passes))
     arrived = lax.all_gather(moved, "core")
-    twice = shape(2, heads, rows, width)
     attended, prior, from_prior, sums = kernel_call(
         attended_body, (twice, block, twice, shape(group, 2, 2 * rows)), 2 * product, "s"
-    )(core, asked, made, states, arrived)
+    )(core, asked, made, states, high, low, passes, arrived)
     sums = lax.all_to_all(sums, "head", 0, 0, tiled=True)
     grad, chip_back, back = kernel_call(
         functools.partial(grad_state_body, heads * width * group),
         (twice, payload, shape(heads * width, width)),
         2 * product,
-    )(sums, attended, asked, made, states)
+    )(sums, attended, asked, made, states, start_high, start_low)
     behind = [(i, i - 2 - 2 * (i % 2)) for i in range(seq)]
     moved_back = lax.ppermute(chip_back, ("chip", "core"), [(a, b) for a, b in behind if b >= 0])
     half = jax.ShapeDtypeStruct((heads, rows, width), BF16)

time: 53 us -> 52 us (0.981)
  Pallas kernels: 8.47 us -> 7.93 us
    pallas_call x7 -> x8, Pallas kernels: 8.47 us -> 7.93 us  [call(): pl.pallas_call(body, out_shape=outs, in_specs=of, scratch_shapes=list(scr...]
  transfers between devices with their start and end apart: 2 -> 2, of which waited for: 2 -> 1; matrix products, arithmetic and copies ran while one was open for 0% -> 0% of each run, Pallas kernels for 7% -> 8%
where the time goes in v5:
time: 52 us; the launch traced here: 51.8 us
  blocking collectives  27.8 us (53%)
  starting transfers between devices  9.13 us (18%)
  Pallas kernels  7.93 us (15%)
  waiting for transfers between devices  6.25 us (12%)
  between operations  0.7 us (1%)
    all_to_all x1, blocking collectives, per_device(): sums = lax.all_to_all(sums, 'head', 0, 0, tiled=True)  13.3 us
    pallas_call x8, Pallas kernels, call(): pl.pallas_call(body, out_shape=outs, in_specs=of, scratch_shapes=list(scr...  7.93 us
    ppermute x1, waiting for transfers between devices, per_device(): lax.ppermute(chip_back, ('chip', 'core'), [(a, b) for a, b in behind if b...  6.24 us
    ppermute x1, starting transfers between devices, per_device(): lax.ppermute(chip_state, ('chip', 'core'), [(a, b) for a, b in ahead if b...  6.18 us
    all_gather x1, blocking collectives, per_device(): arrived_back = lax.all_gather(moved_back, 'core')  4.84 us
    ppermute x1, starting transfers between devices, per_device(): lax.ppermute(chip_back, ('chip', 'core'), [(a, b) for a, b in behind if b...  2.95 us
    all_gather x1, blocking collectives, per_device(): states = lax.all_gather(own, 'core')  2.49 us
    all_gather x1, blocking collectives, per_device(): arrived = lax.all_gather(moved, 'core')  2.39 us
  transfers between devices with their start and end apart: 2, of which 1 were waited for; matrix products, arithmetic and copies ran while one was open for 0% of the time, Pallas kernels for 8%

profile of v5, /device:TPU:199, one launch (start us, length us, event | category | flops | bytes accessed | tf_op | source)
XLA Modules:
  0.0 51.8 jit_solution(12340038616320592924)
XLA Ops:
  0.6 1.5 %shard_map.94 = (f32[520,128]{1,0:T(8,128)S(1)}, f32[4,128,128]{2,1,0:T(8,128)S(1)}, f32[4,128,128]{2,1,0:T(8,128)S(1)}, f32[4,128]{1,0:T(4,128)S(1)}, f32[4,128]{1,0:T(4,128)S(1)}, /*index=5*/s32[1,128]{1,0:T(1,128)S(1)}) custom-call(f32[4,128,128]{2,1,0:T(8,128)} %keys_hbm.1, f32[4,128,128]{2,1,0:T(8,128)} %values_hbm.1, f32[4,128]{1,0:T(4,128)} %gain_hbm.1, ...), custom_call_target="tpu_custom_call" | custom-call | flops 50331648 | bytes 1048576 | tf_op jit(solution)/shard_map/pallas_call | solution.py:40
  2.2 2.5 %all-gather = f32[1040,128]{1,0:T(8,128)S(1)} all-gather(f32[520,128]{1,0:T(8,128)S(1)} %get-tuple-element.45), channel_id=2, replica_groups=mesh['chip'=48,'core'=2,'head'=8] {'core'}, dimensions={0}, use_global_device_ids=true | all-gather | bytes 798720 | tf_op jit(solution)/shard_map/all_gather | solution.py:322
  4.6 0.0 copy-start
  4.7 0.0 copy-start.1
  4.7 6.2 %collective-permute-start = (f32[520,128]{1,0:T(8,128)S(1)}, f32[520,128]{1,0:T(8,128)}, u32[]{:S(2)}, u32[]{:S(2)}) collective-permute-start(f32[520,128]{1,0:T(8,128)S(1)} %shard_map.95.sent), channel_id=1, source_target_pairs={{0,16},{8,40},{16,32},{24,56},{32,48},{40,72},{48,64},{56,88},{64,... | collective-permute-start | bytes 798728 | tf_op jit(solution)/shard_map/ppermute | solution.py:325
  10.9 0.0 copy-done
  10.9 0.0 copy-done.1
  10.9 1.2 %shard_map.96 = (f32[776,128]{1,0:T(8,128)S(1)}, f32[768,128]{1,0:T(8,128)S(1)}, f32[4,128,128]{2,1,0:T(8,128)S(1)}, f32[4,128,128]{2,1,0:T(8,128)S(1)}) custom-call(f32[4,128,128]{2,1,0:T(8,128)S(1)} %copy-done, f32[4,128,128]{2,1,0:T(8,128)S(1)} %get-tuple-element.40.keys, f32[4,128,128]{2,1,0:T(8,128)S(1)} %get-tuple-element.41.values, ...), custom_call_target="tpu_custom_call" | custom-call | flops 100663296 | bytes 1048576 | tf_op jit(solution)/shard_map/pallas_call | solution.py:40
  12.1 2.4 %all-gather.1 = f32[1552,128]{1,0:T(8,128)S(1)} all-gather(f32[776,128]{1,0:T(8,128)S(1)} %get-tuple-element.49), channel_id=3, replica_groups=mesh['chip'=48,'core'=2,'head'=8] {'core'}, dimensions={0}, use_global_device_ids=true | all-gather | bytes 1191936 | tf_op jit(solution)/shard_map/all_gather | solution.py:337
  14.5 0.4 shard_map.97
  15.0 2.4 %all-gather.2 = f32[1536,128]{1,0:T(8,128)S(1)} all-gather(f32[768,128]{1,0:T(8,128)S(1)} %get-tuple-element.51), channel_id=4, replica_groups=mesh['chip'=48,'core'=2,'head'=8] {'core'}, dimensions={0}, use_global_device_ids=true | all-gather | bytes 1179648 | tf_op jit(solution)/shard_map/all_gather | solution.py:339
  17.3 0.0 collective-permute-done
  17.3 2.4 %all-gather.3 = f32[1040,128]{1,0:T(8,128)S(1)} all-gather(f32[520,128]{1,0:T(8,128)} %collective-permute-done), channel_id=5, replica_groups=mesh['chip'=48,'core'=2,'head'=8] {'core'}, dimensions={0}, use_global_device_ids=true | all-gather | bytes 798720 | tf_op jit(solution)/shard_map/all_gather | solution.py:346
  19.7 0.5 %shard_map.98 = (f32[2,4,128,128]{3,2,1,0:T(8,128)S(1)}, f32[4,128,128]{2,1,0:T(8,128)S(1)}, f32[2,4,128,128]{3,2,1,0:T(8,128)S(1)}, f32[8,2,256]{2,1,0:T(2,128)S(1)}) custom-call(s32[1,1]{1,0:T(1,128)} %bitcast.core, f32[2,776,128]{2,1,0:T(8,128)S(1)} %bitcast.13, f32[2,768,128]{2,1,0:T(8,128)S(1)} %bitcast.15, f32[2,520,128]{2,1,0:T(8,128)S(1)} %bitcast.9, ...), custom_call_target="tpu_custom_call" | custom-call | flops 100663296 | bytes 1048576 | tf_op jit(solution)/shard_map/pallas_call | solution.py:40
  20.3 13.3 %all_to_all.5.sums = f32[8,2,256]{2,1,0:T(2,128)S(1)} all-to-all(f32[8,2,256]{2,1,0:T(2,128)S(1)} %get-tuple-element.58), channel_id=1, replica_groups=mesh['chip'=48,'core'=2,'head'=8] {'head'}, dimensions={0} | all-to-all | bytes 32768 | tf_op jit(solution)/shard_map/all_to_all | solution.py:350
  33.6 0.6 %shard_map.99 = (f32[2,4,128,128]{3,2,1,0:T(8,128)S(1)}, f32[520,128]{1,0:T(8,128)S(1)}, f32[512,128]{1,0:T(8,128)S(1)}) custom-call(f32[8,2,256]{2,1,0:T(2,128)S(1)} %all_to_all.5.sums, f32[2,4,128,128]{3,2,1,0:T(8,128)S(1)} %get-tuple-element.59.attended, f32[2,776,128]{2,1,0:T(8,128)S(1)} %bitcast.14, f32[2,768,128]{2,1,0:T(8,128)S(1)} %bitcast.16, ...), custom_call_target="tpu_custom_call" | custom-call | flops 100663296 | bytes 1048576 | tf_op jit(solution)/shard_map/pallas_call | solution.py:40
  34.1 2.9 %collective-permute-start.1 = (f32[520,128]{1,0:T(8,128)S(1)}, f32[520,128]{1,0:T(8,128)S(1)}, u32[]{:S(2)}, u32[]{:S(2)}) collective-permute-start(f32[520,128]{1,0:T(8,128)S(1)} %get-tuple-element.65.sent), channel_id=1, source_target_pairs={{16,0},{32,16},{40,8},{48,32},{56,24},{64,48},{72,40},{80,64},{88,... | collective-permute-start | bytes 798728 | tf_op jit(solution)/shard_map/ppermute | solution.py:357
  37.1 2.4 %shard_map.100 = (f32[4,128,128]{2,1,0:T(8,128)}, f32[4,128,128]{2,1,0:T(8,128)S(1)}, f32[4,128,128]{2,1,0:T(8,128)S(1)}, f32[4,128,128]{2,1,0:T(8,128)S(1)}, bf...) custom-call(s32[1,1]{1,0:T(1,128)} %bitcast.core, ...), custom_call_target="tpu_custom_call" | custom-call | flops 251658240 | bytes 1048576 | tf_op jit(solution)/shard_map/pallas_call | solution.py:40
  39.5 6.2 %collective-permute-done.1 = f32[520,128]{1,0:T(8,128)S(1)} collective-permute-done((f32[520,128]{1,0:T(8,128)S(1)}, f32[520,128]{1,0:T(8,128)S(1)}, u32[]{:S(2)}, u32[]{:S(2)}) %collective-permute-start.1) | collective-permute-done | bytes 266272 | tf_op jit(solution)/shard_map/ppermute | solution.py:357
  45.7 4.8 %all-gather.4 = f32[1040,128]{1,0:T(8,128)S(1)} all-gather(f32[520,128]{1,0:T(8,128)S(1)} %collective-permute-done.1), channel_id=6, replica_groups=mesh['chip'=48,'core'=2,'head'=8] {'core'}, dimensions={0}, use_global_device_ids=true | all-gather | bytes 798720 | tf_op jit(solution)/shard_map/all_gather | solution.py:364
  50.6 1.2 %shard_map.101 = (f32[4,128,128]{2,1,0:T(8,128)}, f32[4,128,128]{2,1,0:T(8,128)}) custom-call(s32[1,1]{1,0:T(1,128)} %bitcast.core, bf16[4,128,128]{2,1,0:T(8,128)(2,1)S(1)} %get-tuple-element.67.keys_high, bf16[4,128,128]{2,1,0:T(8,128)(2,1)S(1)} %get-tuple-element.68.keys_low, bf16[4,128,128]{2,1,0:T(8,128)(2,1)S(1)} %get-tuple-element.69.values_high, ...), custom_call_target="tpu_custom_call" | custom-call | flops 100663296 | bytes 1048576 | tf_op jit(solution)/shard_map/pallas_call | solution.py:40
  (1 shorter events, 0.0 us)
Async XLA Ops:
  4.6 6.2 %copy-start = (f32[4,128,128]{2,1,0:T(8,128)S(1)}, f32[4,128,128]{2,1,0:T(8,128)}, u32[]{:S(2)}) copy-start(f32[4,128,128]{2,1,0:T(8,128)} %queries.3) | copy-start | bytes 786436
  4.7 6.2 %copy-start.1 = (f32[4,128,128]{2,1,0:T(8,128)S(1)}, f32[4,128,128]{2,1,0:T(8,128)}, u32[]{:S(2)}) copy-start(f32[4,128,128]{2,1,0:T(8,128)} %out_grad.1) | copy-start | bytes 786436
  4.7 12.6 %collective-permute-start = (f32[520,128]{1,0:T(8,128)S(1)}, f32[520,128]{1,0:T(8,128)}, u32[]{:S(2)}, u32[]{:S(2)}) collective-permute-start(f32[520,128]{1,0:T(8,128)S(1)} %shard_map.95.sent), channel_id=1, source_target_pairs={{0,16},{8,40},{16,32},{24,56},{32,48},{40,72},{48,64},{56,88},{64,... | collective-permute-start | bytes 798728 | tf_op jit(solution)/shard_map/ppermute | solution.py:325
  34.1 11.6 %collective-permute-start.1 = (f32[520,128]{1,0:T(8,128)S(1)}, f32[520,128]{1,0:T(8,128)S(1)}, u32[]{:S(2)}, u32[]{:S(2)}) collective-permute-start(f32[520,128]{1,0:T(8,128)S(1)} %get-tuple-element.65.sent), channel_id=1, source_target_pairs={{16,0},{32,16},{40,8},{48,32},{56,24},{64,48},{72,40},{80,64},{88,... | collective-permute-start | bytes 798728 | tf_op jit(solution)/shard_map/ppermute | solution.py:357

commit v6 on v5

--- a/solution.py
+++ b/solution.py
@@ -166,6 +166,17 @@
     return jnp.where(near_row == far_row, jnp.exp(total_row), 0.0)
 
 
+def states_ahead(states, arrived, h, width):
+    base = arrived.shape[1] - EXTRA
+    at = slice(h * width, (h + 1) * width)
+    near = row_of(arrived, 0, base + LAST)
+    inner = row_of(states, 0, base + LAST)
+    far = link(near, row_of(arrived, 1, base + LAST), row_of(arrived, 0, base + h))
+    outer_state = arrived[0, at, :] + far * arrived[1, at, :]
+    passed = link(near, inner, row_of(states, 0, base + h))
+    return outer_state, states[0, at, :] + passed * outer_state
+
+
 def prepare_body(asked, states, high, low, start_high, start_low, passes):
     _, heads, rows, width = high.shape
     base = heads * width
@@ -183,12 +194,11 @@
 
 
 def attended_body(
-    core, asked, made, states, high, low, passes, arrived, attended, priors, reaches, sums
+    asked, made, states, high, low, passes, arrived, attended, sums
 ):
     _, heads, rows, width = attended.shape
     base = heads * width
     meta = asked.shape[1] - EXTRA
-    second = core[0, 0] == 1
     near = row_of(arrived, 0, base + LAST)
     inner = row_of(states, 0, base + LAST)
     allowed = [
@@ -198,16 +208,9 @@
     squares = [jnp.zeros((rows, width), F32)] * 2
     inners = [jnp.zeros((rows, width), F32)] * 2
     for h in range(heads):
-        at = slice(h * width, (h + 1) * width)
-        far = link(near, row_of(arrived, 1, base + LAST), row_of(arrived, 0, base + h))
-        outer_state = arrived[0, at, :] + far * arrived[1, at, :]
-        passed = link(near, inner, row_of(states, 0, base + h))
-        inner_state = states[0, at, :] + passed * outer_state
-        priors[h] = pick(second, inner_state, outer_state)
-        for c, state in enumerate((outer_state, inner_state)):
+        for c, state in enumerate(states_ahead(states, arrived, h, width)):
             _, local, scaled = token_rows(asked.at[c], made.at[c], h, heads, rows)
             reach = jnp.where(allowed[c], passes[c, h], 0.0)
-            reaches[c, h] = reach
             value = local + reach * dot3((high[c, h], low[c, h]), split(state), NN)
             attended[c, h] = value
             squares[c] += value * value
@@ -251,33 +254,41 @@
 
 
 def main_grad_body(
-    core, queries, keys, values, decay, within, weighted, grad, prior, from_prior, sent,
+    queries, keys, values, decay, docs, within, weighted, grad, states, arrived, sent,
     query_grad, key_local, value_local, tails, *halves,
 ):
     del sent
-    lower = lower_mask(queries.shape[1])
+    rows, width = queries.shape[1:]
+    base = arrived.shape[1] - EXTRA
+    lower = lower_mask(rows)
+    second = lax.axis_index("core") == 1
+    near = pick(second, row_of(states, 0, base + LAST), row_of(arrived, 0, base + LAST))
+    ahead = as_columns(docs[...].astype(F32), rows) == near
     for h in range(queries.shape[0]):
-        of_grad = split(grad[core[0, 0], h])
+        of_grad = split(grad[lax.axis_index("core"), h])
         of_keys = split(keys[h])
         of_values = split(values[h])
         of_both = split(within[h] * dot3(of_grad, of_values, NT))
-        query_grad[h] = dot3(of_both, of_keys, NN) + from_prior[core[0, 0], h] * dot3(of_grad, split(prior[h]), NT)
+        cumulative = running(lower, decay[h : h + 1, :])
+        outer_state, inner_state = states_ahead(states, arrived, h, width)
+        of_state = split(pick(second, inner_state, outer_state))
+        reach = jnp.where(ahead, jnp.exp(cumulative), 0.0)
+        query_grad[h] = dot3(of_both, of_keys, NN) + reach * dot3(of_grad, of_state, NT)
         key_local[h] = dot3(of_both, split(queries[h]), TN)
         value_local[h] = dot3(split(weighted[h]), of_grad, TN)
         for half, part in zip(halves, (*of_keys, *of_values)):
             half[h] = part
-        cumulative = running(lower, decay[h : h + 1, :])
-        tail = jnp.exp(cumulative[queries.shape[1] - 1 :, :] - cumulative)
+        tail = jnp.exp(cumulative[rows - 1 :, :] - cumulative)
         tails[h] = jnp.broadcast_to(tail, tails.shape[1:])
 
 
 def last_grad_body(
-    core, keys_high, keys_low, values_high, values_low, tails, docs, key_local, value_local,
+    keys_high, keys_low, values_high, values_low, tails, docs, key_local, value_local,
     meta, back, arrived, key_grad_hbm, value_grad_hbm, key_grad, value_grad, sent,
 ):
     heads, rows, width = tails.shape
     base = heads * width
-    first = core[0, 0] == 0
+    first = lax.axis_index("core") == 0
     near = row_of(arrived, 0, base + FIRST)
     chained = near == row_of(arrived, 1, base + FIRST)
     inner = row_of(meta, 1, base + FIRST)
@@ -293,8 +304,11 @@
         to_next = jnp.where(ahead, tails[h], 0.0)
         key_grad[h] = key_local[h] + to_next * dot3((values_high[h], values_low[h]), of_state, NT)
         value_grad[h] = value_local[h] + to_next * dot3((keys_high[h], keys_low[h]), of_state, NN)
+        if h % 2 == 0:
+            continue
         for i, (a, b) in enumerate(((key_grad, key_grad_hbm), (value_grad, value_grad_hbm))):
-            copies.append(pltpu.make_async_copy(a.at[h], b.at[h], sent.at[2 * h + i]))
+            done = slice(h - 1, h + 1)
+            copies.append(pltpu.make_async_copy(a.at[done], b.at[done], sent.at[h - 1 + i]))
             copies[-1].start()
     for copy in copies:
         copy.wait()
@@ -305,7 +319,6 @@
     seq = lax.axis_size("chip") * 2
     group = lax.axis_size("head")
     docs = doc_ids.reshape(1, rows)
-    core = lax.axis_index("core").astype(jnp.int32).reshape(1, 1)
     shape = lambda *dims: jax.ShapeDtypeStruct(dims, F32)
     block = shape(heads, rows, width)
     payload = shape(heads * width + EXTRA, width)
@@ -344,9 +357,9 @@
     )(asked, states)
     moved, made, passes = lax.optimization_barrier((moved, made, passes))
     arrived = lax.all_gather(moved, "core")
-    attended, prior, from_prior, sums = kernel_call(
-        attended_body, (twice, block, twice, shape(group, 2, 2 * rows)), 2 * product, "s"
-    )(core, asked, made, states, high, low, passes, arrived)
+    attended, sums = kernel_call(
+        attended_body, (twice, shape(group, 2, 2 * rows)), 2 * product
+    )(asked, made, states, high, low, passes, arrived)
     sums = lax.all_to_all(sums, "head", 0, 0, tiled=True)
     grad, chip_back, back = kernel_call(
         functools.partial(grad_state_body, heads * width * group),
@@ -357,9 +370,9 @@
     moved_back = lax.ppermute(chip_back, ("chip", "core"), [(a, b) for a, b in behind if b >= 0])
     half = jax.ShapeDtypeStruct((heads, rows, width), BF16)
     query_grad, key_local, value_local, tails, *halves = kernel_call(
-        main_grad_body, (block,) * 4 + (half,) * 4, 5 * product, "s"
+        main_grad_body, (block,) * 4 + (half,) * 4, 5 * product
     )(
-        core, queries, keys, values, log_decay, within, weighted, grad, prior, from_prior, chip_back
+        queries, keys, values, log_decay, docs, within, weighted, grad, states, arrived, chip_back
     )
     arrived_back = lax.all_gather(moved_back, "core")
     held = pltpu.VMEM((heads, rows, width), F32)
@@ -367,10 +380,10 @@
         last_grad_body,
         (block,) * 2,
         2 * product,
-        "s",
+        "",
         "hh",
-        (held, held, pltpu.SemaphoreType.DMA((2 * heads,))),
-    )(core, *halves, tails, docs, key_local, value_local, states, back, arrived_back)
+        (held, held, pltpu.SemaphoreType.DMA((heads,))),
+    )(*halves, tails, docs, key_local, value_local, states, back, arrived_back)
     return query_grad, key_grad, value_grad
 
 

time: 52 us -> 51.7 us (level)
  no operation moved by 1% of the time
where the time goes in v6:
time: 51.7 us; the launch traced here: 51.4 us
  blocking collectives  27.6 us (53%)
  starting transfers between devices  9.04 us (17%)
  Pallas kernels  7.91 us (15%)
  waiting for transfers between devices  6.23 us (12%)
  between operations  0.7 us (1%)
    all_to_all x1, blocking collectives, per_device(): sums = lax.all_to_all(sums, 'head', 0, 0, tiled=True)  13.3 us
    pallas_call x8, Pallas kernels, call(): pl.pallas_call(body, out_shape=outs, in_specs=of, scratch_shapes=list(scr...  7.91 us
    ppermute x1, waiting for transfers between devices, per_device(): lax.ppermute(chip_back, ('chip', 'core'), [(a, b) for a, b in behind if b...  6.22 us
    ppermute x1, starting transfers between devices, per_device(): lax.ppermute(chip_state, ('chip', 'core'), [(a, b) for a, b in ahead if b...  6.18 us
    all_gather x1, blocking collectives, per_device(): arrived_back = lax.all_gather(moved_back, 'core')  4.85 us
    ppermute x1, starting transfers between devices, per_device(): lax.ppermute(chip_back, ('chip', 'core'), [(a, b) for a, b in behind if b...  2.86 us
    all_gather x1, blocking collectives, per_device(): states = lax.all_gather(own, 'core')  2.49 us
    all_gather x1, blocking collectives, per_device(): asked = lax.all_gather(asked, 'core')  2.38 us
  transfers between devices with their start and end apart: 2, of which 1 were waited for; matrix products, arithmetic and copies ran while one was open for 0% of the time, Pallas kernels for 8%

profile of v6, /device:TPU:199, one launch (start us, length us, event | category | flops | bytes accessed | tf_op | source)
XLA Modules:
  0.0 51.4 jit_solution(9098560860155300469)
XLA Ops:
  0.6 1.5 %shard_map.94 = (f32[520,128]{1,0:T(8,128)S(1)}, f32[4,128,128]{2,1,0:T(8,128)S(1)}, f32[4,128,128]{2,1,0:T(8,128)S(1)}, f32[4,128]{1,0:T(4,128)S(1)}, f32[4,128]{1,0:T(4,128)S(1)}, /*index=5*/s32[1,128]{1,0:T(1,128)S(1)}) custom-call(f32[4,128,128]{2,1,0:T(8,128)} %keys_hbm.1, f32[4,128,128]{2,1,0:T(8,128)} %values_hbm.1, f32[4,128]{1,0:T(4,128)} %gain_hbm.1, ...), custom_call_target="tpu_custom_call" | custom-call | flops 50331648 | bytes 1048576 | tf_op jit(solution)/shard_map/pallas_call | solution.py:40
  2.2 2.5 %all-gather = f32[1040,128]{1,0:T(8,128)S(1)} all-gather(f32[520,128]{1,0:T(8,128)S(1)} %get-tuple-element.43), channel_id=2, replica_groups=mesh['chip'=48,'core'=2,'head'=8] {'core'}, dimensions={0}, use_global_device_ids=true | all-gather | bytes 798720 | tf_op jit(solution)/shard_map/all_gather | solution.py:335
  4.6 0.0 copy-start
  4.7 0.0 copy-start.1
  4.7 6.2 %collective-permute-start = (f32[520,128]{1,0:T(8,128)S(1)}, f32[520,128]{1,0:T(8,128)S(1)}, u32[]{:S(2)}, u32[]{:S(2)}) collective-permute-start(f32[520,128]{1,0:T(8,128)S(1)} %shard_map.95.sent), channel_id=1, source_target_pairs={{0,16},{8,40},{16,32},{24,56},{32,48},{40,72},{48,64},{56,88},{64,... | collective-permute-start | bytes 798728 | tf_op jit(solution)/shard_map/ppermute | solution.py:338
  10.9 0.0 copy-done
  10.9 0.0 copy-done.1
  10.9 1.2 %shard_map.96 = (f32[776,128]{1,0:T(8,128)S(1)}, f32[768,128]{1,0:T(8,128)S(1)}, f32[4,128,128]{2,1,0:T(8,128)S(1)}, f32[4,128,128]{2,1,0:T(8,128)S(1)}) custom-call(f32[4,128,128]{2,1,0:T(8,128)S(1)} %copy-done, f32[4,128,128]{2,1,0:T(8,128)S(1)} %get-tuple-element.38.keys, f32[4,128,128]{2,1,0:T(8,128)S(1)} %get-tuple-element.39.values, ...), custom_call_target="tpu_custom_call" | custom-call | flops 100663296 | bytes 1048576 | tf_op jit(solution)/shard_map/pallas_call | solution.py:40
  12.1 2.4 %all-gather.1 = f32[1552,128]{1,0:T(8,128)S(1)} all-gather(f32[776,128]{1,0:T(8,128)S(1)} %get-tuple-element.47), channel_id=3, replica_groups=mesh['chip'=48,'core'=2,'head'=8] {'core'}, dimensions={0}, use_global_device_ids=true | all-gather | bytes 1191936 | tf_op jit(solution)/shard_map/all_gather | solution.py:350
  14.5 0.4 shard_map.97
  15.0 2.4 %all-gather.2 = f32[1536,128]{1,0:T(8,128)S(1)} all-gather(f32[768,128]{1,0:T(8,128)S(1)} %get-tuple-element.49), channel_id=4, replica_groups=mesh['chip'=48,'core'=2,'head'=8] {'core'}, dimensions={0}, use_global_device_ids=true | all-gather | bytes 1179648 | tf_op jit(solution)/shard_map/all_gather | solution.py:352
  17.3 0.0 collective-permute-done
  17.3 2.2 %all-gather.3 = f32[1040,128]{1,0:T(8,128)S(1)} all-gather(f32[520,128]{1,0:T(8,128)S(1)} %collective-permute-done), channel_id=5, replica_groups=mesh['chip'=48,'core'=2,'head'=8] {'core'}, dimensions={0}, use_global_device_ids=true | all-gather | bytes 798720 | tf_op jit(solution)/shard_map/all_gather | solution.py:359
  19.5 0.5 %shard_map.98 = (f32[2,4,128,128]{3,2,1,0:T(8,128)S(1)}, f32[8,2,256]{2,1,0:T(2,128)S(1)}) custom-call(f32[2,776,128]{2,1,0:T(8,128)S(1)} %bitcast.13, f32[2,768,128]{2,1,0:T(8,128)S(1)} %bitcast.15, f32[2,520,128]{2,1,0:T(8,128)S(1)} %bitcast.8, bf16[2,4,128,128]{3,2,1,0:T(8,128)(2,1)S(1)} %get-tuple-element.52.high, ...), custom_call_target="tpu_custom_call" | custom-call | flops 100663296 | bytes 1048576 | tf_op jit(solution)/shard_map/pallas_call | solution.py:40
  20.0 13.3 %all_to_all.5.sums = f32[8,2,256]{2,1,0:T(2,128)S(1)} all-to-all(f32[8,2,256]{2,1,0:T(2,128)S(1)} %get-tuple-element.56), channel_id=1, replica_groups=mesh['chip'=48,'core'=2,'head'=8] {'head'}, dimensions={0} | all-to-all | bytes 32768 | tf_op jit(solution)/shard_map/all_to_all | solution.py:363
  33.3 0.6 %shard_map.99 = (f32[2,4,128,128]{3,2,1,0:T(8,128)S(1)}, f32[520,128]{1,0:T(8,128)S(1)}, f32[512,128]{1,0:T(8,128)S(1)}) custom-call(f32[8,2,256]{2,1,0:T(2,128)S(1)} %all_to_all.5.sums, f32[2,4,128,128]{3,2,1,0:T(8,128)S(1)} %get-tuple-element.57.attended, f32[2,776,128]{2,1,0:T(8,128)S(1)} %bitcast.14, f32[2,768,128]{2,1,0:T(8,128)S(1)} %bitcast.16, ...), custom_call_target="tpu_custom_call" | custom-call | flops 100663296 | bytes 1048576 | tf_op jit(solution)/shard_map/pallas_call | solution.py:40
  33.9 2.9 %collective-permute-start.1 = (f32[520,128]{1,0:T(8,128)S(1)}, f32[520,128]{1,0:T(8,128)S(1)}, u32[]{:S(2)}, u32[]{:S(2)}) collective-permute-start(f32[520,128]{1,0:T(8,128)S(1)} %get-tuple-element.61.sent), channel_id=1, source_target_pairs={{16,0},{32,16},{40,8},{48,32},{56,24},{64,48},{72,40},{80,64},{88,... | collective-permute-start | bytes 798728 | tf_op jit(solution)/shard_map/ppermute | solution.py:370
  36.8 2.4 %shard_map.100 = (f32[4,128,128]{2,1,0:T(8,128)}, f32[4,128,128]{2,1,0:T(8,128)S(1)}, f32[4,128,128]{2,1,0:T(8,128)S(1)}, f32[4,128,128]{2,1,0:T(8,128)S(1)}, bf...) custom-call(f32[4,128,128]{2,1,0:T(8,128)S(1)} %copy-done, ...), custom_call_target="tpu_custom_call" | custom-call | flops 251658240 | bytes 1048576 | tf_op jit(solution)/shard_map/pallas_call | solution.py:40
  39.1 6.2 %collective-permute-done.1 = f32[520,128]{1,0:T(8,128)S(1)} collective-permute-done((f32[520,128]{1,0:T(8,128)S(1)}, f32[520,128]{1,0:T(8,128)S(1)}, u32[]{:S(2)}, u32[]{:S(2)}) %collective-permute-start.1) | collective-permute-done | bytes 266272 | tf_op jit(solution)/shard_map/ppermute | solution.py:370
  45.4 4.8 %all-gather.4 = f32[1040,128]{1,0:T(8,128)S(1)} all-gather(f32[520,128]{1,0:T(8,128)S(1)} %collective-permute-done.1), channel_id=6, replica_groups=mesh['chip'=48,'core'=2,'head'=8] {'core'}, dimensions={0}, use_global_device_ids=true | all-gather | bytes 798720 | tf_op jit(solution)/shard_map/all_gather | solution.py:377
  50.2 1.2 %shard_map.101 = (f32[4,128,128]{2,1,0:T(8,128)}, f32[4,128,128]{2,1,0:T(8,128)}) custom-call(bf16[4,128,128]{2,1,0:T(8,128)(2,1)S(1)} %get-tuple-element.63.keys_high, bf16[4,128,128]{2,1,0:T(8,128)(2,1)S(1)} %get-tuple-element.64.keys_low, bf16[4,128,128]{2,1,0:T(8,128)(2,1)S(1)} %get-tuple-element.65.values_high, ...), custom_call_target="tpu_custom_call" | custom-call | flops 100663296 | bytes 1048576 | tf_op jit(solution)/shard_map/pallas_call | solution.py:40
  (1 shorter events, 0.0 us)
Async XLA Ops:
  4.6 6.2 %copy-start = (f32[4,128,128]{2,1,0:T(8,128)S(1)}, f32[4,128,128]{2,1,0:T(8,128)}, u32[]{:S(2)}) copy-start(f32[4,128,128]{2,1,0:T(8,128)} %queries.3) | copy-start | bytes 786436
  4.7 6.2 %copy-start.1 = (f32[4,128,128]{2,1,0:T(8,128)S(1)}, f32[4,128,128]{2,1,0:T(8,128)}, u32[]{:S(2)}) copy-start(f32[4,128,128]{2,1,0:T(8,128)} %out_grad.1) | copy-start | bytes 786436
  4.7 12.6 %collective-permute-start = (f32[520,128]{1,0:T(8,128)S(1)}, f32[520,128]{1,0:T(8,128)S(1)}, u32[]{:S(2)}, u32[]{:S(2)}) collective-permute-start(f32[520,128]{1,0:T(8,128)S(1)} %shard_map.95.sent), channel_id=1, source_target_pairs={{0,16},{8,40},{16,32},{24,56},{32,48},{40,72},{48,64},{56,88},{64,... | collective-permute-start | bytes 798728 | tf_op jit(solution)/shard_map/ppermute | solution.py:338
  33.9 11.5 %collective-permute-start.1 = (f32[520,128]{1,0:T(8,128)S(1)}, f32[520,128]{1,0:T(8,128)S(1)}, u32[]{:S(2)}, u32[]{:S(2)}) collective-permute-start(f32[520,128]{1,0:T(8,128)S(1)} %get-tuple-element.61.sent), channel_id=1, source_target_pairs={{16,0},{32,16},{40,8},{48,32},{56,24},{64,48},{72,40},{80,64},{88,... | collective-permute-start | bytes 798728 | tf_op jit(solution)/shard_map/ppermute | solution.py:370

commit v7 on v6

--- a/solution.py
+++ b/solution.py
@@ -28,7 +28,7 @@
     return one(left[0], right[0]) + (one(left[0], right[1]) + one(left[1], right[0]))
 
 
-def kernel_call(body, outs, flops, kinds="", out_kinds="", scratch=()):
+def kernel_call(body, outs, flops, kinds="", out_kinds="", scratch=(), aliases=()):
     spaces = {"h": pltpu.HBM, "s": pltpu.SMEM, "v": pltpu.VMEM}
 
     def call(*operands):
@@ -42,6 +42,7 @@
             out_shape=outs,
             in_specs=of,
             scratch_shapes=list(scratch),
+            input_output_aliases=dict(aliases),
             compiler_params=pltpu.CompilerParams(vmem_limit_bytes=VMEM_LIMIT),
             cost_estimate=pl.CostEstimate(flops=flops, bytes_accessed=2**20, transcendentals=0),
             **more,
@@ -100,10 +101,11 @@
 
 def chip_meta(both, out, base, heads):
     width = out.shape[1]
-    out[base : base + heads, :] = both[0, base : base + heads, :] + both[1, base : base + heads, :]
-    out[base + LAST : base + LAST + 1, :] = both[1, base + LAST : base + LAST + 1, :]
-    out[base + FIRST : base + FIRST + 1, :] = both[0, base + FIRST : base + FIRST + 1, :]
-    out[base + FIRST + 1 : base + EXTRA, :] = jnp.zeros((EXTRA - FIRST - 1, width), F32)
+    to = out.shape[0] - EXTRA
+    out[to : to + heads, :] = both[0, base : base + heads, :] + both[1, base : base + heads, :]
+    out[to + LAST : to + LAST + 1, :] = both[1, base + LAST : base + LAST + 1, :]
+    out[to + FIRST : to + FIRST + 1, :] = both[0, base + FIRST : base + FIRST + 1, :]
+    out[to + FIRST + 1 : to + EXTRA, :] = jnp.zeros((EXTRA - FIRST - 1, width), F32)
 
 
 def row_of(ref, which, at):
@@ -228,9 +230,11 @@
 
 
 def grad_state_body(
-    width_all, sums, attended, asked, made, states, start_high, start_low, grad, out, back
-):
+    width_all, sums, attended, asked, made, states, start_high, start_low, grad, *outs_and_back
+):
+    *outs, back = outs_and_back
     _, heads, rows, width = attended.shape
+    each = heads // len(outs)
     base = heads * width
     total = jnp.sum(sums[...], axis=0)
     inverse_row = lax.rsqrt(total[0:1, :] / width_all + EPSILON)
@@ -249,15 +253,17 @@
             of_cores.append(dot3((start_high[c, h], start_low[c, h]), split(value), NN))
         back[at, :] = of_cores[1]
         passed = link(first_label, second_label, row_of(states, 0, base + h))
-        out[at, :] = of_cores[0] + passed * of_cores[1]
-    chip_meta(states, out, base, heads)
+        to = h % each * width
+        outs[h // each][to : to + width, :] = of_cores[0] + passed * of_cores[1]
+    for out in outs:
+        chip_meta(states, out, base, heads)
 
 
 def main_grad_body(
-    queries, keys, values, decay, docs, within, weighted, grad, states, arrived, sent,
+    queries, keys, values, decay, docs, within, weighted, grad, states, arrived, sent, sent_later,
     query_grad, key_local, value_local, tails, *halves,
 ):
-    del sent
+    del sent, sent_later
     rows, width = queries.shape[1:]
     base = arrived.shape[1] - EXTRA
     lower = lower_mask(rows)
@@ -283,33 +289,37 @@
 
 
 def last_grad_body(
-    keys_high, keys_low, values_high, values_low, tails, docs, key_local, value_local,
-    meta, back, arrived, key_grad_hbm, value_grad_hbm, key_grad, value_grad, sent,
-):
+    start, keys_high, keys_low, values_high, values_low, tails, docs, key_local, value_local,
+    meta, back, arrived, *rest,
+):
+    key_grad_hbm, value_grad_hbm, key_grad, value_grad, sent = rest[-5:]
     heads, rows, width = tails.shape
     base = heads * width
+    end = arrived.shape[1] - EXTRA
     first = lax.axis_index("core") == 0
-    near = row_of(arrived, 0, base + FIRST)
-    chained = near == row_of(arrived, 1, base + FIRST)
+    near = row_of(arrived, 0, end + FIRST)
+    chained = near == row_of(arrived, 1, end + FIRST)
     inner = row_of(meta, 1, base + FIRST)
     linked = inner == near
     ahead = as_columns(docs[...].astype(F32), rows) == jnp.where(first, inner, near)
-    copies = []
-    for h in range(heads):
-        at = slice(h * width, (h + 1) * width)
-        weight = jnp.where(chained, jnp.exp(row_of(arrived, 0, base + h)), 0.0)
+    for i in range(end // width):
+        h = start + i
+        at = slice(i * width, (i + 1) * width)
+        weight = jnp.where(chained, jnp.exp(row_of(arrived, 0, end + h)), 0.0)
         state = arrived[0, at, :] + weight * arrived[1, at, :]
         passed = jnp.where(linked, jnp.exp(row_of(meta, 1, base + h)), 0.0)
-        of_state = split(jnp.where(first, back[at, :] + passed * state, state))
+        nearer = back[h * width : (h + 1) * width, :] + passed * state
+        of_state = split(jnp.where(first, nearer, state))
         to_next = jnp.where(ahead, tails[h], 0.0)
-        key_grad[h] = key_local[h] + to_next * dot3((values_high[h], values_low[h]), of_state, NT)
-        value_grad[h] = value_local[h] + to_next * dot3((keys_high[h], keys_low[h]), of_state, NN)
-        if h % 2 == 0:
-            continue
-        for i, (a, b) in enumerate(((key_grad, key_grad_hbm), (value_grad, value_grad_hbm))):
-            done = slice(h - 1, h + 1)
-            copies.append(pltpu.make_async_copy(a.at[done], b.at[done], sent.at[h - 1 + i]))
-            copies[-1].start()
+        key_grad[i] = key_local[h] + to_next * dot3((values_high[h], values_low[h]), of_state, NT)
+        value_grad[i] = value_local[h] + to_next * dot3((keys_high[h], keys_low[h]), of_state, NN)
+    done = slice(start, start + end // width)
+    copies = [
+        pltpu.make_async_copy(key_grad, key_grad_hbm.at[done], sent.at[0]),
+        pltpu.make_async_copy(value_grad, value_grad_hbm.at[done], sent.at[1]),
+    ]
+    for copy in copies:
+        copy.start()
     for copy in copies:
         copy.wait()
 
@@ -361,29 +371,39 @@
         attended_body, (twice, shape(group, 2, 2 * rows)), 2 * product
     )(asked, made, states, high, low, passes, arrived)
     sums = lax.all_to_all(sums, "head", 0, 0, tiled=True)
-    grad, chip_back, back = kernel_call(
+    part = shape(heads // 2 * width + EXTRA, width)
+    grad, *chip_backs, back = kernel_call(
         functools.partial(grad_state_body, heads * width * group),
-        (twice, payload, shape(heads * width, width)),
+        (twice, part, part, shape(heads * width, width)),
         2 * product,
     )(sums, attended, asked, made, states, start_high, start_low)
     behind = [(i, i - 2 - 2 * (i % 2)) for i in range(seq)]
-    moved_back = lax.ppermute(chip_back, ("chip", "core"), [(a, b) for a, b in behind if b >= 0])
+    to = [(a, b) for a, b in behind if b >= 0]
+    moved_backs = [lax.ppermute(a, ("chip", "core"), to) for a in chip_backs]
     half = jax.ShapeDtypeStruct((heads, rows, width), BF16)
     query_grad, key_local, value_local, tails, *halves = kernel_call(
         main_grad_body, (block,) * 4 + (half,) * 4, 5 * product
     )(
-        queries, keys, values, log_decay, docs, within, weighted, grad, states, arrived, chip_back
+        queries, keys, values, log_decay, docs, within, weighted, grad, states, arrived, *chip_backs
     )
-    arrived_back = lax.all_gather(moved_back, "core")
-    held = pltpu.VMEM((heads, rows, width), F32)
-    key_grad, value_grad = kernel_call(
-        last_grad_body,
-        (block,) * 2,
-        2 * product,
-        "",
-        "hh",
-        (held, held, pltpu.SemaphoreType.DMA((heads,))),
-    )(*halves, tails, docs, key_local, value_local, states, back, arrived_back)
+    held = pltpu.VMEM((heads // 2, rows, width), F32)
+    local = (*halves, tails, docs, key_local, value_local, states, back)
+    grads = ()
+    for i, moved_back in enumerate(moved_backs):
+        if i:
+            moved_back, *grads = lax.optimization_barrier((moved_back, *grads))
+        arrived_back = lax.all_gather(moved_back, "core")
+        operands = (*local, arrived_back, *grads)
+        grads = kernel_call(
+            functools.partial(last_grad_body, i * (heads // 2)),
+            (block,) * 2,
+            product,
+            "v" * (len(local) + 1) + "h" * len(grads),
+            "hh",
+            (held, held, pltpu.SemaphoreType.DMA((2,))),
+            [(len(local) + 1 + n, n) for n in range(len(grads))],
+        )(*operands)
+    key_grad, value_grad = grads
     return query_grad, key_grad, value_grad
 
 

time: 51.7 us -> 53.2 us (1.029)
  waiting for transfers between devices: 6.23 us -> 2.42 us
  blocking collectives: 27.6 us -> 30.1 us
  starting transfers between devices: 9.04 us -> 10.9 us
  Pallas kernels: 7.91 us -> 8.74 us
    ppermute x1 -> x2, waiting for transfers between devices: 6.22 us -> 2.41 us  [per_device(): moved_backs = [lax.ppermute(a, ('chip', 'core'), to) for a in chip_backs]]
    all_gather x1 -> x2, blocking collectives: 4.85 us -> 7.37 us  [per_device(): arrived_back = lax.all_gather(moved_back, 'core')]
    ppermute x1 -> x2, starting transfers between devices: 2.86 us -> 4.76 us  [per_device(): moved_backs = [lax.ppermute(a, ('chip', 'core'), to) for a in chip_backs]]
    pallas_call x8 -> x9, Pallas kernels: 7.91 us -> 8.74 us  [call(): pl.pallas_call(body, out_shape=outs, in_specs=of, scratch_shapes=list(scr...]
  transfers between devices with their start and end apart: 2 -> 3, of which waited for: 1 -> 1; matrix products, arithmetic and copies ran while one was open for 0% -> 0% of each run, Pallas kernels for 8% -> 10%
where the time goes in v7:
time: 53.2 us; the launch traced here: 52.9 us
  blocking collectives  30.1 us (57%)
  starting transfers between devices  10.9 us (20%)
  Pallas kernels  8.74 us (16%)
  waiting for transfers between devices  2.42 us (5%)
  between operations  0.73 us (1%)
    all_to_all x1, blocking collectives, per_device(): sums = lax.all_to_all(sums, 'head', 0, 0, tiled=True)  13.3 us
    pallas_call x9, Pallas kernels, call(): pl.pallas_call(body, out_shape=outs, in_specs=of, scratch_shapes=list(scr...  8.74 us
    all_gather x2, blocking collectives, per_device(): arrived_back = lax.all_gather(moved_back, 'core')  7.37 us
    ppermute x1, starting transfers between devices, per_device(): lax.ppermute(chip_state, ('chip', 'core'), [(a, b) for a, b in ahead if b...  6.18 us
    ppermute x2, starting transfers between devices, per_device(): moved_backs = [lax.ppermute(a, ('chip', 'core'), to) for a in chip_backs]  4.76 us
    all_gather x1, blocking collectives, per_device(): states = lax.all_gather(own, 'core')  2.49 us
    ppermute x2, waiting for transfers between devices, per_device(): moved_backs = [lax.ppermute(a, ('chip', 'core'), to) for a in chip_backs]  2.41 us
    all_gather x1, blocking collectives, per_device(): asked = lax.all_gather(asked, 'core')  2.38 us
  transfers between devices with their start and end apart: 3, of which 1 were waited for; matrix products, arithmetic and copies ran while one was open for 0% of the time, Pallas kernels for 10%

profile of v7, /device:TPU:199, one launch (start us, length us, event | category | flops | bytes accessed | tf_op | source)
XLA Modules:
  0.0 52.9 jit_solution(5382066652013406508)
XLA Ops:
  0.6 1.5 %shard_map.94 = (f32[520,128]{1,0:T(8,128)S(1)}, f32[4,128,128]{2,1,0:T(8,128)S(1)}, f32[4,128,128]{2,1,0:T(8,128)S(1)}, f32[4,128]{1,0:T(4,128)S(1)}, f32[4,128]{1,0:T(4,128)S(1)}, /*index=5*/s32[1,128]{1,0:T(1,128)S(1)}) custom-call(f32[4,128,128]{2,1,0:T(8,128)} %keys_hbm.1, f32[4,128,128]{2,1,0:T(8,128)} %values_hbm.1, f32[4,128]{1,0:T(4,128)} %gain_hbm.1, ...), custom_call_target="tpu_custom_call" | custom-call | flops 50331648 | bytes 1048576 | tf_op jit(solution)/shard_map/pallas_call | solution.py:40
  2.2 2.5 %all-gather = f32[1040,128]{1,0:T(8,128)S(1)} all-gather(f32[520,128]{1,0:T(8,128)S(1)} %get-tuple-element.49), channel_id=2, replica_groups=mesh['chip'=48,'core'=2,'head'=8] {'core'}, dimensions={0}, use_global_device_ids=true | all-gather | bytes 798720 | tf_op jit(solution)/shard_map/all_gather | solution.py:345
  4.6 0.0 copy-start
  4.6 0.0 copy-start.1
  4.7 6.2 %collective-permute-start = (f32[520,128]{1,0:T(8,128)S(1)}, f32[520,128]{1,0:T(8,128)S(1)}, u32[]{:S(2)}, u32[]{:S(2)}) collective-permute-start(f32[520,128]{1,0:T(8,128)S(1)} %shard_map.95.sent), channel_id=1, source_target_pairs={{0,16},{8,40},{16,32},{24,56},{32,48},{40,72},{48,64},{56,88},{64,... | collective-permute-start | bytes 798728 | tf_op jit(solution)/shard_map/ppermute | solution.py:348
  10.9 0.0 copy-done
  10.9 0.0 copy-done.1
  10.9 1.2 %shard_map.96 = (f32[776,128]{1,0:T(8,128)S(1)}, f32[768,128]{1,0:T(8,128)S(1)}, f32[4,128,128]{2,1,0:T(8,128)S(1)}, f32[4,128,128]{2,1,0:T(8,128)S(1)}) custom-call(f32[4,128,128]{2,1,0:T(8,128)S(1)} %copy-done, f32[4,128,128]{2,1,0:T(8,128)S(1)} %get-tuple-element.44.keys, f32[4,128,128]{2,1,0:T(8,128)S(1)} %get-tuple-element.45.values, ...), custom_call_target="tpu_custom_call" | custom-call | flops 100663296 | bytes 1048576 | tf_op jit(solution)/shard_map/pallas_call | solution.py:40
  12.1 2.4 %all-gather.1 = f32[1552,128]{1,0:T(8,128)S(1)} all-gather(f32[776,128]{1,0:T(8,128)S(1)} %get-tuple-element.53), channel_id=3, replica_groups=mesh['chip'=48,'core'=2,'head'=8] {'core'}, dimensions={0}, use_global_device_ids=true | all-gather | bytes 1191936 | tf_op jit(solution)/shard_map/all_gather | solution.py:360
  14.5 0.4 shard_map.97
  15.0 2.4 %all-gather.2 = f32[1536,128]{1,0:T(8,128)S(1)} all-gather(f32[768,128]{1,0:T(8,128)S(1)} %get-tuple-element.55), channel_id=4, replica_groups=mesh['chip'=48,'core'=2,'head'=8] {'core'}, dimensions={0}, use_global_device_ids=true | all-gather | bytes 1179648 | tf_op jit(solution)/shard_map/all_gather | solution.py:362
  17.3 0.0 collective-permute-done
  17.3 2.2 %all-gather.3 = f32[1040,128]{1,0:T(8,128)S(1)} all-gather(f32[520,128]{1,0:T(8,128)S(1)} %collective-permute-done), channel_id=5, replica_groups=mesh['chip'=48,'core'=2,'head'=8] {'core'}, dimensions={0}, use_global_device_ids=true | all-gather | bytes 798720 | tf_op jit(solution)/shard_map/all_gather | solution.py:369
  19.5 0.5 shard_map.98
  20.0 13.3 %all_to_all.5.sums = f32[8,2,256]{2,1,0:T(2,128)S(1)} all-to-all(f32[8,2,256]{2,1,0:T(2,128)S(1)} %get-tuple-element.62), channel_id=1, replica_groups=mesh['chip'=48,'core'=2,'head'=8] {'head'}, dimensions={0} | all-to-all | bytes 32768 | tf_op jit(solution)/shard_map/all_to_all | solution.py:373
  33.3 0.6 %shard_map.99 = (f32[2,4,128,128]{3,2,1,0:T(8,128)S(1)}, f32[264,128]{1,0:T(8,128)S(1)}, f32[264,128]{1,0:T(8,128)S(1)}, f32[512,128]{1,0:T(8,128)S(1)}) custom-call(f32[8,2,256]{2,1,0:T(2,128)S(1)} %all_to_all.5.sums, f32[2,4,128,128]{3,2,1,0:T(8,128)S(1)} %get-tuple-element.63.attended, f32[2,776,128]{2,1,0:T(8,128)S(1)} %bitcast.16, ...), custom_call_target="tpu_custom_call" | custom-call | flops 100663296 | bytes 1048576 | tf_op jit(solution)/shard_map/pallas_call | solution.py:40
  33.9 2.8 %collective-permute-start.2 = (f32[264,128]{1,0:T(8,128)S(1)}, f32[264,128]{1,0:T(8,128)S(1)}, u32[]{:S(2)}, u32[]{:S(2)}) collective-permute-start(f32[264,128]{1,0:T(8,128)S(1)} %get-tuple-element.67.sent), channel_id=1, source_target_pairs={{16,0},{32,16},{40,8},{48,32},{56,24},{64,48},{72,40},{80,64},{88,... | collective-permute-start | bytes 405512 | tf_op jit(solution)/shard_map/ppermute | solution.py:382
  36.7 1.9 %collective-permute-start.1 = (f32[264,128]{1,0:T(8,128)S(1)}, f32[264,128]{1,0:T(8,128)S(1)}, u32[]{:S(2)}, u32[]{:S(2)}) collective-permute-start(f32[264,128]{1,0:T(8,128)S(1)} %get-tuple-element.68.sent_later), channel_id=1, source_target_pairs={{16,0},{32,16},{40,8},{48,32},{56,24},{64,48},{72,40},{80,64},{88,... | collective-permute-start | bytes 405512 | tf_op jit(solution)/shard_map/ppermute | solution.py:382
  38.7 2.4 %shard_map.100 = (f32[4,128,128]{2,1,0:T(8,128)}, f32[4,128,128]{2,1,0:T(8,128)S(1)}, f32[4,128,128]{2,1,0:T(8,128)S(1)}, f32[4,128,128]{2,1,0:T(8,128)S(1)}, bf...) custom-call(f32[4,128,128]{2,1,0:T(8,128)S(1)} %copy-done, ...), custom_call_target="tpu_custom_call" | custom-call | flops 251658240 | bytes 1048576 | tf_op jit(solution)/shard_map/pallas_call | solution.py:40
  41.1 2.4 %collective-permute-done.2 = f32[264,128]{1,0:T(8,128)S(1)} collective-permute-done((f32[264,128]{1,0:T(8,128)S(1)}, f32[264,128]{1,0:T(8,128)S(1)}, u32[]{:S(2)}, u32[]{:S(2)}) %collective-permute-start.2) | collective-permute-done | bytes 135200 | tf_op jit(solution)/shard_map/ppermute | solution.py:382
  43.5 5.4 %all-gather.4 = f32[528,128]{1,0:T(8,128)S(1)} all-gather(f32[264,128]{1,0:T(8,128)S(1)} %collective-permute-done.2), channel_id=6, replica_groups=mesh['chip'=48,'core'=2,'head'=8] {'core'}, dimensions={0}, use_global_device_ids=true | all-gather | bytes 405504 | tf_op jit(solution)/shard_map/all_gather | solution.py:395
  48.8 1.0 %shard_map.101 = (f32[4,128,128]{2,1,0:T(8,128)}, f32[4,128,128]{2,1,0:T(8,128)}) custom-call(bf16[4,128,128]{2,1,0:T(8,128)(2,1)S(1)} %get-tuple-element.70.keys_high, bf16[4,128,128]{2,1,0:T(8,128)(2,1)S(1)} %get-tuple-element.71.keys_low, bf16[4,128,128]{2,1,0:T(8,128)(2,1)S(1)} %get-tuple-element.72.values_high, ...), custom_call_target="tpu_custom_call" | custom-call | flops 50331648 | bytes 1048576 | tf_op jit(solution)/shard_map/pallas_call | solution.py:40
  49.9 0.0 collective-permute-done.1
  49.9 2.0 %all-gather.5 = f32[528,128]{1,0:T(8,128)S(1)} all-gather(f32[264,128]{1,0:T(8,128)S(1)} %collective-permute-done.1), channel_id=7, replica_groups=mesh['chip'=48,'core'=2,'head'=8] {'core'}, dimensions={0}, use_global_device_ids=true | all-gather | bytes 405504 | tf_op jit(solution)/shard_map/all_gather | solution.py:395
  51.9 1.0 %shard_map.102 = (f32[4,128,128]{2,1,0:T(8,128)}, f32[4,128,128]{2,1,0:T(8,128)}) custom-call(bf16[4,128,128]{2,1,0:T(8,128)(2,1)S(1)} %get-tuple-element.70.keys_high, bf16[4,128,128]{2,1,0:T(8,128)(2,1)S(1)} %get-tuple-element.71.keys_low, bf16[4,128,128]{2,1,0:T(8,128)(2,1)S(1)} %get-tuple-element.72.values_high, ...), custom_call_target="tpu_custom_call", output_to_operand_aliasing={{0}: (11, {}), {1}: (12, {})} | custom-call | flops 50331648 | bytes 1048576 | tf_op jit(solution)/shard_map/pallas_call | solution.py:40
  (1 shorter events, 0.0 us)
Async XLA Ops:
  4.6 6.2 %copy-start = (f32[4,128,128]{2,1,0:T(8,128)S(1)}, f32[4,128,128]{2,1,0:T(8,128)}, u32[]{:S(2)}) copy-start(f32[4,128,128]{2,1,0:T(8,128)} %queries.3) | copy-start | bytes 786436
  4.6 6.2 %copy-start.1 = (f32[4,128,128]{2,1,0:T(8,128)S(1)}, f32[4,128,128]{2,1,0:T(8,128)}, u32[]{:S(2)}) copy-start(f32[4,128,128]{2,1,0:T(8,128)} %out_grad.1) | copy-start | bytes 786436
  4.7 12.6 %collective-permute-start = (f32[520,128]{1,0:T(8,128)S(1)}, f32[520,128]{1,0:T(8,128)S(1)}, u32[]{:S(2)}, u32[]{:S(2)}) collective-permute-start(f32[520,128]{1,0:T(8,128)S(1)} %shard_map.95.sent), channel_id=1, source_target_pairs={{0,16},{8,40},{16,32},{24,56},{32,48},{40,72},{48,64},{56,88},{64,... | collective-permute-start | bytes 798728 | tf_op jit(solution)/shard_map/ppermute | solution.py:348
  33.9 9.6 %collective-permute-start.2 = (f32[264,128]{1,0:T(8,128)S(1)}, f32[264,128]{1,0:T(8,128)S(1)}, u32[]{:S(2)}, u32[]{:S(2)}) collective-permute-start(f32[264,128]{1,0:T(8,128)S(1)} %get-tuple-element.67.sent), channel_id=1, source_target_pairs={{16,0},{32,16},{40,8},{48,32},{56,24},{64,48},{72,40},{80,64},{88,... | collective-permute-start | bytes 405512 | tf_op jit(solution)/shard_map/ppermute | solution.py:382
  36.7 13.1 %collective-permute-start.1 = (f32[264,128]{1,0:T(8,128)S(1)}, f32[264,128]{1,0:T(8,128)S(1)}, u32[]{:S(2)}, u32[]{:S(2)}) collective-permute-start(f32[264,128]{1,0:T(8,128)S(1)} %get-tuple-element.68.sent_later), channel_id=1, source_target_pairs={{16,0},{32,16},{40,8},{48,32},{56,24},{64,48},{72,40},{80,64},{88,... | collective-permute-start | bytes 405512 | tf_op jit(solution)/shard_map/ppermute | solution.py:382

commit v8 on v6

--- a/solution.py
+++ b/solution.py
@@ -94,7 +94,7 @@
     for copy in copies[2:]:
         copy.wait()
     for h in range(heads):
-        state = dot3(split(keys[h] * weights[h]), split(values[h]), TN)
+        state = dot3(split(keys[h]), split(values[h] * weights[h]), TN)
         out[h * width : (h + 1) * width, :] = state
 
 
@@ -232,6 +232,7 @@
 ):
     _, heads, rows, width = attended.shape
     base = heads * width
+    second = lax.axis_index("core") == 1
     total = jnp.sum(sums[...], axis=0)
     inverse_row = lax.rsqrt(total[0:1, :] / width_all + EPSILON)
     coupling_row = total[1:2, :] / width_all * inverse_row * inverse_row
@@ -241,12 +242,13 @@
     coupling = [as_columns(coupling_row[:, c * rows : (c + 1) * rows], rows) for c in range(2)]
     for h in range(heads):
         at = slice(h * width, (h + 1) * width)
-        of_cores = []
+        of_cores, of_both = [], []
         for c in range(2):
             _, _, scaled = token_rows(asked.at[c], made.at[c], h, heads, rows)
             value = inverse[c] * (scaled - attended[c, h] * coupling[c])
-            grad[c, h] = value
+            of_both.append(value)
             of_cores.append(dot3((start_high[c, h], start_low[c, h]), split(value), NN))
+        grad[h] = pick(second, of_both[1], of_both[0])
         back[at, :] = of_cores[1]
         passed = link(first_label, second_label, row_of(states, 0, base + h))
         out[at, :] = of_cores[0] + passed * of_cores[1]
@@ -265,7 +267,7 @@
     near = pick(second, row_of(states, 0, base + LAST), row_of(arrived, 0, base + LAST))
     ahead = as_columns(docs[...].astype(F32), rows) == near
     for h in range(queries.shape[0]):
-        of_grad = split(grad[lax.axis_index("core"), h])
+        of_grad = split(grad[h])
         of_keys = split(keys[h])
         of_values = split(values[h])
         of_both = split(within[h] * dot3(of_grad, of_values, NT))
@@ -363,7 +365,7 @@
     sums = lax.all_to_all(sums, "head", 0, 0, tiled=True)
     grad, chip_back, back = kernel_call(
         functools.partial(grad_state_body, heads * width * group),
-        (twice, payload, shape(heads * width, width)),
+        (block, payload, shape(heads * width, width)),
         2 * product,
     )(sums, attended, asked, made, states, start_high, start_low)
     behind = [(i, i - 2 - 2 * (i % 2)) for i in range(seq)]

time: 51.7 us -> 51.6 us (level)
  no operation moved by 1% of the time
where the time goes in v8:
time: 51.6 us; the launch traced here: 51.4 us
  blocking collectives  27.5 us (53%)
  starting transfers between devices  9.04 us (18%)
  Pallas kernels  7.87 us (15%)
  waiting for transfers between devices  6.24 us (12%)
  between operations  0.7 us (1%)
    all_to_all x1, blocking collectives, per_device(): sums = lax.all_to_all(sums, 'head', 0, 0, tiled=True)  13.3 us
    pallas_call x8, Pallas kernels, call(): pl.pallas_call(body, out_shape=outs, in_specs=of, scratch_shapes=list(scr...  7.87 us
    ppermute x1, waiting for transfers between devices, per_device(): lax.ppermute(chip_back, ('chip', 'core'), [(a, b) for a, b in behind if b...  6.24 us
    ppermute x1, starting transfers between devices, per_device(): lax.ppermute(chip_state, ('chip', 'core'), [(a, b) for a, b in ahead if b...  6.18 us
    all_gather x1, blocking collectives, per_device(): arrived_back = lax.all_gather(moved_back, 'core')  4.84 us
    ppermute x1, starting transfers between devices, per_device(): lax.ppermute(chip_back, ('chip', 'core'), [(a, b) for a, b in behind if b...  2.85 us
    all_gather x1, blocking collectives, per_device(): states = lax.all_gather(own, 'core')  2.49 us
    all_gather x1, blocking collectives, per_device(): asked = lax.all_gather(asked, 'core')  2.38 us
  transfers between devices with their start and end apart: 2, of which 1 were waited for; matrix products, arithmetic and copies ran while one was open for 0% of the time, Pallas kernels for 8%

profile of v8, /device:TPU:199, one launch (start us, length us, event | category | flops | bytes accessed | tf_op | source)
XLA Modules:
  0.0 51.4 jit_solution(10224958580049306063)
XLA Ops:
  0.6 1.5 %shard_map.94 = (f32[520,128]{1,0:T(8,128)S(1)}, f32[4,128,128]{2,1,0:T(8,128)S(1)}, f32[4,128,128]{2,1,0:T(8,128)S(1)}, f32[4,128]{1,0:T(4,128)S(1)}, f32[4,128]{1,0:T(4,128)S(1)}, /*index=5*/s32[1,128]{1,0:T(1,128)S(1)}) custom-call(f32[4,128,128]{2,1,0:T(8,128)} %keys_hbm.1, f32[4,128,128]{2,1,0:T(8,128)} %values_hbm.1, f32[4,128]{1,0:T(4,128)} %gain_hbm.1, ...), custom_call_target="tpu_custom_call" | custom-call | flops 50331648 | bytes 1048576 | tf_op jit(solution)/shard_map/pallas_call | solution.py:40
  2.1 2.5 %all-gather = f32[1040,128]{1,0:T(8,128)S(1)} all-gather(f32[520,128]{1,0:T(8,128)S(1)} %get-tuple-element.43), channel_id=2, replica_groups=mesh['chip'=48,'core'=2,'head'=8] {'core'}, dimensions={0}, use_global_device_ids=true | all-gather | bytes 798720 | tf_op jit(solution)/shard_map/all_gather | solution.py:337
  4.6 0.0 copy-start
  4.6 0.0 copy-start.1
  4.7 6.2 %collective-permute-start = (f32[520,128]{1,0:T(8,128)S(1)}, f32[520,128]{1,0:T(8,128)S(1)}, u32[]{:S(2)}, u32[]{:S(2)}) collective-permute-start(f32[520,128]{1,0:T(8,128)S(1)} %shard_map.95.sent), channel_id=1, source_target_pairs={{0,16},{8,40},{16,32},{24,56},{32,48},{40,72},{48,64},{56,88},{64,... | collective-permute-start | bytes 798728 | tf_op jit(solution)/shard_map/ppermute | solution.py:340
  10.9 0.0 copy-done
  10.9 0.0 copy-done.1
  10.9 1.2 %shard_map.96 = (f32[776,128]{1,0:T(8,128)S(1)}, f32[768,128]{1,0:T(8,128)S(1)}, f32[4,128,128]{2,1,0:T(8,128)S(1)}, f32[4,128,128]{2,1,0:T(8,128)S(1)}) custom-call(f32[4,128,128]{2,1,0:T(8,128)S(1)} %copy-done, f32[4,128,128]{2,1,0:T(8,128)S(1)} %get-tuple-element.38.keys, f32[4,128,128]{2,1,0:T(8,128)S(1)} %get-tuple-element.39.values, ...), custom_call_target="tpu_custom_call" | custom-call | flops 100663296 | bytes 1048576 | tf_op jit(solution)/shard_map/pallas_call | solution.py:40
  12.1 2.4 %all-gather.1 = f32[1552,128]{1,0:T(8,128)S(1)} all-gather(f32[776,128]{1,0:T(8,128)S(1)} %get-tuple-element.47), channel_id=3, replica_groups=mesh['chip'=48,'core'=2,'head'=8] {'core'}, dimensions={0}, use_global_device_ids=true | all-gather | bytes 1191936 | tf_op jit(solution)/shard_map/all_gather | solution.py:352
  14.5 0.4 shard_map.97
  14.9 2.4 %all-gather.2 = f32[1536,128]{1,0:T(8,128)S(1)} all-gather(f32[768,128]{1,0:T(8,128)S(1)} %get-tuple-element.49), channel_id=4, replica_groups=mesh['chip'=48,'core'=2,'head'=8] {'core'}, dimensions={0}, use_global_device_ids=true | all-gather | bytes 1179648 | tf_op jit(solution)/shard_map/all_gather | solution.py:354
  17.3 0.0 collective-permute-done
  17.3 2.2 %all-gather.3 = f32[1040,128]{1,0:T(8,128)S(1)} all-gather(f32[520,128]{1,0:T(8,128)S(1)} %collective-permute-done), channel_id=5, replica_groups=mesh['chip'=48,'core'=2,'head'=8] {'core'}, dimensions={0}, use_global_device_ids=true | all-gather | bytes 798720 | tf_op jit(solution)/shard_map/all_gather | solution.py:361
  19.5 0.5 shard_map.98
  20.0 13.3 %all_to_all.5.sums = f32[8,2,256]{2,1,0:T(2,128)S(1)} all-to-all(f32[8,2,256]{2,1,0:T(2,128)S(1)} %get-tuple-element.56), channel_id=1, replica_groups=mesh['chip'=48,'core'=2,'head'=8] {'head'}, dimensions={0} | all-to-all | bytes 32768 | tf_op jit(solution)/shard_map/all_to_all | solution.py:365
  33.3 0.6 %shard_map.99 = (f32[4,128,128]{2,1,0:T(8,128)S(1)}, f32[520,128]{1,0:T(8,128)S(1)}, f32[512,128]{1,0:T(8,128)S(1)}) custom-call(f32[8,2,256]{2,1,0:T(2,128)S(1)} %all_to_all.5.sums, f32[2,4,128,128]{3,2,1,0:T(8,128)S(1)} %get-tuple-element.57.attended, f32[2,776,128]{2,1,0:T(8,128)S(1)} %bitcast.14, f32[2,768,128]{2,1,0:T(8,128)S(1)} %bitcast.16, ...), custom_call_target="tpu_custom_call" | custom-call | flops 100663296 | bytes 1048576 | tf_op jit(solution)/shard_map/pallas_call | solution.py:40
  33.8 2.9 %collective-permute-start.1 = (f32[520,128]{1,0:T(8,128)S(1)}, f32[520,128]{1,0:T(8,128)S(1)}, u32[]{:S(2)}, u32[]{:S(2)}) collective-permute-start(f32[520,128]{1,0:T(8,128)S(1)} %get-tuple-element.61.sent), channel_id=1, source_target_pairs={{16,0},{32,16},{40,8},{48,32},{56,24},{64,48},{72,40},{80,64},{88,... | collective-permute-start | bytes 798728 | tf_op jit(solution)/shard_map/ppermute | solution.py:372
  36.7 2.4 %shard_map.100 = (f32[4,128,128]{2,1,0:T(8,128)}, f32[4,128,128]{2,1,0:T(8,128)S(1)}, f32[4,128,128]{2,1,0:T(8,128)S(1)}, f32[4,128,128]{2,1,0:T(8,128)S(1)}, bf...) custom-call(f32[4,128,128]{2,1,0:T(8,128)S(1)} %copy-done, ...), custom_call_target="tpu_custom_call" | custom-call | flops 251658240 | bytes 1048576 | tf_op jit(solution)/shard_map/pallas_call | solution.py:40
  39.1 6.2 %collective-permute-done.1 = f32[520,128]{1,0:T(8,128)S(1)} collective-permute-done((f32[520,128]{1,0:T(8,128)S(1)}, f32[520,128]{1,0:T(8,128)S(1)}, u32[]{:S(2)}, u32[]{:S(2)}) %collective-permute-start.1) | collective-permute-done | bytes 266272 | tf_op jit(solution)/shard_map/ppermute | solution.py:372
  45.3 4.8 %all-gather.4 = f32[1040,128]{1,0:T(8,128)S(1)} all-gather(f32[520,128]{1,0:T(8,128)S(1)} %collective-permute-done.1), channel_id=6, replica_groups=mesh['chip'=48,'core'=2,'head'=8] {'core'}, dimensions={0}, use_global_device_ids=true | all-gather | bytes 798720 | tf_op jit(solution)/shard_map/all_gather | solution.py:379
  50.2 1.2 %shard_map.101 = (f32[4,128,128]{2,1,0:T(8,128)}, f32[4,128,128]{2,1,0:T(8,128)}) custom-call(bf16[4,128,128]{2,1,0:T(8,128)(2,1)S(1)} %get-tuple-element.63.keys_high, bf16[4,128,128]{2,1,0:T(8,128)(2,1)S(1)} %get-tuple-element.64.keys_low, bf16[4,128,128]{2,1,0:T(8,128)(2,1)S(1)} %get-tuple-element.65.values_high, ...), custom_call_target="tpu_custom_call" | custom-call | flops 100663296 | bytes 1048576 | tf_op jit(solution)/shard_map/pallas_call | solution.py:40
  (1 shorter events, 0.0 us)
Async XLA Ops:
  4.6 6.2 %copy-start = (f32[4,128,128]{2,1,0:T(8,128)S(1)}, f32[4,128,128]{2,1,0:T(8,128)}, u32[]{:S(2)}) copy-start(f32[4,128,128]{2,1,0:T(8,128)} %queries.3) | copy-start | bytes 786436
  4.6 6.2 %copy-start.1 = (f32[4,128,128]{2,1,0:T(8,128)S(1)}, f32[4,128,128]{2,1,0:T(8,128)}, u32[]{:S(2)}) copy-start(f32[4,128,128]{2,1,0:T(8,128)} %out_grad.1) | copy-start | bytes 786436
  4.7 12.6 %collective-permute-start = (f32[520,128]{1,0:T(8,128)S(1)}, f32[520,128]{1,0:T(8,128)S(1)}, u32[]{:S(2)}, u32[]{:S(2)}) collective-permute-start(f32[520,128]{1,0:T(8,128)S(1)} %shard_map.95.sent), channel_id=1, source_target_pairs={{0,16},{8,40},{16,32},{24,56},{32,48},{40,72},{48,64},{56,88},{64,... | collective-permute-start | bytes 798728 | tf_op jit(solution)/shard_map/ppermute | solution.py:340
  33.8 11.5 %collective-permute-start.1 = (f32[520,128]{1,0:T(8,128)S(1)}, f32[520,128]{1,0:T(8,128)S(1)}, u32[]{:S(2)}, u32[]{:S(2)}) collective-permute-start(f32[520,128]{1,0:T(8,128)S(1)} %get-tuple-element.61.sent), channel_id=1, source_target_pairs={{16,0},{32,16},{40,8},{48,32},{56,24},{64,48},{72,40},{80,64},{88,... | collective-permute-start | bytes 798728 | tf_op jit(solution)/shard_map/ppermute | solution.py:372

commit v9 on v8

--- a/solution.py
+++ b/solution.py
@@ -306,11 +306,11 @@
         to_next = jnp.where(ahead, tails[h], 0.0)
         key_grad[h] = key_local[h] + to_next * dot3((values_high[h], values_low[h]), of_state, NT)
         value_grad[h] = value_local[h] + to_next * dot3((keys_high[h], keys_low[h]), of_state, NN)
-        if h % 2 == 0:
+        if h < heads - 2:
             continue
         for i, (a, b) in enumerate(((key_grad, key_grad_hbm), (value_grad, value_grad_hbm))):
-            done = slice(h - 1, h + 1)
-            copies.append(pltpu.make_async_copy(a.at[done], b.at[done], sent.at[h - 1 + i]))
+            done = slice(0 if h < heads - 1 else h, h + 1)
+            copies.append(pltpu.make_async_copy(a.at[done], b.at[done], sent.at[2 * (h - heads + 2) + i]))
             copies[-1].start()
     for copy in copies:
         copy.wait()

time: 51.6 us -> 51.7 us (level)
  no operation moved by 1% of the time
where the time goes in v9:
time: 51.7 us; the launch traced here: 51.4 us
  blocking collectives  27.5 us (53%)
  starting transfers between devices  9.04 us (17%)
  Pallas kernels  7.9 us (15%)
  waiting for transfers between devices  6.24 us (12%)
  between operations  0.7 us (1%)
    all_to_all x1, blocking collectives, per_device(): sums = lax.all_to_all(sums, 'head', 0, 0, tiled=True)  13.3 us
    pallas_call x8, Pallas kernels, call(): pl.pallas_call(body, out_shape=outs, in_specs=of, scratch_shapes=list(scr...  7.9 us
    ppermute x1, waiting for transfers between devices, per_device(): lax.ppermute(chip_back, ('chip', 'core'), [(a, b) for a, b in behind if b...  6.24 us
    ppermute x1, starting transfers between devices, per_device(): lax.ppermute(chip_state, ('chip', 'core'), [(a, b) for a, b in ahead if b...  6.18 us
    all_gather x1, blocking collectives, per_device(): arrived_back = lax.all_gather(moved_back, 'core')  4.84 us
    ppermute x1, starting transfers between devices, per_device(): lax.ppermute(chip_back, ('chip', 'core'), [(a, b) for a, b in behind if b...  2.85 us
    all_gather x1, blocking collectives, per_device(): states = lax.all_gather(own, 'core')  2.49 us
    all_gather x1, blocking collectives, per_device(): asked = lax.all_gather(asked, 'core')  2.38 us
  transfers between devices with their start and end apart: 2, of which 1 were waited for; matrix products, arithmetic and copies ran while one was open for 0% of the time, Pallas kernels for 8%

profile of v9, /device:TPU:199, one launch (start us, length us, event | category | flops | bytes accessed | tf_op | source)
XLA Modules:
  0.0 51.4 jit_solution(17432934863746686866)
XLA Ops:
  0.6 1.5 %shard_map.94 = (f32[520,128]{1,0:T(8,128)S(1)}, f32[4,128,128]{2,1,0:T(8,128)S(1)}, f32[4,128,128]{2,1,0:T(8,128)S(1)}, f32[4,128]{1,0:T(4,128)S(1)}, f32[4,128]{1,0:T(4,128)S(1)}, /*index=5*/s32[1,128]{1,0:T(1,128)S(1)}) custom-call(f32[4,128,128]{2,1,0:T(8,128)} %keys_hbm.1, f32[4,128,128]{2,1,0:T(8,128)} %values_hbm.1, f32[4,128]{1,0:T(4,128)} %gain_hbm.1, ...), custom_call_target="tpu_custom_call" | custom-call | flops 50331648 | bytes 1048576 | tf_op jit(solution)/shard_map/pallas_call | solution.py:40
  2.1 2.5 %all-gather = f32[1040,128]{1,0:T(8,128)S(1)} all-gather(f32[520,128]{1,0:T(8,128)S(1)} %get-tuple-element.43), channel_id=2, replica_groups=mesh['chip'=48,'core'=2,'head'=8] {'core'}, dimensions={0}, use_global_device_ids=true | all-gather | bytes 798720 | tf_op jit(solution)/shard_map/all_gather | solution.py:337
  4.6 0.0 copy-start
  4.6 0.0 copy-start.1
  4.7 6.2 %collective-permute-start = (f32[520,128]{1,0:T(8,128)S(1)}, f32[520,128]{1,0:T(8,128)S(1)}, u32[]{:S(2)}, u32[]{:S(2)}) collective-permute-start(f32[520,128]{1,0:T(8,128)S(1)} %shard_map.95.sent), channel_id=1, source_target_pairs={{0,16},{8,40},{16,32},{24,56},{32,48},{40,72},{48,64},{56,88},{64,... | collective-permute-start | bytes 798728 | tf_op jit(solution)/shard_map/ppermute | solution.py:340
  10.9 0.0 copy-done
  10.9 0.0 copy-done.1
  10.9 1.2 %shard_map.96 = (f32[776,128]{1,0:T(8,128)S(1)}, f32[768,128]{1,0:T(8,128)S(1)}, f32[4,128,128]{2,1,0:T(8,128)S(1)}, f32[4,128,128]{2,1,0:T(8,128)S(1)}) custom-call(f32[4,128,128]{2,1,0:T(8,128)S(1)} %copy-done, f32[4,128,128]{2,1,0:T(8,128)S(1)} %get-tuple-element.38.keys, f32[4,128,128]{2,1,0:T(8,128)S(1)} %get-tuple-element.39.values, ...), custom_call_target="tpu_custom_call" | custom-call | flops 100663296 | bytes 1048576 | tf_op jit(solution)/shard_map/pallas_call | solution.py:40
  12.1 2.4 %all-gather.1 = f32[1552,128]{1,0:T(8,128)S(1)} all-gather(f32[776,128]{1,0:T(8,128)S(1)} %get-tuple-element.47), channel_id=3, replica_groups=mesh['chip'=48,'core'=2,'head'=8] {'core'}, dimensions={0}, use_global_device_ids=true | all-gather | bytes 1191936 | tf_op jit(solution)/shard_map/all_gather | solution.py:352
  14.5 0.4 shard_map.97
  14.9 2.4 %all-gather.2 = f32[1536,128]{1,0:T(8,128)S(1)} all-gather(f32[768,128]{1,0:T(8,128)S(1)} %get-tuple-element.49), channel_id=4, replica_groups=mesh['chip'=48,'core'=2,'head'=8] {'core'}, dimensions={0}, use_global_device_ids=true | all-gather | bytes 1179648 | tf_op jit(solution)/shard_map/all_gather | solution.py:354
  17.3 0.0 collective-permute-done
  17.3 2.2 %all-gather.3 = f32[1040,128]{1,0:T(8,128)S(1)} all-gather(f32[520,128]{1,0:T(8,128)S(1)} %collective-permute-done), channel_id=5, replica_groups=mesh['chip'=48,'core'=2,'head'=8] {'core'}, dimensions={0}, use_global_device_ids=true | all-gather | bytes 798720 | tf_op jit(solution)/shard_map/all_gather | solution.py:361
  19.5 0.5 shard_map.98
  20.0 13.3 %all_to_all.5.sums = f32[8,2,256]{2,1,0:T(2,128)S(1)} all-to-all(f32[8,2,256]{2,1,0:T(2,128)S(1)} %get-tuple-element.56), channel_id=1, replica_groups=mesh['chip'=48,'core'=2,'head'=8] {'head'}, dimensions={0} | all-to-all | bytes 32768 | tf_op jit(solution)/shard_map/all_to_all | solution.py:365
  33.3 0.6 %shard_map.99 = (f32[4,128,128]{2,1,0:T(8,128)S(1)}, f32[520,128]{1,0:T(8,128)S(1)}, f32[512,128]{1,0:T(8,128)S(1)}) custom-call(f32[8,2,256]{2,1,0:T(2,128)S(1)} %all_to_all.5.sums, f32[2,4,128,128]{3,2,1,0:T(8,128)S(1)} %get-tuple-element.57.attended, f32[2,776,128]{2,1,0:T(8,128)S(1)} %bitcast.14, f32[2,768,128]{2,1,0:T(8,128)S(1)} %bitcast.16, ...), custom_call_target="tpu_custom_call" | custom-call | flops 100663296 | bytes 1048576 | tf_op jit(solution)/shard_map/pallas_call | solution.py:40
  33.8 2.9 %collective-permute-start.1 = (f32[520,128]{1,0:T(8,128)S(1)}, f32[520,128]{1,0:T(8,128)S(1)}, u32[]{:S(2)}, u32[]{:S(2)}) collective-permute-start(f32[520,128]{1,0:T(8,128)S(1)} %get-tuple-element.61.sent), channel_id=1, source_target_pairs={{16,0},{32,16},{40,8},{48,32},{56,24},{64,48},{72,40},{80,64},{88,... | collective-permute-start | bytes 798728 | tf_op jit(solution)/shard_map/ppermute | solution.py:372
  36.7 2.4 %shard_map.100 = (f32[4,128,128]{2,1,0:T(8,128)}, f32[4,128,128]{2,1,0:T(8,128)S(1)}, f32[4,128,128]{2,1,0:T(8,128)S(1)}, f32[4,128,128]{2,1,0:T(8,128)S(1)}, bf...) custom-call(f32[4,128,128]{2,1,0:T(8,128)S(1)} %copy-done, ...), custom_call_target="tpu_custom_call" | custom-call | flops 251658240 | bytes 1048576 | tf_op jit(solution)/shard_map/pallas_call | solution.py:40
  39.1 6.2 %collective-permute-done.1 = f32[520,128]{1,0:T(8,128)S(1)} collective-permute-done((f32[520,128]{1,0:T(8,128)S(1)}, f32[520,128]{1,0:T(8,128)S(1)}, u32[]{:S(2)}, u32[]{:S(2)}) %collective-permute-start.1) | collective-permute-done | bytes 266272 | tf_op jit(solution)/shard_map/ppermute | solution.py:372
  45.3 4.8 %all-gather.4 = f32[1040,128]{1,0:T(8,128)S(1)} all-gather(f32[520,128]{1,0:T(8,128)S(1)} %collective-permute-done.1), channel_id=6, replica_groups=mesh['chip'=48,'core'=2,'head'=8] {'core'}, dimensions={0}, use_global_device_ids=true | all-gather | bytes 798720 | tf_op jit(solution)/shard_map/all_gather | solution.py:379
  50.2 1.2 %shard_map.101 = (f32[4,128,128]{2,1,0:T(8,128)}, f32[4,128,128]{2,1,0:T(8,128)}) custom-call(bf16[4,128,128]{2,1,0:T(8,128)(2,1)S(1)} %get-tuple-element.63.keys_high, bf16[4,128,128]{2,1,0:T(8,128)(2,1)S(1)} %get-tuple-element.64.keys_low, bf16[4,128,128]{2,1,0:T(8,128)(2,1)S(1)} %get-tuple-element.65.values_high, ...), custom_call_target="tpu_custom_call" | custom-call | flops 100663296 | bytes 1048576 | tf_op jit(solution)/shard_map/pallas_call | solution.py:40
  (1 shorter events, 0.0 us)
Async XLA Ops:
  4.6 6.2 %copy-start = (f32[4,128,128]{2,1,0:T(8,128)S(1)}, f32[4,128,128]{2,1,0:T(8,128)}, u32[]{:S(2)}) copy-start(f32[4,128,128]{2,1,0:T(8,128)} %queries.3) | copy-start | bytes 786436
  4.6 6.2 %copy-start.1 = (f32[4,128,128]{2,1,0:T(8,128)S(1)}, f32[4,128,128]{2,1,0:T(8,128)}, u32[]{:S(2)}) copy-start(f32[4,128,128]{2,1,0:T(8,128)} %out_grad.1) | copy-start | bytes 786436
  4.7 12.6 %collective-permute-start = (f32[520,128]{1,0:T(8,128)S(1)}, f32[520,128]{1,0:T(8,128)S(1)}, u32[]{:S(2)}, u32[]{:S(2)}) collective-permute-start(f32[520,128]{1,0:T(8,128)S(1)} %shard_map.95.sent), channel_id=1, source_target_pairs={{0,16},{8,40},{16,32},{24,56},{32,48},{40,72},{48,64},{56,88},{64,... | collective-permute-start | bytes 798728 | tf_op jit(solution)/shard_map/ppermute | solution.py:340
  33.8 11.5 %collective-permute-start.1 = (f32[520,128]{1,0:T(8,128)S(1)}, f32[520,128]{1,0:T(8,128)S(1)}, u32[]{:S(2)}, u32[]{:S(2)}) collective-permute-start(f32[520,128]{1,0:T(8,128)S(1)} %get-tuple-element.61.sent), channel_id=1, source_target_pairs={{16,0},{32,16},{40,8},{48,32},{56,24},{64,48},{72,40},{80,64},{88,... | collective-permute-start | bytes 798728 | tf_op jit(solution)/shard_map/ppermute | solution.py:372
